TPU v7x, 256 devices: a whole 4x4x8 slice. The times are simulated.
256 devices in a mesh: row: 16 (over x, y), col: 16 (over z, core).
Axes of the slice: x: 4, y: 4, z: 8, core: 2. Of those that a mesh axis runs over, the one named last changes fastest.
Arguments:
- tokens: bfloat16 [512, 12288], P('col', 'row'), may hold values from -6 to 6
- weight_in: bfloat16 [12288, 24576], P('row', 'col'), may hold values from -0.0546875 to 0.0546875
- weight_out: bfloat16 [24576, 12288], P('col', 'row'), may hold values from -0.0390625 to 0.0390625
- cotangent: bfloat16 [512, 12288], P('col', 'row'), may hold values from -6 to 6
Outputs:
- output: bfloat16 [512, 12288], P('col', 'row')
- grad_tokens: bfloat16 [512, 12288], P('col', 'row')
- grad_in: bfloat16 [12288, 24576], P('row', 'col')
- grad_out: bfloat16 [24576, 12288], P('col', 'row')
All inputs are finite; a program needn't handle non-finite values.
Results may differ from a plain program's by a relative error of at most 0.034.
Values may be sent and summed in bfloat16 or wider, within the bound.
No kernel may reach another device: no remote copies, remote signals or barrier semaphores. Data moves between devices by JAX's collectives and lax.ppermute only.
A program may use at most 64 MiB of HBM per device.

v0:
```python
import jax
import jax.numpy as jnp
from jax import lax
from jax.sharding import PartitionSpec as P

tanh_gain = 0.7978845608028654
cubic_term = 0.044715


def gelu_value(hidden):
    return (
        0.5
        * hidden
        * (1.0 + jnp.tanh(tanh_gain * (hidden + cubic_term * hidden * hidden * hidden)))
    )


def gelu_slope(hidden):
    squared = hidden * hidden
    tangent = jnp.tanh(tanh_gain * (hidden + cubic_term * squared * hidden))
    return 0.5 * (1.0 + tangent) + 0.5 * hidden * (1.0 - tangent * tangent) * tanh_gain * (
        1.0 + 3.0 * cubic_term * squared
    )


def contract_rows(left, right):
    return lax.dot_general(
        left, right, (((0,), (0,)), ((), ())), preferred_element_type=jnp.float32
    )


def contract_cols(left, right):
    return lax.dot_general(
        left, right, (((1,), (1,)), ((), ())), preferred_element_type=jnp.float32
    )


def local(tokens, weight_in, weight_out, cotangent):
    token_block, grad_block = (
        lax.all_gather(tokens, "col", axis=0, tiled=True),
        lax.all_gather(cotangent, "col", axis=0, tiled=True),
    )
    grad_scale = token_block.shape[0] ** (-0.5)
    partial_value = jnp.dot(token_block, weight_in, preferred_element_type=jnp.float32)
    hidden = lax.psum(partial_value.astype(jnp.bfloat16), "row").astype(jnp.float32)
    activation = gelu_value(hidden).astype(jnp.bfloat16)
    picked = activation
    output = lax.psum_scatter(
        jnp.dot(picked, weight_out, preferred_element_type=jnp.float32).astype(jnp.bfloat16),
        "col",
        scatter_dimension=0,
        tiled=True,
    )
    grad_out = (contract_rows(activation, grad_block) * grad_scale).astype(jnp.bfloat16)
    grad_partial = contract_cols(grad_block, weight_out)
    grad_activation = lax.psum(grad_partial.astype(jnp.bfloat16), "row").astype(jnp.float32)
    grad_hidden = (grad_activation * gelu_slope(hidden)).astype(jnp.bfloat16)
    grad_in = (contract_rows(token_block, grad_hidden) * grad_scale).astype(jnp.bfloat16)
    picked = grad_hidden
    grad_tokens = lax.psum_scatter(
        contract_cols(picked, weight_in).astype(jnp.bfloat16),
        "col",
        scatter_dimension=0,
        tiled=True,
    )
    return (output, grad_tokens, grad_in, grad_out)


def solution(mesh):
    in_specs = (P("col", "row"), P("row", "col"), P("col", "row"), P("col", "row"))
    out_specs = (P("col", "row"), P("col", "row"), P("row", "col"), P("col", "row"))
    return jax.shard_map(local, mesh=mesh, in_specs=in_specs, out_specs=out_specs, check_vma=False)
```

profile of v0, /device:TPU:24, one launch (start us, length us, event | category | flops | bytes accessed | tf_op | source)
XLA Modules:
  0.0 283.8 jit_solution(16198810424053517689)
XLA Ops:
  7.2 0.0 copy-start
  7.2 0.0 all-reduce.3.cloned.1.call-start
  7.2 22.5 %all_gather.6 = bf16[512,768]{1,0:T(8,128)(2,1)S(1)} all-gather(bf16[32,768]{1,0:T(8,128)(2,1)} %param.4), channel_id=1, replica_groups=mesh['row'=16,'col'=16] {'col'}, dimensions={0}, use_global_device_ids=true | all-gather | bytes 835584 | tf_op jit(solution)/shard_map/all_gather | solution.py:40
  29.7 0.0 copy-start.2
  29.7 16.9 %all_gather.7 = bf16[512,768]{1,0:T(8,128)(2,1)S(1)} all-gather(bf16[32,768]{1,0:T(8,128)(2,1)} %param.7), channel_id=1, replica_groups=mesh['row'=16,'col'=16] {'col'}, dimensions={0}, use_global_device_ids=true | all-gather | bytes 835584 | tf_op jit(solution)/shard_map/all_gather | solution.py:41
  46.6 0.0 copy-done.2
  46.6 4.2 %convolution_convert_fusion.1 = bf16[512,1536]{1,0:T(8,128)(2,1)} fusion(bf16[512,768]{1,0:T(8,128)(2,1)S(1)} %all_gather.6, bf16[768,1536]{1,0:T(8,128)(2,1)} %param.5), kind=kOutput, calls=%fused_computation.28 | convolution fusion | flops 1208745984 | bytes 4718592 | tf_op jit(solution)/shard_map/dot_general | solution.py:44
  50.8 0.0 copy-done
  50.8 2.6 convolution_convert_fusion
  53.4 0.0 all-reduce.3.cloned.1.call-update
  53.4 0.0 reduce-scatter.3.cloned.1.call-start
  53.4 103.7 %all-reduce.3.cloned.1.call-done = (bf16[512,1536]{1,0:T(8,128)(2,1)}, bf16[512,1536]{1,0:T(8,128)(2,1)}) async-done(((bf16[512,1536]{1,0:T(8,128)(2,1)}, bf16[512,1536]{1,0:T(8,128)(2,1)}), (bf16[512,1536]{1,0:T(8,128)(2,1)}, bf16[512,1536]{1,0:T(8,128)(2,1)})) %all-reduce.3.cloned.1.call-update) | async-done | bytes 3145744 | tf_op jit(solution)/shard_map/psum | solution.py:45
  157.1 4.3 %convolution_convert_fusion.3 = bf16[512,768]{1,0:T(8,128)(2,1)} fusion(bf16[1536,768]{1,0:T(8,128)(2,1)S(1)} %copy-done, bf16[512,1536]{1,0:T(8,128)(2,1)} %get-tuple-element.8), kind=kOutput, calls=%fused_computation.30 | convolution fusion | flops 1216217088 | bytes 4718592 | tf_op jit(solution)/shard_map/dot_general | solution.py:49
  161.4 0.0 reduce-scatter.3.cloned.1.call-update
  161.5 0.0 reduce-scatter.5.cloned.1.call-start
  161.5 0.0 copy-start.3
  161.5 4.1 %fusion.8 = bf16[512,1536]{1,0:T(8,128)(2,1)S(1)} fusion(bf16[512,1536]{1,0:T(8,128)(2,1)} %get-tuple-element.8, bf16[512,1536]{1,0:T(8,128)(2,1)} %get-tuple-element.9), kind=kLoop, calls=%fused_computation.18 | loop fusion | flops 15728640 | bytes 4718592 | tf_op jit(solution)/shard_map/convert_element_type | solution.py:57
  165.6 0.0 copy-start.1
  165.7 1.1 copy-done.1
  166.8 0.0 copy-done.3
  166.8 2.3 convolution_convert_fusion.2
  169.1 0.0 reduce-scatter.5.cloned.1.call-update
  169.1 4.4 %fusion.16 = bf16[768,1536]{0,1:T(8,128)(2,1)} fusion(bf16[512,1536]{1,0:T(8,128)(2,1)} %copy-done.1, bf16[512,768]{1,0:T(8,128)(2,1)} %copy-done.2), kind=kOutput, calls=%fused_computation.26 | convolution fusion | flops 1210318848 | bytes 4718592 | tf_op jit(solution)/shard_map/dot_general | solution.py:27
  173.6 4.3 %copy.8 = bf16[768,1536]{1,0:T(8,128)(2,1)} copy(bf16[768,1536]{0,1:T(8,128)(2,1)} %fusion.16) | data formatting | bytes 4718592
  177.8 4.8 %multiply_convert_fusion = bf16[1536,768]{1,0:T(8,128)(2,1)} fusion(bf16[512,768]{1,0:T(8,128)(2,1)S(1)} %all_gather.7, bf16[512,1536]{1,0:T(8,128)(2,1)} %get-tuple-element.8), kind=kOutput, calls=%fused_computation.8 | convolution fusion | flops 1218183168 | bytes 4718592 | tf_op jit(solution)/shard_map/dot_general | solution.py:27
  182.6 36.1 %reduce-scatter.3.cloned.1.call-done = bf16[32,768]{1,0:T(8,128)(2,1)} async-done(((bf16[512,768]{1,0:T(8,128)(2,1)}), bf16[32,768]{1,0:T(8,128)(2,1)}) %reduce-scatter.3.cloned.1.call-update) | async-done | bytes 49168 | tf_op jit(solution)/shard_map/reduce_scatter | solution.py:48
  218.7 58.6 %reduce-scatter.5.cloned.1.call-done = bf16[32,768]{1,0:T(8,128)(2,1)} async-done(((bf16[512,768]{1,0:T(8,128)(2,1)}), bf16[32,768]{1,0:T(8,128)(2,1)}) %reduce-scatter.5.cloned.1.call-update) | async-done | bytes 49168 | tf_op jit(solution)/shard_map/reduce_scatter | solution.py:60
Async XLA Ops:
  7.2 43.6 %copy-start = (bf16[1536,768]{1,0:T(8,128)(2,1)S(1)}, bf16[1536,768]{1,0:T(8,128)(2,1)}, u32[]{:S(2)}) copy-start(bf16[1536,768]{1,0:T(8,128)(2,1)} %param.6) | copy-start | bytes 7077892
  7.2 149.9 %all-reduce.3.cloned.1.call-start = ((), (), s32[]{:S(2)}) async-start(), calls=%async_computation.4 | async-start | bytes 6291456 | tf_op jit(solution)/shard_map/psum | solution.py:45
  29.7 16.9 %copy-start.2 = (bf16[512,768]{1,0:T(8,128)(2,1)}, bf16[512,768]{1,0:T(8,128)(2,1)S(1)}, u32[]{:S(2)}) copy-start(bf16[512,768]{1,0:T(8,128)(2,1)S(1)} %all_gather.6) | copy-start | bytes 2359300
  53.4 165.3 %reduce-scatter.3.cloned.1.call-start = ((), (), s32[]{:S(2)}) async-start(), calls=%async_computation.2 | async-start | bytes 835584 | tf_op jit(solution)/shard_map/reduce_scatter | solution.py:48
  161.5 115.8 %reduce-scatter.5.cloned.1.call-start = ((), (), s32[]{:S(2)}) async-start(), calls=%async_computation.3 | async-start | bytes 835584 | tf_op jit(solution)/shard_map/reduce_scatter | solution.py:60
  161.5 5.3 %copy-start.3 = (bf16[768,1536]{1,0:T(8,128)(2,1)S(1)}, bf16[768,1536]{1,0:T(8,128)(2,1)}, u32[]{:S(2)}) copy-start(bf16[768,1536]{1,0:T(8,128)(2,1)} %param.5) | copy-start | bytes 7077892
  165.6 1.1 copy-start.1
Sparse Core Ops, SparseCore 0:
  53.5 103.5 all-reduce.2
  161.6 57.0 reduce-scatter.2
  221.9 55.3 reduce-scatter.4
where the time goes:
time: 284 us
  waiting for transfers between devices  198 us (70%)
  blocking collectives  39.4 us (14%)
  matrix products  22.6 us (8%)
  between operations  13.8 us (5%)
  local copies, waits for them, and re-layouts  5.42 us (2%)
  other arithmetic  4.11 us (1%)
    psum x1, waiting for transfers between devices, local(): lax.psum(partial_value.astype(jnp.bfloat16), 'row').astype(jnp.float32)  104 us
    reduce_scatter x1, waiting for transfers between devices, local(): lax.psum_scatter(contract_cols(picked, weight_in).astype(jnp.bfloat16), '...  58.6 us
    reduce_scatter x1, waiting for transfers between devices, local(): lax.psum_scatter(jnp.dot(picked, weight_out, preferred_element_type=jnp.f...  36.1 us
    all_gather x1, blocking collectives, local(): lax.all_gather(tokens, 'col', axis=0, tiled=True)  22.5 us
    all_gather x1, blocking collectives, local(): lax.all_gather(cotangent, 'col', axis=0, tiled=True)  16.9 us
    dot_general x2, matrix products, contract_rows(): lax.dot_general(left, right, (((0,), (0,)), ((), ())), preferred_element_...  9.24 us
  transfers between devices with their start and end apart: 3, of which 3 were waited for; matrix products, arithmetic and copies ran while one was open for 7% of the time, Pallas kernels for 0%

commit v1 on v0

v1 whole, which is shorter than its diff:
```python
import jax
import jax.numpy as jnp
from jax import lax
from jax.sharding import PartitionSpec as P

tanh_gain = 0.7978845608028654
cubic_term = 0.044715
side = 4
planes = 8


def gelu_parts(hidden):
    squared = hidden * hidden
    tangent = jnp.tanh(tanh_gain * (hidden + cubic_term * squared * hidden))
    value = 0.5 * hidden * (1.0 + tangent)
    slope = 0.5 * (1.0 + tangent) + 0.5 * hidden * (1.0 - tangent * tangent) * tanh_gain * (
        1.0 + 3.0 * cubic_term * squared
    )
    return value, slope


def contract_rows(left, right):
    return lax.dot_general(
        left, right, (((0,), (0,)), ((), ())), preferred_element_type=jnp.float32
    )


def contract_cols(left, right):
    return lax.dot_general(
        left, right, (((1,), (1,)), ((), ())), preferred_element_type=jnp.float32
    )


def device(x, y, z, core):
    return ((x % side) * side + y % side) * (planes * 2) + z * 2 + core


def ring_pairs(first, shift):
    pairs = []
    for x in range(side):
        for y in range(side):
            for z in range(planes):
                for core in range(2):
                    along_x = (core == 0) == first
                    to = device(x + shift, y, z, core) if along_x else device(x, y + shift, z, core)
                    pairs.append((device(x, y, z, core), to))
    return pairs


ring_shift = {
    (first, shift): ring_pairs(first, shift) for first in (True, False) for shift in (1, 2, 3)
}
core_pairs = [(i, i ^ 1) for i in range(planes * 2)]
plane_groups = [[z * 2 + core for z in range(planes)] for core in range(2)]
both = ("row", "col")


def other_core(block):
    return lax.ppermute(block, "col", core_pairs)


def over_planes(blocks):
    return lax.all_to_all(blocks, "col", 0, 0, tiled=True, axis_index_groups=plane_groups)


def gather_tokens(block):
    rows, width = block.shape
    mine = over_planes(jnp.broadcast_to(block[None], (planes, rows, width)))
    mine = mine.reshape(planes * rows, width)
    return jnp.concatenate([mine, other_core(mine)], axis=0)


def scatter_tokens(partial):
    half, width = partial.shape[0] // 2, partial.shape[1]
    pair = partial[:half].astype(jnp.float32) + other_core(partial[half:]).astype(jnp.float32)
    blocks = pair.astype(jnp.bfloat16).reshape(planes, half // planes, width)
    return jnp.sum(over_planes(blocks).astype(jnp.float32), axis=0).astype(jnp.bfloat16)


def ring_reduce(partial, place, first):
    blocks = partial.reshape(side, partial.shape[0] // side, partial.shape[1])
    came = [
        lax.ppermute(
            lax.dynamic_index_in_dim(blocks, (place + shift) % side, 0, keepdims=False),
            both,
            ring_shift[first, shift],
        )
        for shift in (1, 3, 2)
    ]
    total = lax.dynamic_index_in_dim(blocks, place, 0, keepdims=False).astype(jnp.float32)
    for block in came:
        total = total + block.astype(jnp.float32)
    return total


def ring_gather(block, place, first):
    rows, width = block.shape
    whole = jnp.zeros((side, rows, width), block.dtype)
    whole = lax.dynamic_update_index_in_dim(whole, block, place, 0)
    for shift in (1, 3, 2):
        came = lax.ppermute(block, both, ring_shift[first, shift])
        whole = lax.dynamic_update_index_in_dim(whole, came, (place - shift) % side, 0)
    return whole.reshape(side * rows, width)


def local(tokens, weight_in, weight_out, cotangent):
    chip, core = lax.axis_index("row"), lax.axis_index("col") % 2
    x, y = chip // side, chip % side
    place_one, place_two = jnp.where(core == 0, x, y), jnp.where(core == 0, y, x)

    def reduce_features(partial):
        total = ring_reduce(partial, place_one, True)
        return ring_reduce(total.astype(jnp.bfloat16), place_two, False)

    def gather_features(block):
        return ring_gather(ring_gather(block, place_two, False), place_one, True)

    token_block = gather_tokens(tokens)
    grad_block = gather_tokens(cotangent)
    grad_scale = token_block.shape[0] ** (-0.5)
    partial_value = jnp.dot(token_block, weight_in, preferred_element_type=jnp.float32)
    hidden = reduce_features(partial_value.astype(jnp.bfloat16))
    value, slope = gelu_parts(hidden)
    activation = gather_features(value.astype(jnp.bfloat16))
    grad_partial = contract_cols(grad_block, weight_out)
    grad_activation = reduce_features(grad_partial.astype(jnp.bfloat16))
    grad_hidden = gather_features((grad_activation * slope).astype(jnp.bfloat16))
    output = scatter_tokens(
        jnp.dot(activation, weight_out, preferred_element_type=jnp.float32).astype(jnp.bfloat16)
    )
    grad_out = (contract_rows(activation, grad_block) * grad_scale).astype(jnp.bfloat16)
    grad_tokens = scatter_tokens(contract_cols(grad_hidden, weight_in).astype(jnp.bfloat16))
    grad_in = (contract_rows(token_block, grad_hidden) * grad_scale).astype(jnp.bfloat16)
    return (output, grad_tokens, grad_in, grad_out)


def solution(mesh):
    in_specs = (P("col", "row"), P("row", "col"), P("col", "row"), P("col", "row"))
    out_specs = (P("col", "row"), P("col", "row"), P("row", "col"), P("col", "row"))
    return jax.shard_map(local, mesh=mesh, in_specs=in_specs, out_specs=out_specs, check_vma=False)
```

time: 284 us -> 151 us (0.53)
  waiting for transfers between devices: 198 us -> 52.5 us
  starting transfers between devices: 0.12 us -> 40.7 us
  blocking collectives: 39.4 us -> 22.9 us
  between operations: 13.8 us -> 1.11 us
  matrix products: 22.6 us -> 18.5 us
  local copies, waits for them, and re-layouts: 5.42 us -> 9.08 us
    psum x1 -> x0, waiting for transfers between devices: 104 us -> none  [local(): lax.psum(partial_value.astype(jnp.bfloat16), 'row').astype(jnp.float32)]
    reduce_scatter x2 -> x0, waiting for transfers between devices: 94.7 us -> none  [the longest x1 58.6 us: local(): lax.psum_scatter(contract_cols(picked, weight_in).astype(jnp.bfloat16), '...]
    all_gather x2 -> x0, blocking collectives: 39.4 us -> none  [the longest x1 22.5 us: local(): lax.all_gather(tokens, 'col', axis=0, tiled=True)]
    ppermute x0 -> x28, starting transfers between devices: none -> 30.2 us  [the longest x12 15.3 us: ring_gather(): came = lax.ppermute(block, both, ring_shift[first, shift])]
    ppermute x0 -> x28, waiting for transfers between devices: none -> 26.9 us  [the longest x12 16.2 us: ring_reduce(): lax.ppermute(lax.dynamic_index_in_dim(blocks, (place + shift) % side, 0,...]
    all_to_all x0 -> x3, waiting for transfers between devices: none -> 25.6 us  [over_planes(): lax.all_to_all(blocks, 'col', 0, 0, tiled=True, axis_index_groups=plane_g...]
    all_to_all x0 -> x1, blocking collectives: none -> 22.9 us  [over_planes(): lax.all_to_all(blocks, 'col', 0, 0, tiled=True, axis_index_groups=plane_g...]
    all_to_all x0 -> x3, starting transfers between devices: none -> 10.6 us  [over_planes(): lax.all_to_all(blocks, 'col', 0, 0, tiled=True, axis_index_groups=plane_g...]
  transfers between devices with their start and end apart: 3 -> 31, of which waited for: 3 -> 16; matrix products, arithmetic and copies ran while one was open for 7% -> 19% of each run, Pallas kernels for 0% -> 0%
where the time goes in v1:
time: 151 us
  waiting for transfers between devices  52.5 us (35%)
  starting transfers between devices  40.7 us (27%)
  blocking collectives  22.9 us (15%)
  matrix products  18.5 us (12%)
  local copies, waits for them, and re-layouts  9.08 us (6%)
  other arithmetic  5.97 us (4%)
    all_to_all x3, waiting for transfers between devices, over_planes(): lax.all_to_all(blocks, 'col', 0, 0, tiled=True, axis_index_groups=plane_g...  25.6 us
    all_to_all x1, blocking collectives, over_planes(): lax.all_to_all(blocks, 'col', 0, 0, tiled=True, axis_index_groups=plane_g...  22.9 us
    ppermute x12, waiting for transfers between devices, ring_reduce(): lax.ppermute(lax.dynamic_index_in_dim(blocks, (place + shift) % side, 0,...  16.2 us
    ppermute x12, starting transfers between devices, ring_gather(): came = lax.ppermute(block, both, ring_shift[first, shift])  15.3 us
    ppermute x12, starting transfers between devices, ring_reduce(): lax.ppermute(lax.dynamic_index_in_dim(blocks, (place + shift) % side, 0,...  14.6 us
    all_to_all x3, starting transfers between devices, over_planes(): lax.all_to_all(blocks, 'col', 0, 0, tiled=True, axis_index_groups=plane_g...  10.6 us
    ppermute x12, waiting for transfers between devices, ring_gather(): came = lax.ppermute(block, both, ring_shift[first, shift])  9.02 us
    dot_general x2, matrix products, contract_rows(): lax.dot_general(left, right, (((0,), (0,)), ((), ())), preferred_element_...  8.76 us
  transfers between devices with their start and end apart: 31, of which 16 were waited for; matrix products, arithmetic and copies ran while one was open for 19% of the time, Pallas kernels for 0%

profile of v1, /device:TPU:24, one launch (start us, length us, event | category | flops | bytes accessed | tf_op | source)
XLA Modules:
  0.0 150.8 jit_solution(11644793030687190841)
XLA Ops:
  1.6 22.9 %all_to_all.20 = bf16[8,32,768]{2,1,0:T(8,128)(2,1)S(1)} all-to-all(bf16[8,32,768]{2,1,0:T(8,128)(2,1)S(1)} %broadcast_in_dim.71), channel_id=1, replica_groups={{0,2,4,6,8,10,12,14},{1,3,5,7,9,11,13,15},{16,18,20,22,24,26,28,30},{17..., dimensions={0} | all-to-all | bytes 786432 | tf_op jit(solution)/shard_map/all_to_all | solution.py:63
  24.6 1.6 %broadcast_in_dim.62 = bf16[8,32,768]{2,1,0:T(8,128)(2,1)} broadcast(bf16[32,768]{1,0:T(8,128)(2,1)} %param.4), dimensions={1,2} | broadcast | bytes 442368 | tf_op jit(solution)/shard_map/broadcast_in_dim | solution.py:68
  26.1 3.5 %all-to-all-start = ((bf16[8,32,768]{2,1,0:T(8,128)(2,1)}), bf16[8,32,768]{2,1,0:T(8,128)(2,1)S(1)}, u32[]{:S(2)}, u32[]{:S(2)}) async-start(bf16[8,32,768]{2,1,0:T(8,128)(2,1)} %broadcast_in_dim.62), calls=%async_computation | async-start | bytes 786432 | tf_op jit(solution)/shard_map/all_to_all | solution.py:63
  29.9 13.2 %all-to-all-done = bf16[8,32,768]{2,1,0:T(8,128)(2,1)S(1)} async-done(((bf16[8,32,768]{2,1,0:T(8,128)(2,1)}), bf16[8,32,768]{2,1,0:T(8,128)(2,1)S(1)}, u32[]{:S(2)}, u32[]{:S(2)}) %all-to-all-start) | async-done | bytes 393248 | tf_op jit(solution)/shard_map/all_to_all | solution.py:63
  43.1 3.4 %convolution_convert_fusion = bf16[512,1536]{1,0:T(8,128)(2,1)S(1)} fusion(bf16[1536,768]{1,0:T(8,128)(2,1)} %param.6, bf16[256,768]{1,0:T(8,128)(2,1)S(1)} %collective-permute-done.14, bf16[256,768]{1,0:T(8,128)(2,1)S(1)} %bitcast.117), kind=kOutput, calls=%fused_computation.2 | convolution fusion | flops 1210318848 | bytes 4718592 | tf_op jit(solution)/shard_map/dot_general | solution.py:29
  46.5 1.6 %collective-permute-start.15 = (bf16[128,1536]{1,0:T(8,128)(2,1)S(1)}, bf16[128,1536]{1,0:T(8,128)(2,1)S(1)}, u32[]{:S(2)}, u32[]{:S(2)}) collective-permute-start(bf16[128,1536]{1,0:T(8,128)(2,1)S(1)} %get-tuple-element.8), channel_id=1, source_target_pairs={{0,64},{1,17},{2,66},{3,19},{4,68},{5,21},{6,70},{7,23},{8,72},{9,... | collective-permute-start | bytes 1179656 | tf_op jit(solution)/shard_map/ppermute | solution.py:83
  48.1 1.7 %collective-permute-start.16 = (bf16[128,1536]{1,0:T(8,128)(2,1)S(1)}, bf16[128,1536]{1,0:T(8,128)(2,1)S(1)}, u32[]{:S(2)}, u32[]{:S(2)}) collective-permute-start(bf16[128,1536]{1,0:T(8,128)(2,1)S(1)} %get-tuple-element.10), channel_id=1, source_target_pairs={{0,192},{1,49},{2,194},{3,51},{4,196},{5,53},{6,198},{7,55},{8,200... | collective-permute-start | bytes 1179656 | tf_op jit(solution)/shard_map/ppermute | solution.py:83
  49.9 1.8 %collective-permute-start.17 = (bf16[128,1536]{1,0:T(8,128)(2,1)S(1)}, bf16[128,1536]{1,0:T(8,128)(2,1)S(1)}, u32[]{:S(2)}, u32[]{:S(2)}) collective-permute-start(bf16[128,1536]{1,0:T(8,128)(2,1)S(1)} %get-tuple-element.9), channel_id=1, source_target_pairs={{0,128},{1,33},{2,130},{3,35},{4,132},{5,37},{6,134},{7,39},{8,136... | collective-permute-start | bytes 1179656 | tf_op jit(solution)/shard_map/ppermute | solution.py:83
  53.9 2.6 %collective-permute-start.2 = (bf16[128,1536]{1,0:T(8,128)(2,1)S(1)}, bf16[128,1536]{1,0:T(8,128)(2,1)S(1)}, u32[]{:S(2)}, u32[]{:S(2)}) collective-permute-start(bf16[128,1536]{1,0:T(8,128)(2,1)S(1)} %get-tuple-element.13), channel_id=1, source_target_pairs={{0,192},{1,49},{2,194},{3,51},{4,196},{5,53},{6,198},{7,55},{8,200... | collective-permute-start | bytes 1179656 | tf_op jit(solution)/shard_map/ppermute | solution.py:83
  57.4 2.0 %collective-permute-done.16 = bf16[128,1536]{1,0:T(8,128)(2,1)S(1)} collective-permute-done((bf16[128,1536]{1,0:T(8,128)(2,1)S(1)}, bf16[128,1536]{1,0:T(8,128)(2,1)S(1)}, u32[]{:S(2)}, u32[]{:S(2)}) %collective-permute-start.16) | collective-permute-done | bytes 393248 | tf_op jit(solution)/shard_map/ppermute | solution.py:83
  62.1 1.8 %collective-permute-start.19 = (bf16[32,1536]{1,0:T(8,128)(2,1)}, bf16[32,1536]{1,0:T(8,128)(2,1)}, u32[]{:S(2)}, u32[]{:S(2)}) collective-permute-start(bf16[32,1536]{1,0:T(8,128)(2,1)} %get-tuple-element.16), channel_id=1, source_target_pairs={{0,48},{1,193},{2,50},{3,195},{4,52},{5,197},{6,54},{7,199},{8,56}... | collective-permute-start | bytes 294920 | tf_op jit(solution)/shard_map/ppermute | solution.py:83
  63.9 2.9 %collective-permute-done.1 = bf16[128,1536]{1,0:T(8,128)(2,1)S(1)} collective-permute-done((bf16[128,1536]{1,0:T(8,128)(2,1)S(1)}, bf16[128,1536]{1,0:T(8,128)(2,1)S(1)}, u32[]{:S(2)}, u32[]{:S(2)}) %collective-permute-start.1) | collective-permute-done | bytes 393248 | tf_op jit(solution)/shard_map/ppermute | solution.py:83
  66.7 4.7 %collective-permute-done.3 = bf16[128,1536]{1,0:T(8,128)(2,1)S(1)} collective-permute-done((bf16[128,1536]{1,0:T(8,128)(2,1)S(1)}, bf16[128,1536]{1,0:T(8,128)(2,1)S(1)}, u32[]{:S(2)}, u32[]{:S(2)}) %collective-permute-start.3) | collective-permute-done | bytes 393248 | tf_op jit(solution)/shard_map/ppermute | solution.py:83
  72.4 2.0 %collective-permute-start.5 = (bf16[32,1536]{1,0:T(8,128)(2,1)}, bf16[32,1536]{1,0:T(8,128)(2,1)}, u32[]{:S(2)}, u32[]{:S(2)}) collective-permute-start(bf16[32,1536]{1,0:T(8,128)(2,1)} %get-tuple-element.19), channel_id=1, source_target_pairs={{0,48},{1,193},{2,50},{3,195},{4,52},{5,197},{6,54},{7,199},{8,56}... | collective-permute-start | bytes 294920 | tf_op jit(solution)/shard_map/ppermute | solution.py:83
  75.6 1.7 %collective-permute-done.4 = bf16[32,1536]{1,0:T(8,128)(2,1)} collective-permute-done((bf16[32,1536]{1,0:T(8,128)(2,1)}, bf16[32,1536]{1,0:T(8,128)(2,1)}, u32[]{:S(2)}, u32[]{:S(2)}) %collective-permute-start.4) | collective-permute-done | bytes 98336 | tf_op jit(solution)/shard_map/ppermute | solution.py:83
  78.5 2.3 %collective-permute-done.6 = bf16[32,1536]{1,0:T(8,128)(2,1)} collective-permute-done((bf16[32,1536]{1,0:T(8,128)(2,1)}, bf16[32,1536]{1,0:T(8,128)(2,1)}, u32[]{:S(2)}, u32[]{:S(2)}) %collective-permute-start.6) | collective-permute-done | bytes 98336 | tf_op jit(solution)/shard_map/ppermute | solution.py:83
  86.7 2.3 %collective-permute-start.7 = (bf16[32,1536]{1,0:T(8,128)(2,1)S(1)}, bf16[32,1536]{1,0:T(8,128)(2,1)S(1)}, u32[]{:S(2)}, u32[]{:S(2)}) collective-permute-start(bf16[32,1536]{1,0:T(8,128)(2,1)S(1)} %get-tuple-element.7), channel_id=1, source_target_pairs={{0,16},{1,65},{2,18},{3,67},{4,20},{5,69},{6,22},{7,71},{8,24},{9,... | collective-permute-start | bytes 294920 | tf_op jit(solution)/shard_map/ppermute | solution.py:101
  89.0 2.2 %collective-permute-start.9 = (bf16[32,1536]{1,0:T(8,128)(2,1)S(1)}, bf16[32,1536]{1,0:T(8,128)(2,1)S(1)}, u32[]{:S(2)}, u32[]{:S(2)}) collective-permute-start(bf16[32,1536]{1,0:T(8,128)(2,1)S(1)} %get-tuple-element.7), channel_id=1, source_target_pairs={{0,32},{1,129},{2,34},{3,131},{4,36},{5,133},{6,38},{7,135},{8,40}... | collective-permute-start | bytes 294920 | tf_op jit(solution)/shard_map/ppermute | solution.py:101
  92.7 1.8 %collective-permute-start.25 = (bf16[128,1536]{1,0:T(8,128)(2,1)S(1)}, bf16[128,1536]{1,0:T(8,128)(2,1)S(1)}, u32[]{:S(2)}, u32[]{:S(2)}) collective-permute-start(bf16[128,1536]{1,0:T(8,128)(2,1)S(1)} %bitcast.111), channel_id=1, source_target_pairs={{0,192},{1,49},{2,194},{3,51},{4,196},{5,53},{6,198},{7,55},{8,200... | collective-permute-start | bytes 1179656 | tf_op jit(solution)/shard_map/ppermute | solution.py:101
  94.9 2.0 %collective-permute-done.8 = bf16[32,1536]{1,0:T(8,128)(2,1)S(1)} collective-permute-done((bf16[32,1536]{1,0:T(8,128)(2,1)S(1)}, bf16[32,1536]{1,0:T(8,128)(2,1)S(1)}, u32[]{:S(2)}, u32[]{:S(2)}) %collective-permute-start.8) | collective-permute-done | bytes 98336 | tf_op jit(solution)/shard_map/ppermute | solution.py:101
  96.9 1.6 %collective-permute-start.10 = (bf16[128,1536]{1,0:T(8,128)(2,1)S(1)}, bf16[128,1536]{1,0:T(8,128)(2,1)S(1)}, u32[]{:S(2)}, u32[]{:S(2)}) collective-permute-start(bf16[128,1536]{1,0:T(8,128)(2,1)S(1)} %bitcast.106), channel_id=1, source_target_pairs={{0,64},{1,17},{2,66},{3,19},{4,68},{5,21},{6,70},{7,23},{8,72},{9,... | collective-permute-start | bytes 1179656 | tf_op jit(solution)/shard_map/ppermute | solution.py:101
  98.5 1.7 %collective-permute-start.11 = (bf16[128,1536]{1,0:T(8,128)(2,1)S(1)}, bf16[128,1536]{1,0:T(8,128)(2,1)S(1)}, u32[]{:S(2)}, u32[]{:S(2)}) collective-permute-start(bf16[128,1536]{1,0:T(8,128)(2,1)S(1)} %bitcast.107), channel_id=1, source_target_pairs={{0,192},{1,49},{2,194},{3,51},{4,196},{5,53},{6,198},{7,55},{8,200... | collective-permute-start | bytes 1179656 | tf_op jit(solution)/shard_map/ppermute | solution.py:101
  106.5 2.5 %collective-permute-done.10 = bf16[128,1536]{1,0:T(8,128)(2,1)S(1)} collective-permute-done((bf16[128,1536]{1,0:T(8,128)(2,1)S(1)}, bf16[128,1536]{1,0:T(8,128)(2,1)S(1)}, u32[]{:S(2)}, u32[]{:S(2)}) %collective-permute-start.10) | collective-permute-done | bytes 393248 | tf_op jit(solution)/shard_map/ppermute | solution.py:101
  109.8 2.7 %collective-permute-done.11 = bf16[128,1536]{1,0:T(8,128)(2,1)S(1)} collective-permute-done((bf16[128,1536]{1,0:T(8,128)(2,1)S(1)}, bf16[128,1536]{1,0:T(8,128)(2,1)S(1)}, u32[]{:S(2)}, u32[]{:S(2)}) %collective-permute-start.11) | collective-permute-done | bytes 393248 | tf_op jit(solution)/shard_map/ppermute | solution.py:101
  114.9 3.7 %all-to-all-start.3 = ((bf16[8,32,768]{2,1,0:T(8,128)(2,1)}), bf16[8,32,768]{2,1,0:T(8,128)(2,1)S(1)}, u32[]{:S(2)}, u32[]{:S(2)}) async-start(bf16[8,32,768]{2,1,0:T(8,128)(2,1)} %bitcast.43), calls=%async_computation.3 | async-start | bytes 786432 | tf_op jit(solution)/shard_map/all_to_all | solution.py:63
  118.6 3.5 %convolution_convert_fusion.3 = bf16[512,768]{1,0:T(8,128)(2,1)S(1)} fusion(bf16[512,1536]{1,0:T(8,128)(2,1)} %bitcast.20, bf16[1536,768]{1,0:T(8,128)(2,1)} %param.6), kind=kOutput, calls=%fused_computation.5 | convolution fusion | flops 1208352768 | bytes 4718592 | tf_op jit(solution)/shard_map/dot_general | solution.py:129
  122.2 1.7 %collective-permute-done.13 = bf16[256,768]{1,0:T(8,128)(2,1)S(1)} collective-permute-done((bf16[256,768]{1,0:T(8,128)(2,1)S(1)}, bf16[256,768]{1,0:T(8,128)(2,1)S(1)}, u32[]{:S(2)}, u32[]{:S(2)}) %collective-permute-start.13) | collective-permute-done | bytes 393248 | tf_op jit(solution)/shard_map/ppermute | solution.py:59
  124.8 7.5 %all-to-all-done.3 = bf16[8,32,768]{2,1,0:T(8,128)(2,1)S(1)} async-done(((bf16[8,32,768]{2,1,0:T(8,128)(2,1)}), bf16[8,32,768]{2,1,0:T(8,128)(2,1)S(1)}, u32[]{:S(2)}, u32[]{:S(2)}) %all-to-all-start.3) | async-done | bytes 393248 | tf_op jit(solution)/shard_map/all_to_all | solution.py:63
  132.4 3.5 %all-to-all-start.1 = ((bf16[8,32,768]{2,1,0:T(8,128)(2,1)}), bf16[8,32,768]{2,1,0:T(8,128)(2,1)S(1)}, u32[]{:S(2)}, u32[]{:S(2)}) async-start(bf16[8,32,768]{2,1,0:T(8,128)(2,1)} %bitcast.21), calls=%async_computation.1 | async-start | bytes 786432 | tf_op jit(solution)/shard_map/all_to_all | solution.py:63
  135.8 4.5 %multiply_convert_fusion.1 = bf16[768,1536]{1,0:T(8,128)(2,1)} fusion(bf16[512,1536]{1,0:T(8,128)(2,1)} %bitcast.101, bf16[256,768]{1,0:T(8,128)(2,1)} %copy-done.5, bf16[256,768]{1,0:T(8,128)(2,1)} %bitcast.121), kind=kOutput, calls=%fused_computation.1 | convolution fusion | flops 1211891712 | bytes 4718592 | tf_op jit(solution)/shard_map/dot_general | solution.py:23
  140.4 4.2 %multiply_convert_fusion = bf16[1536,768]{1,0:T(8,128)(2,1)} fusion(bf16[512,1536]{1,0:T(8,128)(2,1)} %bitcast.20, bf16[256,768]{1,0:T(8,128)(2,1)S(1)} %copy-done.4, bf16[256,768]{1,0:T(8,128)(2,1)S(1)} %bitcast.118), kind=kOutput, calls=%fused_computation | convolution fusion | flops 1211891712 | bytes 4718592 | tf_op jit(solution)/shard_map/dot_general | solution.py:23
  145.3 4.9 %all-to-all-done.1 = bf16[8,32,768]{2,1,0:T(8,128)(2,1)S(1)} async-done(((bf16[8,32,768]{2,1,0:T(8,128)(2,1)}), bf16[8,32,768]{2,1,0:T(8,128)(2,1)S(1)}, u32[]{:S(2)}, u32[]{:S(2)}) %all-to-all-start.1) | async-done | bytes 393248 | tf_op jit(solution)/shard_map/all_to_all | solution.py:63
  (83 shorter events, 29.8 us)
Async XLA Ops:
  0.6 51.0 %copy-start = (bf16[768,1536]{1,0:T(8,128)(2,1)S(1)}, bf16[768,1536]{1,0:T(8,128)(2,1)}, u32[]{:S(2)}) copy-start(bf16[768,1536]{1,0:T(8,128)(2,1)} %param.5) | copy-start | bytes 7077892
  26.1 16.9 %all-to-all-start = ((bf16[8,32,768]{2,1,0:T(8,128)(2,1)}), bf16[8,32,768]{2,1,0:T(8,128)(2,1)S(1)}, u32[]{:S(2)}, u32[]{:S(2)}) async-start(bf16[8,32,768]{2,1,0:T(8,128)(2,1)} %broadcast_in_dim.62), calls=%async_computation | async-start | bytes 786432 | tf_op jit(solution)/shard_map/all_to_all | solution.py:63
  29.6 13.4 %collective-permute-start.14 = (bf16[256,768]{1,0:T(8,128)(2,1)S(1)}, bf16[256,768]{1,0:T(8,128)(2,1)S(1)}, u32[]{:S(2)}, u32[]{:S(2)}) collective-permute-start(bf16[256,768]{1,0:T(8,128)(2,1)S(1)} %bitcast.116), channel_id=1, source_target_pairs={{0,1},{1,0},{2,3},{3,2},{4,5},{5,4},{6,7},{7,6},{8,9},{9,8},{10,11... | collective-permute-start | bytes 1179656 | tf_op jit(solution)/shard_map/ppermute | solution.py:59
  43.0 8.6 %collective-permute-start = (bf16[256,768]{1,0:T(8,128)(2,1)S(1)}, bf16[256,768]{1,0:T(8,128)(2,1)S(1)}, u32[]{:S(2)}, u32[]{:S(2)}) collective-permute-start(bf16[256,768]{1,0:T(8,128)(2,1)S(1)} %bitcast.119), channel_id=1, source_target_pairs={{0,1},{1,0},{2,3},{3,2},{4,5},{5,4},{6,7},{7,6},{8,9},{9,8},{10,11... | collective-permute-start | bytes 1179656 | tf_op jit(solution)/shard_map/ppermute | solution.py:59
  46.5 10.0 %collective-permute-start.15 = (bf16[128,1536]{1,0:T(8,128)(2,1)S(1)}, bf16[128,1536]{1,0:T(8,128)(2,1)S(1)}, u32[]{:S(2)}, u32[]{:S(2)}) collective-permute-start(bf16[128,1536]{1,0:T(8,128)(2,1)S(1)} %get-tuple-element.8), channel_id=1, source_target_pairs={{0,64},{1,17},{2,66},{3,19},{4,68},{5,21},{6,70},{7,23},{8,72},{9,... | collective-permute-start | bytes 1179656 | tf_op jit(solution)/shard_map/ppermute | solution.py:83
  48.1 11.3 %collective-permute-start.16 = (bf16[128,1536]{1,0:T(8,128)(2,1)S(1)}, bf16[128,1536]{1,0:T(8,128)(2,1)S(1)}, u32[]{:S(2)}, u32[]{:S(2)}) collective-permute-start(bf16[128,1536]{1,0:T(8,128)(2,1)S(1)} %get-tuple-element.10), channel_id=1, source_target_pairs={{0,192},{1,49},{2,194},{3,51},{4,196},{5,53},{6,198},{7,55},{8,200... | collective-permute-start | bytes 1179656 | tf_op jit(solution)/shard_map/ppermute | solution.py:83
  49.9 11.1 %collective-permute-start.17 = (bf16[128,1536]{1,0:T(8,128)(2,1)S(1)}, bf16[128,1536]{1,0:T(8,128)(2,1)S(1)}, u32[]{:S(2)}, u32[]{:S(2)}) collective-permute-start(bf16[128,1536]{1,0:T(8,128)(2,1)S(1)} %get-tuple-element.9), channel_id=1, source_target_pairs={{0,128},{1,33},{2,130},{3,35},{4,132},{5,37},{6,134},{7,39},{8,136... | collective-permute-start | bytes 1179656 | tf_op jit(solution)/shard_map/ppermute | solution.py:83
  53.2 13.5 %collective-permute-start.1 = (bf16[128,1536]{1,0:T(8,128)(2,1)S(1)}, bf16[128,1536]{1,0:T(8,128)(2,1)S(1)}, u32[]{:S(2)}, u32[]{:S(2)}) collective-permute-start(bf16[128,1536]{1,0:T(8,128)(2,1)S(1)} %get-tuple-element.11), channel_id=1, source_target_pairs={{0,64},{1,17},{2,66},{3,19},{4,68},{5,21},{6,70},{7,23},{8,72},{9,... | collective-permute-start | bytes 1179656 | tf_op jit(solution)/shard_map/ppermute | solution.py:83
  53.9 12.8 %collective-permute-start.2 = (bf16[128,1536]{1,0:T(8,128)(2,1)S(1)}, bf16[128,1536]{1,0:T(8,128)(2,1)S(1)}, u32[]{:S(2)}, u32[]{:S(2)}) collective-permute-start(bf16[128,1536]{1,0:T(8,128)(2,1)S(1)} %get-tuple-element.13), channel_id=1, source_target_pairs={{0,192},{1,49},{2,194},{3,51},{4,196},{5,53},{6,198},{7,55},{8,200... | collective-permute-start | bytes 1179656 | tf_op jit(solution)/shard_map/ppermute | solution.py:83
  56.5 14.9 %collective-permute-start.3 = (bf16[128,1536]{1,0:T(8,128)(2,1)S(1)}, bf16[128,1536]{1,0:T(8,128)(2,1)S(1)}, u32[]{:S(2)}, u32[]{:S(2)}) collective-permute-start(bf16[128,1536]{1,0:T(8,128)(2,1)S(1)} %get-tuple-element.12), channel_id=1, source_target_pairs={{0,128},{1,33},{2,130},{3,35},{4,132},{5,37},{6,134},{7,39},{8,136... | collective-permute-start | bytes 1179656 | tf_op jit(solution)/shard_map/ppermute | solution.py:83
  61.8 12.6 %collective-permute-start.18 = (bf16[32,1536]{1,0:T(8,128)(2,1)S(1)}, bf16[32,1536]{1,0:T(8,128)(2,1)}, u32[]{:S(2)}, u32[]{:S(2)}) collective-permute-start(bf16[32,1536]{1,0:T(8,128)(2,1)S(1)} %get-tuple-element.14), channel_id=1, source_target_pairs={{0,16},{1,65},{2,18},{3,67},{4,20},{5,69},{6,22},{7,71},{8,24},{9,... | collective-permute-start | bytes 294920 | tf_op jit(solution)/shard_map/ppermute | solution.py:83
  62.1 13.6 %collective-permute-start.19 = (bf16[32,1536]{1,0:T(8,128)(2,1)}, bf16[32,1536]{1,0:T(8,128)(2,1)}, u32[]{:S(2)}, u32[]{:S(2)}) collective-permute-start(bf16[32,1536]{1,0:T(8,128)(2,1)} %get-tuple-element.16), channel_id=1, source_target_pairs={{0,48},{1,193},{2,50},{3,195},{4,52},{5,197},{6,54},{7,199},{8,56}... | collective-permute-start | bytes 294920 | tf_op jit(solution)/shard_map/ppermute | solution.py:83
  66.7 8.9 %collective-permute-start.20 = (bf16[32,1536]{1,0:T(8,128)(2,1)}, bf16[32,1536]{1,0:T(8,128)(2,1)}, u32[]{:S(2)}, u32[]{:S(2)}) collective-permute-start(bf16[32,1536]{1,0:T(8,128)(2,1)} %get-tuple-element.15), channel_id=1, source_target_pairs={{0,32},{1,129},{2,34},{3,131},{4,36},{5,133},{6,38},{7,135},{8,40}... | collective-permute-start | bytes 294920 | tf_op jit(solution)/shard_map/ppermute | solution.py:83
  72.4 4.9 %collective-permute-start.4 = (bf16[32,1536]{1,0:T(8,128)(2,1)}, bf16[32,1536]{1,0:T(8,128)(2,1)}, u32[]{:S(2)}, u32[]{:S(2)}) collective-permute-start(bf16[32,1536]{1,0:T(8,128)(2,1)} %get-tuple-element.17), channel_id=1, source_target_pairs={{0,16},{1,65},{2,18},{3,67},{4,20},{5,69},{6,22},{7,71},{8,24},{9,... | collective-permute-start | bytes 294920 | tf_op jit(solution)/shard_map/ppermute | solution.py:83
  72.4 6.1 %collective-permute-start.5 = (bf16[32,1536]{1,0:T(8,128)(2,1)}, bf16[32,1536]{1,0:T(8,128)(2,1)}, u32[]{:S(2)}, u32[]{:S(2)}) collective-permute-start(bf16[32,1536]{1,0:T(8,128)(2,1)} %get-tuple-element.19), channel_id=1, source_target_pairs={{0,48},{1,193},{2,50},{3,195},{4,52},{5,197},{6,54},{7,199},{8,56}... | collective-permute-start | bytes 294920 | tf_op jit(solution)/shard_map/ppermute | solution.py:83
  74.4 6.4 %collective-permute-start.6 = (bf16[32,1536]{1,0:T(8,128)(2,1)}, bf16[32,1536]{1,0:T(8,128)(2,1)}, u32[]{:S(2)}, u32[]{:S(2)}) collective-permute-start(bf16[32,1536]{1,0:T(8,128)(2,1)} %get-tuple-element.18), channel_id=1, source_target_pairs={{0,32},{1,129},{2,34},{3,131},{4,36},{5,133},{6,38},{7,135},{8,40}... | collective-permute-start | bytes 294920 | tf_op jit(solution)/shard_map/ppermute | solution.py:83
  82.2 6.8 %collective-permute-start.21 = (bf16[32,1536]{1,0:T(8,128)(2,1)S(1)}, bf16[32,1536]{1,0:T(8,128)(2,1)S(1)}, u32[]{:S(2)}, u32[]{:S(2)}) collective-permute-start(bf16[32,1536]{1,0:T(8,128)(2,1)S(1)} %get-tuple-element.5), channel_id=1, source_target_pairs={{0,16},{1,65},{2,18},{3,67},{4,20},{5,69},{6,22},{7,71},{8,24},{9,... | collective-permute-start | bytes 294920 | tf_op jit(solution)/shard_map/ppermute | solution.py:101
  83.5 7.6 %collective-permute-start.22 = (bf16[32,1536]{1,0:T(8,128)(2,1)S(1)}, bf16[32,1536]{1,0:T(8,128)(2,1)S(1)}, u32[]{:S(2)}, u32[]{:S(2)}) collective-permute-start(bf16[32,1536]{1,0:T(8,128)(2,1)S(1)} %get-tuple-element.5), channel_id=1, source_target_pairs={{0,48},{1,193},{2,50},{3,195},{4,52},{5,197},{6,54},{7,199},{8,56}... | collective-permute-start | bytes 294920 | tf_op jit(solution)/shard_map/ppermute | solution.py:101
  84.3 6.8 %collective-permute-start.23 = (bf16[32,1536]{1,0:T(8,128)(2,1)S(1)}, bf16[32,1536]{1,0:T(8,128)(2,1)S(1)}, u32[]{:S(2)}, u32[]{:S(2)}) collective-permute-start(bf16[32,1536]{1,0:T(8,128)(2,1)S(1)} %get-tuple-element.5), channel_id=1, source_target_pairs={{0,32},{1,129},{2,34},{3,131},{4,36},{5,133},{6,38},{7,135},{8,40}... | collective-permute-start | bytes 294920 | tf_op jit(solution)/shard_map/ppermute | solution.py:101
  86.7 7.8 %collective-permute-start.7 = (bf16[32,1536]{1,0:T(8,128)(2,1)S(1)}, bf16[32,1536]{1,0:T(8,128)(2,1)S(1)}, u32[]{:S(2)}, u32[]{:S(2)}) collective-permute-start(bf16[32,1536]{1,0:T(8,128)(2,1)S(1)} %get-tuple-element.7), channel_id=1, source_target_pairs={{0,16},{1,65},{2,18},{3,67},{4,20},{5,69},{6,22},{7,71},{8,24},{9,... | collective-permute-start | bytes 294920 | tf_op jit(solution)/shard_map/ppermute | solution.py:101
  89.0 7.9 %collective-permute-start.8 = (bf16[32,1536]{1,0:T(8,128)(2,1)S(1)}, bf16[32,1536]{1,0:T(8,128)(2,1)S(1)}, u32[]{:S(2)}, u32[]{:S(2)}) collective-permute-start(bf16[32,1536]{1,0:T(8,128)(2,1)S(1)} %get-tuple-element.7), channel_id=1, source_target_pairs={{0,48},{1,193},{2,50},{3,195},{4,52},{5,197},{6,54},{7,199},{8,56}... | collective-permute-start | bytes 294920 | tf_op jit(solution)/shard_map/ppermute | solution.py:101
  89.0 7.9 %collective-permute-start.9 = (bf16[32,1536]{1,0:T(8,128)(2,1)S(1)}, bf16[32,1536]{1,0:T(8,128)(2,1)S(1)}, u32[]{:S(2)}, u32[]{:S(2)}) collective-permute-start(bf16[32,1536]{1,0:T(8,128)(2,1)S(1)} %get-tuple-element.7), channel_id=1, source_target_pairs={{0,32},{1,129},{2,34},{3,131},{4,36},{5,133},{6,38},{7,135},{8,40}... | collective-permute-start | bytes 294920 | tf_op jit(solution)/shard_map/ppermute | solution.py:101
  91.2 11.3 %collective-permute-start.24 = (bf16[128,1536]{1,0:T(8,128)(2,1)S(1)}, bf16[128,1536]{1,0:T(8,128)(2,1)S(1)}, u32[]{:S(2)}, u32[]{:S(2)}) collective-permute-start(bf16[128,1536]{1,0:T(8,128)(2,1)S(1)} %bitcast.110), channel_id=1, source_target_pairs={{0,64},{1,17},{2,66},{3,19},{4,68},{5,21},{6,70},{7,23},{8,72},{9,... | collective-permute-start | bytes 1179656 | tf_op jit(solution)/shard_map/ppermute | solution.py:101
  92.7 11.4 %collective-permute-start.25 = (bf16[128,1536]{1,0:T(8,128)(2,1)S(1)}, bf16[128,1536]{1,0:T(8,128)(2,1)S(1)}, u32[]{:S(2)}, u32[]{:S(2)}) collective-permute-start(bf16[128,1536]{1,0:T(8,128)(2,1)S(1)} %bitcast.111), channel_id=1, source_target_pairs={{0,192},{1,49},{2,194},{3,51},{4,196},{5,53},{6,198},{7,55},{8,200... | collective-permute-start | bytes 1179656 | tf_op jit(solution)/shard_map/ppermute | solution.py:101
  94.5 10.4 %collective-permute-start.26 = (bf16[128,1536]{1,0:T(8,128)(2,1)S(1)}, bf16[128,1536]{1,0:T(8,128)(2,1)S(1)}, u32[]{:S(2)}, u32[]{:S(2)}) collective-permute-start(bf16[128,1536]{1,0:T(8,128)(2,1)S(1)} %bitcast.112), channel_id=1, source_target_pairs={{0,128},{1,33},{2,130},{3,35},{4,132},{5,37},{6,134},{7,39},{8,136... | collective-permute-start | bytes 1179656 | tf_op jit(solution)/shard_map/ppermute | solution.py:101
  96.9 12.1 %collective-permute-start.10 = (bf16[128,1536]{1,0:T(8,128)(2,1)S(1)}, bf16[128,1536]{1,0:T(8,128)(2,1)S(1)}, u32[]{:S(2)}, u32[]{:S(2)}) collective-permute-start(bf16[128,1536]{1,0:T(8,128)(2,1)S(1)} %bitcast.106), channel_id=1, source_target_pairs={{0,64},{1,17},{2,66},{3,19},{4,68},{5,21},{6,70},{7,23},{8,72},{9,... | collective-permute-start | bytes 1179656 | tf_op jit(solution)/shard_map/ppermute | solution.py:101
  98.5 14.0 %collective-permute-start.11 = (bf16[128,1536]{1,0:T(8,128)(2,1)S(1)}, bf16[128,1536]{1,0:T(8,128)(2,1)S(1)}, u32[]{:S(2)}, u32[]{:S(2)}) collective-permute-start(bf16[128,1536]{1,0:T(8,128)(2,1)S(1)} %bitcast.107), channel_id=1, source_target_pairs={{0,192},{1,49},{2,194},{3,51},{4,196},{5,53},{6,198},{7,55},{8,200... | collective-permute-start | bytes 1179656 | tf_op jit(solution)/shard_map/ppermute | solution.py:101
  102.5 10.8 %collective-permute-start.12 = (bf16[128,1536]{1,0:T(8,128)(2,1)S(1)}, bf16[128,1536]{1,0:T(8,128)(2,1)S(1)}, u32[]{:S(2)}, u32[]{:S(2)}) collective-permute-start(bf16[128,1536]{1,0:T(8,128)(2,1)S(1)} %bitcast.109), channel_id=1, source_target_pairs={{0,128},{1,33},{2,130},{3,35},{4,132},{5,37},{6,134},{7,39},{8,136... | collective-permute-start | bytes 1179656 | tf_op jit(solution)/shard_map/ppermute | solution.py:101
  106.4 7.7 %collective-permute-start.27 = (bf16[256,768]{1,0:T(8,128)(2,1)S(1)}, bf16[256,768]{1,0:T(8,128)(2,1)S(1)}, u32[]{:S(2)}, u32[]{:S(2)}) collective-permute-start(bf16[256,768]{1,0:T(8,128)(2,1)S(1)} %slice.19), channel_id=1, source_target_pairs={{0,1},{1,0},{2,3},{3,2},{4,5},{5,4},{6,7},{7,6},{8,9},{9,8},{10,11... | collective-permute-start | bytes 1179656 | tf_op jit(solution)/shard_map/ppermute | solution.py:59
  114.9 17.5 %all-to-all-start.3 = ((bf16[8,32,768]{2,1,0:T(8,128)(2,1)}), bf16[8,32,768]{2,1,0:T(8,128)(2,1)S(1)}, u32[]{:S(2)}, u32[]{:S(2)}) async-start(bf16[8,32,768]{2,1,0:T(8,128)(2,1)} %bitcast.43), calls=%async_computation.3 | async-start | bytes 786432 | tf_op jit(solution)/shard_map/all_to_all | solution.py:63
  122.1 1.8 %collective-permute-start.13 = (bf16[256,768]{1,0:T(8,128)(2,1)S(1)}, bf16[256,768]{1,0:T(8,128)(2,1)S(1)}, u32[]{:S(2)}, u32[]{:S(2)}) collective-permute-start(bf16[256,768]{1,0:T(8,128)(2,1)S(1)} %slice.17), channel_id=1, source_target_pairs={{0,1},{1,0},{2,3},{3,2},{4,5},{5,4},{6,7},{7,6},{8,9},{9,8},{10,11... | collective-permute-start | bytes 1179656 | tf_op jit(solution)/shard_map/ppermute | solution.py:59
  132.4 17.8 %all-to-all-start.1 = ((bf16[8,32,768]{2,1,0:T(8,128)(2,1)}), bf16[8,32,768]{2,1,0:T(8,128)(2,1)S(1)}, u32[]{:S(2)}, u32[]{:S(2)}) async-start(bf16[8,32,768]{2,1,0:T(8,128)(2,1)} %bitcast.21), calls=%async_computation.1 | async-start | bytes 786432 | tf_op jit(solution)/shard_map/all_to_all | solution.py:63
  (5 other events, 19.4 us)

commit v2 on v0

v2 whole, which is shorter than its diff:
```python
import jax
import jax.numpy as jnp
from jax import lax
from jax.sharding import PartitionSpec as P

tanh_gain = 0.7978845608028654
cubic_term = 0.044715
side = 4
planes = 8
chunks = ((4, 3, -3, -2), (2, 1, -1, 0))
both = ("row", "col")


def gelu_parts(hidden):
    squared = hidden * hidden
    tangent = jnp.tanh(tanh_gain * (hidden + cubic_term * squared * hidden))
    value = 0.5 * hidden * (1.0 + tangent)
    slope = 0.5 * (1.0 + tangent) + 0.5 * hidden * (1.0 - tangent * tangent) * tanh_gain * (
        1.0 + 3.0 * cubic_term * squared
    )
    return value, slope


def contract_rows(left, right):
    return lax.dot_general(
        left, right, (((0,), (0,)), ((), ())), preferred_element_type=jnp.float32
    )


def contract_cols(left, right):
    return lax.dot_general(
        left, right, (((1,), (1,)), ((), ())), preferred_element_type=jnp.float32
    )


def device(x, y, z, core):
    return (x * side + y) * (planes * 2) + z * 2 + core


def ring_pairs(first, flip):
    pairs = []
    for x in range(side):
        for y in range(side):
            for z in range(planes):
                for core in range(2):
                    along_x = (core == 0) == first
                    to = device(x ^ flip, y, z, core) if along_x else device(x, y ^ flip, z, core)
                    pairs.append((device(x, y, z, core), to))
    return pairs


flips = (1, 3, 2)
ring = {(first, flip): ring_pairs(first, flip) for first in (True, False) for flip in flips}
core_pairs = [(i, i ^ 1) for i in range(planes * 2)]


def other_core(block):
    return lax.ppermute(block, "col", core_pairs)


def to_plane(block, ahead):
    if ahead == 0:
        return block
    pairs = [(i, (i + 2 * ahead) % (planes * 2)) for i in range(planes * 2)]
    return lax.ppermute(block, "col", pairs)


def after(value, *others):
    return lax.optimization_barrier((value, others))[0]


def ring_send(blocks, place, first):
    return [
        lax.ppermute(
            lax.dynamic_index_in_dim(blocks, place ^ flip, 1, keepdims=False), both, ring[first, flip]
        )
        for flip in flips
    ]


def ring_sum(blocks, place, came):
    total = lax.dynamic_index_in_dim(blocks, place, 1, keepdims=False).astype(jnp.float32)
    for block in came:
        total = total + block.astype(jnp.float32)
    return total


def ring_share(block, first):
    return [lax.ppermute(block, both, ring[first, flip]) for flip in flips]


def ring_join(block, place, came):
    count, rows, width = block.shape
    whole = jnp.zeros((count, side, rows, width), block.dtype)
    whole = lax.dynamic_update_index_in_dim(whole, block, place, 1)
    for flip, piece in zip(flips, came):
        whole = lax.dynamic_update_index_in_dim(whole, piece, place ^ flip, 1)
    return whole.reshape(count, side * rows, width)


def local(tokens, weight_in, weight_out, cotangent):
    chip, core = lax.axis_index("row"), lax.axis_index("col") % 2
    x, y = chip // side, chip % side
    place_one, place_two = jnp.where(core == 0, x, y), jnp.where(core == 0, y, x)
    rows, width = tokens.shape
    hidden_width = weight_in.shape[1]
    grad_scale = (rows * planes * 2) ** (-0.5)
    half = planes // 2 * rows

    pair = jnp.stack([tokens, cotangent])
    order = chunks[0] + chunks[1]
    mine = lax.optimization_barrier([to_plane(pair, -ahead) for ahead in order])
    mine = jnp.stack(mine, axis=1).reshape(2, 2, half, width)
    gathered = jnp.stack([mine, other_core(mine)], axis=2).reshape(2, 4 * half, width)

    def project(chunk):
        rows_here = slice(chunk * 2 * half, (chunk + 1) * 2 * half)
        value_part = jnp.dot(gathered[0, rows_here], weight_in, preferred_element_type=jnp.float32)
        grad_part = contract_cols(gathered[1, rows_here], weight_out)
        parts = jnp.stack([value_part.astype(jnp.bfloat16), grad_part.astype(jnp.bfloat16)])
        return parts.reshape(2, side, -1, hidden_width)

    def middle(parts, came):
        parts = ring_sum(parts, place_one, came).astype(jnp.bfloat16)
        return parts.reshape(2, side, -1, hidden_width)

    def activate(parts, came):
        hidden, grad_activation = ring_sum(parts, place_two, came)
        value, slope = gelu_parts(hidden)
        return jnp.stack([value.astype(jnp.bfloat16), (grad_activation * slope).astype(jnp.bfloat16)])

    def project_back(acts):
        output_part = jnp.dot(acts[0], weight_out, preferred_element_type=jnp.float32)
        input_part = contract_cols(acts[1], weight_in)
        return jnp.stack([output_part.astype(jnp.bfloat16), input_part.astype(jnp.bfloat16)])

    def fold(parts):
        parts = parts[:, :half].astype(jnp.float32) + other_core(parts[:, half:]).astype(jnp.float32)
        return parts.astype(jnp.bfloat16).reshape(2, planes // 2, rows, width)

    def send_back(parts, chunk):
        return [to_plane(parts[:, i], ahead) for i, ahead in enumerate(chunks[chunk])]

    a_part = project(0)
    a_came = ring_send(a_part, place_one, True)
    b_part = project(1)
    b_came = ring_send(b_part, place_one, True)
    a_mid = middle(a_part, a_came)
    a_came = ring_send(a_mid, place_two, False)
    b_mid = middle(b_part, after(b_came, a_came))
    b_came = ring_send(b_mid, place_two, False)
    a_act = activate(a_mid, a_came)
    a_came = ring_share(a_act, False)
    b_act = activate(b_mid, after(b_came, a_came))
    b_came = ring_share(b_act, False)
    a_act = ring_join(a_act, place_two, a_came)
    a_came = ring_share(a_act, True)
    b_act = ring_join(b_act, place_two, b_came)
    b_came = ring_share(b_act, True)
    a_act = ring_join(a_act, place_one, a_came)
    a_back = fold(project_back(a_act))
    b_act = ring_join(b_act, place_one, after(b_came, a_back))
    a_sent = send_back(a_back, 0)
    b_back = fold(project_back(b_act))
    b_sent = send_back(b_back, 1)

    total = a_sent[0].astype(jnp.float32)
    for block in a_sent[1:] + b_sent:
        total = total + block.astype(jnp.float32)
    total = total.astype(jnp.bfloat16)
    acts = jnp.concatenate([a_act, b_act], axis=1)
    grad_out = (contract_rows(acts[0], gathered[1]) * grad_scale).astype(jnp.bfloat16)
    grad_in = (contract_rows(gathered[0], acts[1]) * grad_scale).astype(jnp.bfloat16)
    return (total[0], total[1], grad_in, grad_out)


def solution(mesh):
    in_specs = (P("col", "row"), P("row", "col"), P("col", "row"), P("col", "row"))
    out_specs = (P("col", "row"), P("col", "row"), P("row", "col"), P("col", "row"))
    return jax.shard_map(local, mesh=mesh, in_specs=in_specs, out_specs=out_specs, check_vma=False)
```

time: 284 us -> 129 us (0.45)
  waiting for transfers between devices: 198 us -> 35.8 us
  starting transfers between devices: 0.12 us -> 70.5 us
  blocking collectives: 39.4 us -> 0 us
  between operations: 13.8 us -> 1.27 us
  matrix products: 22.6 us -> 12 us
    psum x1 -> x0, waiting for transfers between devices: 104 us -> none  [local(): lax.psum(partial_value.astype(jnp.bfloat16), 'row').astype(jnp.float32)]
    reduce_scatter x2 -> x0, waiting for transfers between devices: 94.7 us -> none  [the longest x1 58.6 us: local(): lax.psum_scatter(contract_cols(picked, weight_in).astype(jnp.bfloat16), '...]
    ppermute x0 -> x41, starting transfers between devices: none -> 70.5 us  [the longest x14 33.7 us: to_plane(): return lax.ppermute(block, 'col', pairs)]
    all_gather x2 -> x0, blocking collectives: 39.4 us -> none  [the longest x1 22.5 us: local(): lax.all_gather(tokens, 'col', axis=0, tiled=True)]
    ppermute x0 -> x41, waiting for transfers between devices: none -> 35.8 us  [the longest x12 14.5 us: ring_share(): return [lax.ppermute(block, both, ring[first, flip]) for flip in flips]]
    dot_general x2 -> x4, matrix products: 8.53 us -> 3.09 us  [the longest x2 1.55 us: project_back(): jnp.dot(acts[0], weight_out, preferred_element_type=jnp.float32)]
    unnamed x9 -> x11, local copies, waits for them, and re-layouts: 5.42 us -> 1.61 us
    another operation x0 -> x7, other arithmetic: none -> 3.59 us  [the longest x2 2.53 us: local(): jnp.stack([mine, other_core(mine)], axis=2).reshape(2, 4 * half, width)]
  transfers between devices with their start and end apart: 3 -> 41, of which waited for: 3 -> 18; matrix products, arithmetic and copies ran while one was open for 7% -> 9% of each run, Pallas kernels for 0% -> 0%
where the time goes in v2:
time: 129 us; the launch traced here: 128 us
  starting transfers between devices  70.5 us (55%)
  waiting for transfers between devices  35.8 us (28%)
  matrix products  12 us (9%)
  other arithmetic  4.81 us (4%)
  local copies, waits for them, and re-layouts  3.43 us (3%)
    ppermute x14, starting transfers between devices, to_plane(): return lax.ppermute(block, 'col', pairs)  33.7 us
    ppermute x12, starting transfers between devices, ring_send(): lax.ppermute(lax.dynamic_index_in_dim(blocks, place ^ flip, 1, keepdims=F...  19.2 us
    ppermute x12, starting transfers between devices, ring_share(): return [lax.ppermute(block, both, ring[first, flip]) for flip in flips]  17.4 us
    ppermute x12, waiting for transfers between devices, ring_share(): return [lax.ppermute(block, both, ring[first, flip]) for flip in flips]  14.5 us
    ppermute x12, waiting for transfers between devices, ring_send(): lax.ppermute(lax.dynamic_index_in_dim(blocks, place ^ flip, 1, keepdims=F...  9.81 us
    ppermute x14, waiting for transfers between devices, to_plane(): return lax.ppermute(block, 'col', pairs)  9.14 us
    dot_general x2, matrix products, contract_rows(): lax.dot_general(left, right, (((0,), (0,)), ((), ())), preferred_element_...  5.66 us
    dot_general x4, matrix products, contract_cols(): lax.dot_general(left, right, (((1,), (1,)), ((), ())), preferred_element_...  3.24 us
  transfers between devices with their start and end apart: 41, of which 18 were waited for; matrix products, arithmetic and copies ran while one was open for 9% of the time, Pallas kernels for 0%

profile of v2, /device:TPU:24, one launch (start us, length us, event | category | flops | bytes accessed | tf_op | source)
XLA Modules:
  0.0 127.8 jit_solution(13988609838298532916)
XLA Ops:
  1.6 7.3 %collective-permute-start = (bf16[2,32,768]{2,1,0:T(8,128)(2,1)S(1)}, bf16[2,32,768]{2,1,0:T(8,128)(2,1)S(1)}, u32[]{:S(2)}, u32[]{:S(2)}) collective-permute-start(bf16[2,32,768]{2,1,0:T(8,128)(2,1)S(1)} %pad_maximum_fusion.4), channel_id=1, source_target_pairs={{0,8},{1,9},{2,10},{3,11},{4,12},{5,13},{6,14},{7,15},{8,0},{9,1},... | collective-permute-start | bytes 294920 | tf_op jit(solution)/shard_map/ppermute | solution.py:65
  8.9 3.8 %collective-permute-start.2 = (bf16[2,32,768]{2,1,0:T(8,128)(2,1)S(1)}, bf16[2,32,768]{2,1,0:T(8,128)(2,1)S(1)}, u32[]{:S(2)}, u32[]{:S(2)}) collective-permute-start(bf16[2,32,768]{2,1,0:T(8,128)(2,1)S(1)} %pad_maximum_fusion.4), channel_id=1, source_target_pairs={{0,6},{1,7},{2,8},{3,9},{4,10},{5,11},{6,12},{7,13},{8,14},{9,15},... | collective-permute-start | bytes 294920 | tf_op jit(solution)/shard_map/ppermute | solution.py:65
  12.7 2.7 %collective-permute-start.3 = (bf16[2,32,768]{2,1,0:T(8,128)(2,1)S(1)}, bf16[2,32,768]{2,1,0:T(8,128)(2,1)S(1)}, u32[]{:S(2)}, u32[]{:S(2)}) collective-permute-start(bf16[2,32,768]{2,1,0:T(8,128)(2,1)S(1)} %pad_maximum_fusion.4), channel_id=1, source_target_pairs={{0,4},{1,5},{2,6},{3,7},{4,8},{5,9},{6,10},{7,11},{8,12},{9,13},{1... | collective-permute-start | bytes 294920 | tf_op jit(solution)/shard_map/ppermute | solution.py:65
  17.6 3.0 %collective-permute-done.1 = bf16[2,32,768]{2,1,0:T(8,128)(2,1)S(1)} collective-permute-done((bf16[2,32,768]{2,1,0:T(8,128)(2,1)S(1)}, bf16[2,32,768]{2,1,0:T(8,128)(2,1)S(1)}, u32[]{:S(2)}, u32[]{:S(2)}) %collective-permute-start.1) | collective-permute-done | bytes 98336 | tf_op jit(solution)/shard_map/ppermute | solution.py:65
  20.6 3.0 %collective-permute-start.6 = (bf16[2,32,768]{2,1,0:T(8,128)(2,1)S(1)}, bf16[2,32,768]{2,1,0:T(8,128)(2,1)S(1)}, u32[]{:S(2)}, u32[]{:S(2)}) collective-permute-start(bf16[2,32,768]{2,1,0:T(8,128)(2,1)S(1)} %pad_maximum_fusion.4), channel_id=1, source_target_pairs={{0,2},{1,3},{2,4},{3,5},{4,6},{5,7},{6,8},{7,9},{8,10},{9,11},{10,... | collective-permute-start | bytes 294920 | tf_op jit(solution)/shard_map/ppermute | solution.py:65
  24.9 2.3 %collective-permute-done.5 = bf16[2,32,768]{2,1,0:T(8,128)(2,1)S(1)} collective-permute-done((bf16[2,32,768]{2,1,0:T(8,128)(2,1)S(1)}, bf16[2,32,768]{2,1,0:T(8,128)(2,1)S(1)}, u32[]{:S(2)}, u32[]{:S(2)}) %collective-permute-start.5) | collective-permute-done | bytes 98336 | tf_op jit(solution)/shard_map/ppermute | solution.py:65
  27.5 2.3 %collective-permute-done.7 = bf16[2,2,128,768]{3,2,1,0:T(8,128)(2,1)} collective-permute-done((bf16[2,2,128,768]{3,2,1,0:T(8,128)(2,1)S(1)}, bf16[2,2,128,768]{3,2,1,0:T(8,128)(2,1)}, u32[]{:S(2)}, u32[]{:S(2)}) %collective-permute-start.7) | collective-permute-done | bytes 786464 | tf_op jit(solution)/shard_map/ppermute | solution.py:58
  31.3 1.5 %copy-done.1 = bf16[768,1536]{1,0:T(8,128)(2,1)S(1)} copy-done((bf16[768,1536]{1,0:T(8,128)(2,1)S(1)}, bf16[768,1536]{1,0:T(8,128)(2,1)}, u32[]{:S(2)}) %copy-start.1) | copy-done | bytes 2359320
  35.3 3.1 %collective-permute-start.10 = (bf16[2,64,1536]{2,1,0:T(8,128)(2,1)S(1)}, bf16[2,64,1536]{2,1,0:T(8,128)(2,1)S(1)}, u32[]{:S(2)}, u32[]{:S(2)}) collective-permute-start(bf16[2,64,1536]{2,1,0:T(8,128)(2,1)S(1)} %get-tuple-element.46), channel_id=1, source_target_pairs={{0,128},{1,33},{2,130},{3,35},{4,132},{5,37},{6,134},{7,39},{8,136... | collective-permute-start | bytes 1179656 | tf_op jit(solution)/shard_map/ppermute | solution.py:74
  42.0 2.1 %collective-permute-start.26 = (bf16[2,64,1536]{2,1,0:T(8,128)(2,1)S(1)}, bf16[2,64,1536]{2,1,0:T(8,128)(2,1)S(1)}, u32[]{:S(2)}, u32[]{:S(2)}) collective-permute-start(bf16[2,64,1536]{2,1,0:T(8,128)(2,1)S(1)} %get-tuple-element.49), channel_id=1, source_target_pairs={{0,192},{1,49},{2,194},{3,51},{4,196},{5,53},{6,198},{7,55},{8,200... | collective-permute-start | bytes 1179656 | tf_op jit(solution)/shard_map/ppermute | solution.py:74
  44.8 4.3 %collective-permute-done.8 = bf16[2,64,1536]{2,1,0:T(8,128)(2,1)S(1)} collective-permute-done((bf16[2,64,1536]{2,1,0:T(8,128)(2,1)S(1)}, bf16[2,64,1536]{2,1,0:T(8,128)(2,1)S(1)}, u32[]{:S(2)}, u32[]{:S(2)}) %collective-permute-start.8) | collective-permute-done | bytes 393248 | tf_op jit(solution)/shard_map/ppermute | solution.py:74
  51.2 2.3 %collective-permute-start.13 = (bf16[2,16,1536]{2,1,0:T(8,128)(2,1)S(1)}, bf16[2,16,1536]{2,1,0:T(8,128)(2,1)S(1)}, u32[]{:S(2)}, u32[]{:S(2)}) collective-permute-start(bf16[2,16,1536]{2,1,0:T(8,128)(2,1)S(1)} %get-tuple-element.60), channel_id=1, source_target_pairs={{0,32},{1,129},{2,34},{3,131},{4,36},{5,133},{6,38},{7,135},{8,40}... | collective-permute-start | bytes 294920 | tf_op jit(solution)/shard_map/ppermute | solution.py:74
  54.9 3.0 %collective-permute-start.27 = (bf16[2,64,1536]{2,1,0:T(8,128)(2,1)S(1)}, bf16[2,64,1536]{2,1,0:T(8,128)(2,1)S(1)}, u32[]{:S(2)}, u32[]{:S(2)}) collective-permute-start(bf16[2,64,1536]{2,1,0:T(8,128)(2,1)S(1)} %get-tuple-element.47), channel_id=1, source_target_pairs={{0,128},{1,33},{2,130},{3,35},{4,132},{5,37},{6,134},{7,39},{8,136... | collective-permute-start | bytes 1179656 | tf_op jit(solution)/shard_map/ppermute | solution.py:74
  58.8 2.1 %collective-permute-start.15 = (bf16[2,16,1536]{2,1,0:T(8,128)(2,1)S(1)}, bf16[2,16,1536]{2,1,0:T(8,128)(2,1)S(1)}, u32[]{:S(2)}, u32[]{:S(2)}) collective-permute-start(bf16[2,16,1536]{2,1,0:T(8,128)(2,1)S(1)} %pad_maximum_fusion.5), channel_id=1, source_target_pairs={{0,48},{1,193},{2,50},{3,195},{4,52},{5,197},{6,54},{7,199},{8,56}... | collective-permute-start | bytes 294920 | tf_op jit(solution)/shard_map/ppermute | solution.py:89
  62.2 4.2 %collective-permute-done.27 = bf16[2,64,1536]{2,1,0:T(8,128)(2,1)S(1)} collective-permute-done((bf16[2,64,1536]{2,1,0:T(8,128)(2,1)S(1)}, bf16[2,64,1536]{2,1,0:T(8,128)(2,1)S(1)}, u32[]{:S(2)}, u32[]{:S(2)}) %collective-permute-start.27) | collective-permute-done | bytes 393248 | tf_op jit(solution)/shard_map/ppermute | solution.py:74
  68.6 2.3 %collective-permute-start.30 = (bf16[2,16,1536]{2,1,0:T(8,128)(2,1)S(1)}, bf16[2,16,1536]{2,1,0:T(8,128)(2,1)S(1)}, u32[]{:S(2)}, u32[]{:S(2)}) collective-permute-start(bf16[2,16,1536]{2,1,0:T(8,128)(2,1)S(1)} %get-tuple-element.57), channel_id=1, source_target_pairs={{0,32},{1,129},{2,34},{3,131},{4,36},{5,133},{6,38},{7,135},{8,40}... | collective-permute-start | bytes 294920 | tf_op jit(solution)/shard_map/ppermute | solution.py:74
  71.9 2.4 %collective-permute-start.18 = (bf16[2,64,1536]{2,1,0:T(8,128)(2,1)S(1)}, bf16[2,64,1536]{2,1,0:T(8,128)(2,1)S(1)}, u32[]{:S(2)}, u32[]{:S(2)}) collective-permute-start(bf16[2,64,1536]{2,1,0:T(8,128)(2,1)S(1)} %bitcast.276), channel_id=1, source_target_pairs={{0,192},{1,49},{2,194},{3,51},{4,196},{5,53},{6,198},{7,55},{8,200... | collective-permute-start | bytes 1179656 | tf_op jit(solution)/shard_map/ppermute | solution.py:89
  76.3 2.6 %collective-permute-start.32 = (bf16[2,16,1536]{2,1,0:T(8,128)(2,1)S(1)}, bf16[2,16,1536]{2,1,0:T(8,128)(2,1)S(1)}, u32[]{:S(2)}, u32[]{:S(2)}) collective-permute-start(bf16[2,16,1536]{2,1,0:T(8,128)(2,1)S(1)} %pad_maximum_fusion.6), channel_id=1, source_target_pairs={{0,48},{1,193},{2,50},{3,195},{4,52},{5,197},{6,54},{7,199},{8,56}... | collective-permute-start | bytes 294920 | tf_op jit(solution)/shard_map/ppermute | solution.py:89
  79.2 2.1 %collective-permute-done.31 = bf16[2,16,1536]{2,1,0:T(8,128)(2,1)S(1)} collective-permute-done((bf16[2,16,1536]{2,1,0:T(8,128)(2,1)S(1)}, bf16[2,16,1536]{2,1,0:T(8,128)(2,1)S(1)}, u32[]{:S(2)}, u32[]{:S(2)}) %collective-permute-start.31) | collective-permute-done | bytes 98336 | tf_op jit(solution)/shard_map/ppermute | solution.py:89
  81.3 1.8 %collective-permute-start.33 = (bf16[2,16,1536]{2,1,0:T(8,128)(2,1)S(1)}, bf16[2,16,1536]{2,1,0:T(8,128)(2,1)S(1)}, u32[]{:S(2)}, u32[]{:S(2)}) collective-permute-start(bf16[2,16,1536]{2,1,0:T(8,128)(2,1)S(1)} %pad_maximum_fusion.6), channel_id=1, source_target_pairs={{0,32},{1,129},{2,34},{3,131},{4,36},{5,133},{6,38},{7,135},{8,40}... | collective-permute-start | bytes 294920 | tf_op jit(solution)/shard_map/ppermute | solution.py:89
  83.3 1.5 %collective-permute-done.18 = bf16[2,64,1536]{2,1,0:T(8,128)(2,1)S(1)} collective-permute-done((bf16[2,64,1536]{2,1,0:T(8,128)(2,1)S(1)}, bf16[2,64,1536]{2,1,0:T(8,128)(2,1)S(1)}, u32[]{:S(2)}, u32[]{:S(2)}) %collective-permute-start.18) | collective-permute-done | bytes 393248 | tf_op jit(solution)/shard_map/ppermute | solution.py:89
  88.2 2.6 %collective-permute-start.35 = (bf16[2,64,1536]{2,1,0:T(8,128)(2,1)S(1)}, bf16[2,64,1536]{2,1,0:T(8,128)(2,1)S(1)}, u32[]{:S(2)}, u32[]{:S(2)}) collective-permute-start(bf16[2,64,1536]{2,1,0:T(8,128)(2,1)S(1)} %bitcast.272), channel_id=1, source_target_pairs={{0,192},{1,49},{2,194},{3,51},{4,196},{5,53},{6,198},{7,55},{8,200... | collective-permute-start | bytes 1179656 | tf_op jit(solution)/shard_map/ppermute | solution.py:89
  92.5 3.4 %collective-permute-done.34 = bf16[2,64,1536]{2,1,0:T(8,128)(2,1)S(1)} collective-permute-done((bf16[2,64,1536]{2,1,0:T(8,128)(2,1)S(1)}, bf16[2,64,1536]{2,1,0:T(8,128)(2,1)S(1)}, u32[]{:S(2)}, u32[]{:S(2)}) %collective-permute-start.34) | collective-permute-done | bytes 393248 | tf_op jit(solution)/shard_map/ppermute | solution.py:89
  95.9 4.4 %collective-permute-done.35 = bf16[2,64,1536]{2,1,0:T(8,128)(2,1)S(1)} collective-permute-done((bf16[2,64,1536]{2,1,0:T(8,128)(2,1)S(1)}, bf16[2,64,1536]{2,1,0:T(8,128)(2,1)S(1)}, u32[]{:S(2)}, u32[]{:S(2)}) %collective-permute-start.35) | collective-permute-done | bytes 393248 | tf_op jit(solution)/shard_map/ppermute | solution.py:89
  100.3 1.6 %collective-permute-done.36 = bf16[2,64,1536]{2,1,0:T(8,128)(2,1)S(1)} collective-permute-done((bf16[2,64,1536]{2,1,0:T(8,128)(2,1)S(1)}, bf16[2,64,1536]{2,1,0:T(8,128)(2,1)S(1)}, u32[]{:S(2)}, u32[]{:S(2)}) %collective-permute-start.36) | collective-permute-done | bytes 393248 | tf_op jit(solution)/shard_map/ppermute | solution.py:89
  104.0 4.1 %collective-permute-start.21 = (bf16[2,32,768]{2,1,0:T(8,128)(2,1)S(1)}, bf16[2,32,768]{2,1,0:T(8,128)(2,1)S(1)}, u32[]{:S(2)}, u32[]{:S(2)}) collective-permute-start(bf16[2,32,768]{2,1,0:T(8,128)(2,1)S(1)} %get-tuple-element.50), channel_id=1, source_target_pairs={{0,8},{1,9},{2,10},{3,11},{4,12},{5,13},{6,14},{7,15},{8,0},{9,1},... | collective-permute-start | bytes 294920 | tf_op jit(solution)/shard_map/ppermute | solution.py:65
  109.5 3.6 %collective-permute-start.23 = (bf16[2,32,768]{2,1,0:T(8,128)(2,1)S(1)}, bf16[2,32,768]{2,1,0:T(8,128)(2,1)S(1)}, u32[]{:S(2)}, u32[]{:S(2)}) collective-permute-start(bf16[2,32,768]{2,1,0:T(8,128)(2,1)S(1)} %get-tuple-element.51), channel_id=1, source_target_pairs={{0,10},{1,11},{2,12},{3,13},{4,14},{5,15},{6,0},{7,1},{8,2},{9,3},... | collective-permute-start | bytes 294920 | tf_op jit(solution)/shard_map/ppermute | solution.py:65
  114.1 2.8 %multiply_convert_fusion.1 = bf16[768,1536]{1,0:T(8,128)(2,1)} fusion(bf16[512,768]{1,0:T(8,128)(2,1)S(1)} %bitcast.284, bf16[2,256,1536]{2,1,0:T(8,128)(2,1)S(1)} %bitcast.251, bf16[2,256,1536]{2,1,0:T(8,128)(2,1)S(1)} %bitcast.249), kind=kOutput, calls=%fused_computation.1 | convolution fusion | flops 1213464576 | bytes 6291456 | tf_op jit(solution)/shard_map/dot_general | solution.py:25
  117.1 1.9 %collective-permute-start.38 = (bf16[2,32,768]{2,1,0:T(8,128)(2,1)S(1)}, bf16[2,32,768]{2,1,0:T(8,128)(2,1)S(1)}, u32[]{:S(2)}, u32[]{:S(2)}) collective-permute-start(bf16[2,32,768]{2,1,0:T(8,128)(2,1)S(1)} %get-tuple-element.54), channel_id=1, source_target_pairs={{0,4},{1,5},{2,6},{3,7},{4,8},{5,9},{6,10},{7,11},{8,12},{9,13},{1... | collective-permute-start | bytes 294920 | tf_op jit(solution)/shard_map/ppermute | solution.py:65
  120.1 2.1 %collective-permute-start.40 = (bf16[2,32,768]{2,1,0:T(8,128)(2,1)S(1)}, bf16[2,32,768]{2,1,0:T(8,128)(2,1)S(1)}, u32[]{:S(2)}, u32[]{:S(2)}) collective-permute-start(bf16[2,32,768]{2,1,0:T(8,128)(2,1)S(1)} %get-tuple-element.55), channel_id=1, source_target_pairs={{0,14},{1,15},{2,0},{3,1},{4,2},{5,3},{6,4},{7,5},{8,6},{9,7},{10,... | collective-permute-start | bytes 294920 | tf_op jit(solution)/shard_map/ppermute | solution.py:65
  122.3 2.8 %multiply_convert_fusion = bf16[1536,768]{1,0:T(8,128)(2,1)} fusion(bf16[512,768]{1,0:T(8,128)(2,1)S(1)} %bitcast.283, bf16[2,256,1536]{2,1,0:T(8,128)(2,1)S(1)} %bitcast.250, bf16[2,256,1536]{2,1,0:T(8,128)(2,1)S(1)} %bitcast.252), kind=kOutput, calls=%fused_computation | convolution fusion | flops 1213464576 | bytes 6291456 | tf_op jit(solution)/shard_map/dot_general | solution.py:25
  125.5 1.6 %collective-permute-done.39 = bf16[2,32,768]{2,1,0:T(8,128)(2,1)S(1)} collective-permute-done((bf16[2,32,768]{2,1,0:T(8,128)(2,1)S(1)}, bf16[2,32,768]{2,1,0:T(8,128)(2,1)S(1)}, u32[]{:S(2)}, u32[]{:S(2)}) %collective-permute-start.39) | collective-permute-done | bytes 98336 | tf_op jit(solution)/shard_map/ppermute | solution.py:65
  (120 shorter events, 35.7 us)
Async XLA Ops:
  1.6 15.2 %collective-permute-start = (bf16[2,32,768]{2,1,0:T(8,128)(2,1)S(1)}, bf16[2,32,768]{2,1,0:T(8,128)(2,1)S(1)}, u32[]{:S(2)}, u32[]{:S(2)}) collective-permute-start(bf16[2,32,768]{2,1,0:T(8,128)(2,1)S(1)} %pad_maximum_fusion.4), channel_id=1, source_target_pairs={{0,8},{1,9},{2,10},{3,11},{4,12},{5,13},{6,14},{7,15},{8,0},{9,1},... | collective-permute-start | bytes 294920 | tf_op jit(solution)/shard_map/ppermute | solution.py:65
  8.9 11.7 %collective-permute-start.1 = (bf16[2,32,768]{2,1,0:T(8,128)(2,1)S(1)}, bf16[2,32,768]{2,1,0:T(8,128)(2,1)S(1)}, u32[]{:S(2)}, u32[]{:S(2)}) collective-permute-start(bf16[2,32,768]{2,1,0:T(8,128)(2,1)S(1)} %pad_maximum_fusion.4), channel_id=1, source_target_pairs={{0,10},{1,11},{2,12},{3,13},{4,14},{5,15},{6,0},{7,1},{8,2},{9,3},... | collective-permute-start | bytes 294920 | tf_op jit(solution)/shard_map/ppermute | solution.py:65
  8.9 15.1 %collective-permute-start.2 = (bf16[2,32,768]{2,1,0:T(8,128)(2,1)S(1)}, bf16[2,32,768]{2,1,0:T(8,128)(2,1)S(1)}, u32[]{:S(2)}, u32[]{:S(2)}) collective-permute-start(bf16[2,32,768]{2,1,0:T(8,128)(2,1)S(1)} %pad_maximum_fusion.4), channel_id=1, source_target_pairs={{0,6},{1,7},{2,8},{3,9},{4,10},{5,11},{6,12},{7,13},{8,14},{9,15},... | collective-permute-start | bytes 294920 | tf_op jit(solution)/shard_map/ppermute | solution.py:65
  12.7 11.3 %collective-permute-start.3 = (bf16[2,32,768]{2,1,0:T(8,128)(2,1)S(1)}, bf16[2,32,768]{2,1,0:T(8,128)(2,1)S(1)}, u32[]{:S(2)}, u32[]{:S(2)}) collective-permute-start(bf16[2,32,768]{2,1,0:T(8,128)(2,1)S(1)} %pad_maximum_fusion.4), channel_id=1, source_target_pairs={{0,4},{1,5},{2,6},{3,7},{4,8},{5,9},{6,10},{7,11},{8,12},{9,13},{1... | collective-permute-start | bytes 294920 | tf_op jit(solution)/shard_map/ppermute | solution.py:65
  15.4 9.5 %collective-permute-start.4 = (bf16[2,32,768]{2,1,0:T(8,128)(2,1)S(1)}, bf16[2,32,768]{2,1,0:T(8,128)(2,1)S(1)}, u32[]{:S(2)}, u32[]{:S(2)}) collective-permute-start(bf16[2,32,768]{2,1,0:T(8,128)(2,1)S(1)} %pad_maximum_fusion.4), channel_id=1, source_target_pairs={{0,12},{1,13},{2,14},{3,15},{4,0},{5,1},{6,2},{7,3},{8,4},{9,5},{1... | collective-permute-start | bytes 294920 | tf_op jit(solution)/shard_map/ppermute | solution.py:65
  16.9 10.4 %collective-permute-start.5 = (bf16[2,32,768]{2,1,0:T(8,128)(2,1)S(1)}, bf16[2,32,768]{2,1,0:T(8,128)(2,1)S(1)}, u32[]{:S(2)}, u32[]{:S(2)}) collective-permute-start(bf16[2,32,768]{2,1,0:T(8,128)(2,1)S(1)} %pad_maximum_fusion.4), channel_id=1, source_target_pairs={{0,14},{1,15},{2,0},{3,1},{4,2},{5,3},{6,4},{7,5},{8,6},{9,7},{10,... | collective-permute-start | bytes 294920 | tf_op jit(solution)/shard_map/ppermute | solution.py:65
  35.3 9.5 %collective-permute-start.10 = (bf16[2,64,1536]{2,1,0:T(8,128)(2,1)S(1)}, bf16[2,64,1536]{2,1,0:T(8,128)(2,1)S(1)}, u32[]{:S(2)}, u32[]{:S(2)}) collective-permute-start(bf16[2,64,1536]{2,1,0:T(8,128)(2,1)S(1)} %get-tuple-element.46), channel_id=1, source_target_pairs={{0,128},{1,33},{2,130},{3,35},{4,132},{5,37},{6,134},{7,39},{8,136... | collective-permute-start | bytes 1179656 | tf_op jit(solution)/shard_map/ppermute | solution.py:74
  38.4 10.6 %collective-permute-start.8 = (bf16[2,64,1536]{2,1,0:T(8,128)(2,1)S(1)}, bf16[2,64,1536]{2,1,0:T(8,128)(2,1)S(1)}, u32[]{:S(2)}, u32[]{:S(2)}) collective-permute-start(bf16[2,64,1536]{2,1,0:T(8,128)(2,1)S(1)} %get-tuple-element.44), channel_id=1, source_target_pairs={{0,64},{1,17},{2,66},{3,19},{4,68},{5,21},{6,70},{7,23},{8,72},{9,... | collective-permute-start | bytes 1179656 | tf_op jit(solution)/shard_map/ppermute | solution.py:74
  39.0 10.0 %collective-permute-start.9 = (bf16[2,64,1536]{2,1,0:T(8,128)(2,1)S(1)}, bf16[2,64,1536]{2,1,0:T(8,128)(2,1)S(1)}, u32[]{:S(2)}, u32[]{:S(2)}) collective-permute-start(bf16[2,64,1536]{2,1,0:T(8,128)(2,1)S(1)} %get-tuple-element.45), channel_id=1, source_target_pairs={{0,192},{1,49},{2,194},{3,51},{4,196},{5,53},{6,198},{7,55},{8,200... | collective-permute-start | bytes 1179656 | tf_op jit(solution)/shard_map/ppermute | solution.py:74
  40.5 20.4 %collective-permute-start.25 = (bf16[2,64,1536]{2,1,0:T(8,128)(2,1)S(1)}, bf16[2,64,1536]{2,1,0:T(8,128)(2,1)S(1)}, u32[]{:S(2)}, u32[]{:S(2)}) collective-permute-start(bf16[2,64,1536]{2,1,0:T(8,128)(2,1)S(1)} %get-tuple-element.48), channel_id=1, source_target_pairs={{0,64},{1,17},{2,66},{3,19},{4,68},{5,21},{6,70},{7,23},{8,72},{9,... | collective-permute-start | bytes 1179656 | tf_op jit(solution)/shard_map/ppermute | solution.py:74
  42.0 20.2 %collective-permute-start.26 = (bf16[2,64,1536]{2,1,0:T(8,128)(2,1)S(1)}, bf16[2,64,1536]{2,1,0:T(8,128)(2,1)S(1)}, u32[]{:S(2)}, u32[]{:S(2)}) collective-permute-start(bf16[2,64,1536]{2,1,0:T(8,128)(2,1)S(1)} %get-tuple-element.49), channel_id=1, source_target_pairs={{0,192},{1,49},{2,194},{3,51},{4,196},{5,53},{6,198},{7,55},{8,200... | collective-permute-start | bytes 1179656 | tf_op jit(solution)/shard_map/ppermute | solution.py:74
  50.1 7.7 %collective-permute-start.12 = (bf16[2,16,1536]{2,1,0:T(8,128)(2,1)S(1)}, bf16[2,16,1536]{2,1,0:T(8,128)(2,1)S(1)}, u32[]{:S(2)}, u32[]{:S(2)}) collective-permute-start(bf16[2,16,1536]{2,1,0:T(8,128)(2,1)S(1)} %get-tuple-element.61), channel_id=1, source_target_pairs={{0,48},{1,193},{2,50},{3,195},{4,52},{5,197},{6,54},{7,199},{8,56}... | collective-permute-start | bytes 294920 | tf_op jit(solution)/shard_map/ppermute | solution.py:74
  54.9 11.6 %collective-permute-start.27 = (bf16[2,64,1536]{2,1,0:T(8,128)(2,1)S(1)}, bf16[2,64,1536]{2,1,0:T(8,128)(2,1)S(1)}, u32[]{:S(2)}, u32[]{:S(2)}) collective-permute-start(bf16[2,64,1536]{2,1,0:T(8,128)(2,1)S(1)} %get-tuple-element.47), channel_id=1, source_target_pairs={{0,128},{1,33},{2,130},{3,35},{4,132},{5,37},{6,134},{7,39},{8,136... | collective-permute-start | bytes 1179656 | tf_op jit(solution)/shard_map/ppermute | solution.py:74
  58.0 10.6 %collective-permute-start.14 = (bf16[2,16,1536]{2,1,0:T(8,128)(2,1)S(1)}, bf16[2,16,1536]{2,1,0:T(8,128)(2,1)S(1)}, u32[]{:S(2)}, u32[]{:S(2)}) collective-permute-start(bf16[2,16,1536]{2,1,0:T(8,128)(2,1)S(1)} %pad_maximum_fusion.5), channel_id=1, source_target_pairs={{0,16},{1,65},{2,18},{3,67},{4,20},{5,69},{6,22},{7,71},{8,24},{9,... | collective-permute-start | bytes 294920 | tf_op jit(solution)/shard_map/ppermute | solution.py:89
  58.8 12.1 %collective-permute-start.15 = (bf16[2,16,1536]{2,1,0:T(8,128)(2,1)S(1)}, bf16[2,16,1536]{2,1,0:T(8,128)(2,1)S(1)}, u32[]{:S(2)}, u32[]{:S(2)}) collective-permute-start(bf16[2,16,1536]{2,1,0:T(8,128)(2,1)S(1)} %pad_maximum_fusion.5), channel_id=1, source_target_pairs={{0,48},{1,193},{2,50},{3,195},{4,52},{5,197},{6,54},{7,199},{8,56}... | collective-permute-start | bytes 294920 | tf_op jit(solution)/shard_map/ppermute | solution.py:89
  60.9 10.1 %collective-permute-start.16 = (bf16[2,16,1536]{2,1,0:T(8,128)(2,1)S(1)}, bf16[2,16,1536]{2,1,0:T(8,128)(2,1)S(1)}, u32[]{:S(2)}, u32[]{:S(2)}) collective-permute-start(bf16[2,16,1536]{2,1,0:T(8,128)(2,1)S(1)} %pad_maximum_fusion.5), channel_id=1, source_target_pairs={{0,32},{1,129},{2,34},{3,131},{4,36},{5,133},{6,38},{7,135},{8,40}... | collective-permute-start | bytes 294920 | tf_op jit(solution)/shard_map/ppermute | solution.py:89
  66.7 7.5 %collective-permute-start.28 = (bf16[2,16,1536]{2,1,0:T(8,128)(2,1)S(1)}, bf16[2,16,1536]{2,1,0:T(8,128)(2,1)S(1)}, u32[]{:S(2)}, u32[]{:S(2)}) collective-permute-start(bf16[2,16,1536]{2,1,0:T(8,128)(2,1)S(1)} %get-tuple-element.59), channel_id=1, source_target_pairs={{0,16},{1,65},{2,18},{3,67},{4,20},{5,69},{6,22},{7,71},{8,24},{9,... | collective-permute-start | bytes 294920 | tf_op jit(solution)/shard_map/ppermute | solution.py:74
  67.6 7.6 %collective-permute-start.29 = (bf16[2,16,1536]{2,1,0:T(8,128)(2,1)S(1)}, bf16[2,16,1536]{2,1,0:T(8,128)(2,1)S(1)}, u32[]{:S(2)}, u32[]{:S(2)}) collective-permute-start(bf16[2,16,1536]{2,1,0:T(8,128)(2,1)S(1)} %get-tuple-element.58), channel_id=1, source_target_pairs={{0,48},{1,193},{2,50},{3,195},{4,52},{5,197},{6,54},{7,199},{8,56}... | collective-permute-start | bytes 294920 | tf_op jit(solution)/shard_map/ppermute | solution.py:74
  68.6 7.2 %collective-permute-start.30 = (bf16[2,16,1536]{2,1,0:T(8,128)(2,1)S(1)}, bf16[2,16,1536]{2,1,0:T(8,128)(2,1)S(1)}, u32[]{:S(2)}, u32[]{:S(2)}) collective-permute-start(bf16[2,16,1536]{2,1,0:T(8,128)(2,1)S(1)} %get-tuple-element.57), channel_id=1, source_target_pairs={{0,32},{1,129},{2,34},{3,131},{4,36},{5,133},{6,38},{7,135},{8,40}... | collective-permute-start | bytes 294920 | tf_op jit(solution)/shard_map/ppermute | solution.py:74
  71.0 12.2 %collective-permute-start.17 = (bf16[2,64,1536]{2,1,0:T(8,128)(2,1)S(1)}, bf16[2,64,1536]{2,1,0:T(8,128)(2,1)S(1)}, u32[]{:S(2)}, u32[]{:S(2)}) collective-permute-start(bf16[2,64,1536]{2,1,0:T(8,128)(2,1)S(1)} %bitcast.275), channel_id=1, source_target_pairs={{0,64},{1,17},{2,66},{3,19},{4,68},{5,21},{6,70},{7,23},{8,72},{9,... | collective-permute-start | bytes 1179656 | tf_op jit(solution)/shard_map/ppermute | solution.py:89
  71.9 12.9 %collective-permute-start.18 = (bf16[2,64,1536]{2,1,0:T(8,128)(2,1)S(1)}, bf16[2,64,1536]{2,1,0:T(8,128)(2,1)S(1)}, u32[]{:S(2)}, u32[]{:S(2)}) collective-permute-start(bf16[2,64,1536]{2,1,0:T(8,128)(2,1)S(1)} %bitcast.276), channel_id=1, source_target_pairs={{0,192},{1,49},{2,194},{3,51},{4,196},{5,53},{6,198},{7,55},{8,200... | collective-permute-start | bytes 1179656 | tf_op jit(solution)/shard_map/ppermute | solution.py:89
  74.2 11.9 %collective-permute-start.19 = (bf16[2,64,1536]{2,1,0:T(8,128)(2,1)S(1)}, bf16[2,64,1536]{2,1,0:T(8,128)(2,1)S(1)}, u32[]{:S(2)}, u32[]{:S(2)}) collective-permute-start(bf16[2,64,1536]{2,1,0:T(8,128)(2,1)S(1)} %bitcast.277), channel_id=1, source_target_pairs={{0,128},{1,33},{2,130},{3,35},{4,132},{5,37},{6,134},{7,39},{8,136... | collective-permute-start | bytes 1179656 | tf_op jit(solution)/shard_map/ppermute | solution.py:89
  88.1 7.9 %collective-permute-start.34 = (bf16[2,64,1536]{2,1,0:T(8,128)(2,1)S(1)}, bf16[2,64,1536]{2,1,0:T(8,128)(2,1)S(1)}, u32[]{:S(2)}, u32[]{:S(2)}) collective-permute-start(bf16[2,64,1536]{2,1,0:T(8,128)(2,1)S(1)} %bitcast.271), channel_id=1, source_target_pairs={{0,64},{1,17},{2,66},{3,19},{4,68},{5,21},{6,70},{7,23},{8,72},{9,... | collective-permute-start | bytes 1179656 | tf_op jit(solution)/shard_map/ppermute | solution.py:89
  88.2 12.2 %collective-permute-start.35 = (bf16[2,64,1536]{2,1,0:T(8,128)(2,1)S(1)}, bf16[2,64,1536]{2,1,0:T(8,128)(2,1)S(1)}, u32[]{:S(2)}, u32[]{:S(2)}) collective-permute-start(bf16[2,64,1536]{2,1,0:T(8,128)(2,1)S(1)} %bitcast.272), channel_id=1, source_target_pairs={{0,192},{1,49},{2,194},{3,51},{4,196},{5,53},{6,198},{7,55},{8,200... | collective-permute-start | bytes 1179656 | tf_op jit(solution)/shard_map/ppermute | solution.py:89
  90.8 11.2 %collective-permute-start.36 = (bf16[2,64,1536]{2,1,0:T(8,128)(2,1)S(1)}, bf16[2,64,1536]{2,1,0:T(8,128)(2,1)S(1)}, u32[]{:S(2)}, u32[]{:S(2)}) collective-permute-start(bf16[2,64,1536]{2,1,0:T(8,128)(2,1)S(1)} %bitcast.273), channel_id=1, source_target_pairs={{0,128},{1,33},{2,130},{3,35},{4,132},{5,37},{6,134},{7,39},{8,136... | collective-permute-start | bytes 1179656 | tf_op jit(solution)/shard_map/ppermute | solution.py:89
  103.8 13.1 %collective-permute-start.37 = (bf16[2,128,768]{2,1,0:T(8,128)(2,1)S(1)}, bf16[2,128,768]{2,1,0:T(8,128)(2,1)S(1)}, u32[]{:S(2)}, u32[]{:S(2)}) collective-permute-start(bf16[2,128,768]{2,1,0:T(8,128)(2,1)S(1)} %pad_maximum_fusion.2), channel_id=1, source_target_pairs={{0,1},{1,0},{2,3},{3,2},{4,5},{5,4},{6,7},{7,6},{8,9},{9,8},{10,11... | collective-permute-start | bytes 1179656 | tf_op jit(solution)/shard_map/ppermute | solution.py:58
  104.0 15.1 %collective-permute-start.21 = (bf16[2,32,768]{2,1,0:T(8,128)(2,1)S(1)}, bf16[2,32,768]{2,1,0:T(8,128)(2,1)S(1)}, u32[]{:S(2)}, u32[]{:S(2)}) collective-permute-start(bf16[2,32,768]{2,1,0:T(8,128)(2,1)S(1)} %get-tuple-element.50), channel_id=1, source_target_pairs={{0,8},{1,9},{2,10},{3,11},{4,12},{5,13},{6,14},{7,15},{8,0},{9,1},... | collective-permute-start | bytes 294920 | tf_op jit(solution)/shard_map/ppermute | solution.py:65
  108.0 12.1 %collective-permute-start.22 = (bf16[2,32,768]{2,1,0:T(8,128)(2,1)S(1)}, bf16[2,32,768]{2,1,0:T(8,128)(2,1)S(1)}, u32[]{:S(2)}, u32[]{:S(2)}) collective-permute-start(bf16[2,32,768]{2,1,0:T(8,128)(2,1)S(1)} %get-tuple-element.52), channel_id=1, source_target_pairs={{0,6},{1,7},{2,8},{3,9},{4,10},{5,11},{6,12},{7,13},{8,14},{9,15},... | collective-permute-start | bytes 294920 | tf_op jit(solution)/shard_map/ppermute | solution.py:65
  109.5 15.6 %collective-permute-start.23 = (bf16[2,32,768]{2,1,0:T(8,128)(2,1)S(1)}, bf16[2,32,768]{2,1,0:T(8,128)(2,1)S(1)}, u32[]{:S(2)}, u32[]{:S(2)}) collective-permute-start(bf16[2,32,768]{2,1,0:T(8,128)(2,1)S(1)} %get-tuple-element.51), channel_id=1, source_target_pairs={{0,10},{1,11},{2,12},{3,13},{4,14},{5,15},{6,0},{7,1},{8,2},{9,3},... | collective-permute-start | bytes 294920 | tf_op jit(solution)/shard_map/ppermute | solution.py:65
  113.1 12.4 %collective-permute-start.24 = (bf16[2,32,768]{2,1,0:T(8,128)(2,1)S(1)}, bf16[2,32,768]{2,1,0:T(8,128)(2,1)S(1)}, u32[]{:S(2)}, u32[]{:S(2)}) collective-permute-start(bf16[2,32,768]{2,1,0:T(8,128)(2,1)S(1)} %get-tuple-element.53), channel_id=1, source_target_pairs={{0,12},{1,13},{2,14},{3,15},{4,0},{5,1},{6,2},{7,3},{8,4},{9,5},{1... | collective-permute-start | bytes 294920 | tf_op jit(solution)/shard_map/ppermute | solution.py:65
  117.1 8.4 %collective-permute-start.38 = (bf16[2,32,768]{2,1,0:T(8,128)(2,1)S(1)}, bf16[2,32,768]{2,1,0:T(8,128)(2,1)S(1)}, u32[]{:S(2)}, u32[]{:S(2)}) collective-permute-start(bf16[2,32,768]{2,1,0:T(8,128)(2,1)S(1)} %get-tuple-element.54), channel_id=1, source_target_pairs={{0,4},{1,5},{2,6},{3,7},{4,8},{5,9},{6,10},{7,11},{8,12},{9,13},{1... | collective-permute-start | bytes 294920 | tf_op jit(solution)/shard_map/ppermute | solution.py:65
  119.0 8.0 %collective-permute-start.39 = (bf16[2,32,768]{2,1,0:T(8,128)(2,1)S(1)}, bf16[2,32,768]{2,1,0:T(8,128)(2,1)S(1)}, u32[]{:S(2)}, u32[]{:S(2)}) collective-permute-start(bf16[2,32,768]{2,1,0:T(8,128)(2,1)S(1)} %get-tuple-element.56), channel_id=1, source_target_pairs={{0,2},{1,3},{2,4},{3,5},{4,6},{5,7},{6,8},{7,9},{8,10},{9,11},{10,... | collective-permute-start | bytes 294920 | tf_op jit(solution)/shard_map/ppermute | solution.py:65
  (11 other events, 86.9 us)

commit v3 on v2

v3 whole, which is shorter than its diff:
```python
import jax
import jax.numpy as jnp
from jax import lax
from jax.sharding import PartitionSpec as P

tanh_gain = 0.7978845608028654
cubic_term = 0.044715
side = 4
planes = 8
order = (0, 1, 2, 6, 7, 3, 5, 4)
sent_order = (1, 2, 4, 5, 3, 7, 6)
both = ("row", "col")


def gelu_parts(hidden):
    squared = hidden * hidden
    tangent = jnp.tanh(tanh_gain * (hidden + cubic_term * squared * hidden))
    value = 0.5 * hidden * (1.0 + tangent)
    slope = 0.5 * (1.0 + tangent) + 0.5 * hidden * (1.0 - tangent * tangent) * tanh_gain * (
        1.0 + 3.0 * cubic_term * squared
    )
    return value, slope


def contract_rows(left, right):
    return lax.dot_general(
        left, right, (((0,), (0,)), ((), ())), preferred_element_type=jnp.float32
    )


def contract_cols(left, right):
    return lax.dot_general(
        left, right, (((1,), (1,)), ((), ())), preferred_element_type=jnp.float32
    )


def device(x, y, z, core):
    return (x * side + y) * (planes * 2) + z * 2 + core


def ring_pairs(first, flip):
    pairs = []
    for x in range(side):
        for y in range(side):
            for z in range(planes):
                for core in range(2):
                    along_x = (core == 0) == first
                    to = device(x ^ flip, y, z, core) if along_x else device(x, y ^ flip, z, core)
                    pairs.append((device(x, y, z, core), to))
    return pairs


flips = (1, 3, 2)
ring = {(first, flip): ring_pairs(first, flip) for first in (True, False) for flip in flips}
core_pairs = [(i, i ^ 1) for i in range(planes * 2)]


def other_core(block):
    return lax.ppermute(block, "col", core_pairs)


def to_plane(block, flip):
    if flip == 0:
        return block
    return lax.ppermute(block, "col", [(i, i ^ (2 * flip)) for i in range(planes * 2)])


def after(value, *others):
    return lax.optimization_barrier((value, others))[0]


def ring_send(blocks, place, first):
    pieces = [
        lax.dynamic_index_in_dim(blocks, place ^ flip, 1, keepdims=False) for flip in flips + (0,)
    ]
    pieces = lax.optimization_barrier(pieces)
    came = [lax.ppermute(piece, both, ring[first, flip]) for flip, piece in zip(flips, pieces)]
    return came + pieces[3:]


def ring_sum(came):
    total = came[-1].astype(jnp.float32)
    for block in came[:-1]:
        total = total + block.astype(jnp.float32)
    return total


def ring_share(block, first):
    return [lax.ppermute(block, both, ring[first, flip]) for flip in flips]


def ring_join(block, place, came):
    axis = block.ndim - 2
    whole = jnp.zeros(block.shape[:axis] + (side,) + block.shape[axis:], block.dtype)
    whole = lax.dynamic_update_index_in_dim(whole, block, place, axis)
    for flip, piece in zip(flips, came):
        whole = lax.dynamic_update_index_in_dim(whole, piece, place ^ flip, axis)
    return whole.reshape(block.shape[:axis] + (-1, block.shape[-1]))


def local(tokens, weight_in, weight_out, cotangent):
    chip, core = lax.axis_index("row"), lax.axis_index("col") % 2
    x, y = chip // side, chip % side
    place_one, place_two = jnp.where(core == 0, x, y), jnp.where(core == 0, y, x)
    rows, width = tokens.shape
    hidden_width = weight_in.shape[1]
    grad_scale = (rows * planes * 2) ** (-0.5)

    def project(block):
        value_part = jnp.dot(block[0], weight_in, preferred_element_type=jnp.float32)
        grad_part = contract_cols(block[1], weight_out)
        parts = jnp.stack([value_part.astype(jnp.bfloat16), grad_part.astype(jnp.bfloat16)])
        return parts.reshape(2, side, -1, hidden_width)

    def project_back(acts):
        output_part = jnp.dot(acts[0], weight_out, preferred_element_type=jnp.float32)
        return output_part, contract_cols(acts[1], weight_in)

    pair = jnp.stack([tokens, cotangent])
    mine = lax.optimization_barrier([to_plane(pair, flip) for flip in order])
    own = jnp.stack(mine, axis=1).reshape(2, planes * rows, width)
    other = other_core(own)

    own_part = project(own)
    own_came = ring_send(own_part, place_one, True)
    other_part = project(after(other, own_part))
    other_came = ring_send(other_part, place_one, True)
    own_sum = ring_sum(own_came).astype(jnp.bfloat16)
    other_sum = ring_sum(other_came).astype(jnp.bfloat16)
    sums = [part.reshape(2, side, -1, hidden_width) for part in (own_sum, other_sum)]

    def pick(place):
        return jnp.stack(
            [lax.dynamic_index_in_dim(part, place, 1, keepdims=False) for part in sums]
        )

    came = [lax.ppermute(pick(place_two ^ flip), both, ring[False, flip]) for flip in flips]
    sums = pick(place_two).astype(jnp.float32)
    for block in came:
        sums = sums + block.astype(jnp.float32)
    value, slope = gelu_parts(sums[:, 0])
    acts = jnp.stack([value, sums[:, 1] * slope], axis=1).astype(jnp.bfloat16)
    acts = ring_join(acts, place_two, ring_share(acts, False))
    acts = ring_join(acts, place_one, ring_share(acts, True))
    other_back = jnp.stack(project_back(acts[1])).astype(jnp.bfloat16)
    own_act = after(acts[0], other_back)
    back = jnp.stack(project_back(own_act)) + other_core(other_back).astype(jnp.float32)
    back = back.astype(jnp.bfloat16).reshape(2, planes, rows, width)
    came = {flip: to_plane(back[:, order.index(flip)], flip) for flip in sent_order}

    acts = after(jnp.concatenate([acts[0], acts[1]], axis=1), came[1], came[2])
    gathered = jnp.concatenate([own, other], axis=1)
    grad_out = (contract_rows(acts[0], gathered[1]) * grad_scale).astype(jnp.bfloat16)
    grad_in = (contract_rows(gathered[0], acts[1]) * grad_scale).astype(jnp.bfloat16)
    total = after(back[:, order.index(0)], grad_in, grad_out).astype(jnp.float32)
    for flip in sent_order:
        total = total + came[flip].astype(jnp.float32)
    total = total.astype(jnp.bfloat16)
    return (total[0], total[1], grad_in, grad_out)


def solution(mesh):
    in_specs = (P("col", "row"), P("row", "col"), P("col", "row"), P("col", "row"))
    out_specs = (P("col", "row"), P("col", "row"), P("row", "col"), P("col", "row"))
    return jax.shard_map(local, mesh=mesh, in_specs=in_specs, out_specs=out_specs, check_vma=False)
```

time: 129 us -> 127 us (0.984); the launches traced: 128 us -> 124 us
  starting transfers between devices: 70.5 us -> 52.6 us
  waiting for transfers between devices: 35.8 us -> 53.3 us
  other arithmetic: 4.81 us -> 2.59 us
    ppermute x26 -> x23, waiting for transfers between devices: 19 us -> 29.6 us  [the longest x14 13 us: to_plane(): lax.ppermute(block, 'col', [(i, i ^ 2 * flip) for i in range(planes * 2)])]
    ppermute x26 -> x23, starting transfers between devices: 52.9 us -> 43.7 us  [the longest x14 30.6 us: to_plane(): lax.ppermute(block, 'col', [(i, i ^ 2 * flip) for i in range(planes * 2)])]
    ppermute x12 -> x6, waiting for transfers between devices: 14.5 us -> 23.4 us  [ring_share(): return [lax.ppermute(block, both, ring[first, flip]) for flip in flips]]
    ppermute x12 -> x6, starting transfers between devices: 17.4 us -> 8.72 us  [ring_share(): return [lax.ppermute(block, both, ring[first, flip]) for flip in flips]]
    another operation x6, other arithmetic: 2.61 us -> 0.3 us  [the longest x2 2.53 us: local(): jnp.stack([mine, other_core(mine)], axis=2).reshape(2, 4 * half, width)]
    ppermute x3 -> x2, waiting for transfers between devices: 2.33 us -> 0.37 us  [other_core(): return lax.ppermute(block, 'col', core_pairs)]
  transfers between devices with their start and end apart: 41 -> 31, of which waited for: 18 -> 17; matrix products, arithmetic and copies ran while one was open for 9% -> 10% of each run, Pallas kernels for 0% -> 0%
where the time goes in v3:
time: 127 us; the launch traced here: 124 us
  waiting for transfers between devices  53.3 us (42%)
  starting transfers between devices  52.6 us (41%)
  matrix products  12 us (9%)
  local copies, waits for them, and re-layouts  2.73 us (2%)
  other arithmetic  2.59 us (2%)
    ppermute x14, starting transfers between devices, to_plane(): lax.ppermute(block, 'col', [(i, i ^ 2 * flip) for i in range(planes * 2)])  30.6 us
    ppermute x6, waiting for transfers between devices, ring_share(): return [lax.ppermute(block, both, ring[first, flip]) for flip in flips]  23.4 us
    ppermute x14, waiting for transfers between devices, to_plane(): lax.ppermute(block, 'col', [(i, i ^ 2 * flip) for i in range(planes * 2)])  13 us
    ppermute x6, waiting for transfers between devices, ring_send(): lax.ppermute(piece, both, ring[first, flip])  11 us
    ppermute x6, starting transfers between devices, ring_send(): lax.ppermute(piece, both, ring[first, flip])  9.2 us
    ppermute x6, starting transfers between devices, ring_share(): return [lax.ppermute(block, both, ring[first, flip]) for flip in flips]  8.72 us
    dot_general x2, matrix products, contract_rows(): lax.dot_general(left, right, (((0,), (0,)), ((), ())), preferred_element_...  5.67 us
    ppermute x3, waiting for transfers between devices, local(): lax.ppermute(pick(place_two ^ flip), both, ring[False, flip])  5.6 us
  transfers between devices with their start and end apart: 31, of which 17 were waited for; matrix products, arithmetic and copies ran while one was open for 10% of the time, Pallas kernels for 0%

profile of v3, /device:TPU:24, one launch (start us, length us, event | category | flops | bytes accessed | tf_op | source)
XLA Modules:
  0.0 124.3 jit_solution(2934138006933466359)
XLA Ops:
  1.6 2.0 %collective-permute-start = (bf16[2,32,768]{2,1,0:T(8,128)(2,1)S(1)}, bf16[2,32,768]{2,1,0:T(8,128)(2,1)S(1)}, u32[]{:S(2)}, u32[]{:S(2)}) collective-permute-start(bf16[2,32,768]{2,1,0:T(8,128)(2,1)S(1)} %pad_maximum_fusion.9), channel_id=1, source_target_pairs={{0,2},{1,3},{2,0},{3,1},{4,6},{5,7},{6,4},{7,5},{8,10},{9,11},{10,... | collective-permute-start | bytes 294920 | tf_op jit(solution)/shard_map/ppermute | solution.py:65
  3.6 3.3 %collective-permute-start.1 = (bf16[2,32,768]{2,1,0:T(8,128)(2,1)S(1)}, bf16[2,32,768]{2,1,0:T(8,128)(2,1)S(1)}, u32[]{:S(2)}, u32[]{:S(2)}) collective-permute-start(bf16[2,32,768]{2,1,0:T(8,128)(2,1)S(1)} %pad_maximum_fusion.9), channel_id=1, source_target_pairs={{0,4},{1,5},{2,6},{3,7},{4,0},{5,1},{6,2},{7,3},{8,12},{9,13},{10,... | collective-permute-start | bytes 294920 | tf_op jit(solution)/shard_map/ppermute | solution.py:65
  6.9 3.6 %collective-permute-start.2 = (bf16[2,32,768]{2,1,0:T(8,128)(2,1)S(1)}, bf16[2,32,768]{2,1,0:T(8,128)(2,1)S(1)}, u32[]{:S(2)}, u32[]{:S(2)}) collective-permute-start(bf16[2,32,768]{2,1,0:T(8,128)(2,1)S(1)} %pad_maximum_fusion.9), channel_id=1, source_target_pairs={{0,12},{1,13},{2,14},{3,15},{4,8},{5,9},{6,10},{7,11},{8,4},{9,5},... | collective-permute-start | bytes 294920 | tf_op jit(solution)/shard_map/ppermute | solution.py:65
  10.5 1.9 %collective-permute-start.4 = (bf16[2,32,768]{2,1,0:T(8,128)(2,1)S(1)}, bf16[2,32,768]{2,1,0:T(8,128)(2,1)S(1)}, u32[]{:S(2)}, u32[]{:S(2)}) collective-permute-start(bf16[2,32,768]{2,1,0:T(8,128)(2,1)S(1)} %pad_maximum_fusion.9), channel_id=1, source_target_pairs={{0,6},{1,7},{2,4},{3,5},{4,2},{5,3},{6,0},{7,1},{8,14},{9,15},{10,... | collective-permute-start | bytes 294920 | tf_op jit(solution)/shard_map/ppermute | solution.py:65
  12.4 4.1 %collective-permute-start.5 = (bf16[2,32,768]{2,1,0:T(8,128)(2,1)S(1)}, bf16[2,32,768]{2,1,0:T(8,128)(2,1)S(1)}, u32[]{:S(2)}, u32[]{:S(2)}) collective-permute-start(bf16[2,32,768]{2,1,0:T(8,128)(2,1)S(1)} %pad_maximum_fusion.9), channel_id=1, source_target_pairs={{0,10},{1,11},{2,8},{3,9},{4,14},{5,15},{6,12},{7,13},{8,2},{9,3},... | collective-permute-start | bytes 294920 | tf_op jit(solution)/shard_map/ppermute | solution.py:65
  17.5 9.0 %collective-permute-done.3 = bf16[2,32,768]{2,1,0:T(8,128)(2,1)S(1)} collective-permute-done((bf16[2,32,768]{2,1,0:T(8,128)(2,1)S(1)}, bf16[2,32,768]{2,1,0:T(8,128)(2,1)S(1)}, u32[]{:S(2)}, u32[]{:S(2)}) %collective-permute-start.3) | collective-permute-done | bytes 98336 | tf_op jit(solution)/shard_map/ppermute | solution.py:65
  29.5 3.1 %collective-permute-start.9 = (bf16[2,64,1536]{2,1,0:T(8,128)(2,1)S(1)}, bf16[2,64,1536]{2,1,0:T(8,128)(2,1)S(1)}, u32[]{:S(2)}, u32[]{:S(2)}) collective-permute-start(bf16[2,64,1536]{2,1,0:T(8,128)(2,1)S(1)} %get-tuple-element.35), channel_id=1, source_target_pairs={{0,128},{1,33},{2,130},{3,35},{4,132},{5,37},{6,134},{7,39},{8,136... | collective-permute-start | bytes 1179656 | tf_op jit(solution)/shard_map/ppermute | solution.py:77
  35.5 3.6 %collective-permute-start.13 = (bf16[2,64,1536]{2,1,0:T(8,128)(2,1)S(1)}, bf16[2,64,1536]{2,1,0:T(8,128)(2,1)S(1)}, u32[]{:S(2)}, u32[]{:S(2)}) collective-permute-start(bf16[2,64,1536]{2,1,0:T(8,128)(2,1)S(1)} %get-tuple-element.40), channel_id=1, source_target_pairs={{0,128},{1,33},{2,130},{3,35},{4,132},{5,37},{6,134},{7,39},{8,136... | collective-permute-start | bytes 1179656 | tf_op jit(solution)/shard_map/ppermute | solution.py:77
  40.5 2.6 %collective-permute-done.8 = bf16[2,64,1536]{2,1,0:T(8,128)(2,1)S(1)} collective-permute-done((bf16[2,64,1536]{2,1,0:T(8,128)(2,1)S(1)}, bf16[2,64,1536]{2,1,0:T(8,128)(2,1)S(1)}, u32[]{:S(2)}, u32[]{:S(2)}) %collective-permute-start.8) | collective-permute-done | bytes 393248 | tf_op jit(solution)/shard_map/ppermute | solution.py:77
  43.4 4.0 %collective-permute-done.13 = bf16[2,64,1536]{2,1,0:T(8,128)(2,1)S(1)} collective-permute-done((bf16[2,64,1536]{2,1,0:T(8,128)(2,1)S(1)}, bf16[2,64,1536]{2,1,0:T(8,128)(2,1)S(1)}, u32[]{:S(2)}, u32[]{:S(2)}) %collective-permute-start.13) | collective-permute-done | bytes 393248 | tf_op jit(solution)/shard_map/ppermute | solution.py:77
  47.4 4.1 %collective-permute-done.12 = bf16[2,64,1536]{2,1,0:T(8,128)(2,1)S(1)} collective-permute-done((bf16[2,64,1536]{2,1,0:T(8,128)(2,1)S(1)}, bf16[2,64,1536]{2,1,0:T(8,128)(2,1)S(1)}, u32[]{:S(2)}, u32[]{:S(2)}) %collective-permute-start.12) | collective-permute-done | bytes 393248 | tf_op jit(solution)/shard_map/ppermute | solution.py:77
  52.0 1.3 %collective-permute-start.16 = (bf16[2,2,16,1536]{3,2,0,1:T(8,128)(2,1)S(1)}, bf16[2,2,16,1536]{3,2,0,1:T(8,128)(2,1)S(1)}, u32[]{:S(2)}, u32[]{:S(2)}) collective-permute-start(bf16[2,2,16,1536]{3,2,0,1:T(8,128)(2,1)S(1)} %pad_maximum_fusion.6), channel_id=1, source_target_pairs={{0,32},{1,129},{2,34},{3,131},{4,36},{5,133},{6,38},{7,135},{8,40}... | collective-permute-start | bytes 589832 | tf_op jit(solution)/shard_map/ppermute | solution.py:137
  53.3 2.3 %collective-permute-start.15 = (bf16[2,2,16,1536]{3,2,0,1:T(8,128)(2,1)S(1)}, bf16[2,2,16,1536]{3,2,0,1:T(8,128)(2,1)S(1)}, u32[]{:S(2)}, u32[]{:S(2)}) collective-permute-start(bf16[2,2,16,1536]{3,2,0,1:T(8,128)(2,1)S(1)} %pad_maximum_fusion.5), channel_id=1, source_target_pairs={{0,48},{1,193},{2,50},{3,195},{4,52},{5,197},{6,54},{7,199},{8,56}... | collective-permute-start | bytes 589832 | tf_op jit(solution)/shard_map/ppermute | solution.py:137
  56.0 3.4 %collective-permute-done.16 = bf16[2,2,16,1536]{3,2,0,1:T(8,128)(2,1)S(1)} collective-permute-done((bf16[2,2,16,1536]{3,2,0,1:T(8,128)(2,1)S(1)}, bf16[2,2,16,1536]{3,2,0,1:T(8,128)(2,1)S(1)}, u32[]{:S(2)}, u32[]{:S(2)}) %collective-permute-start.16) | collective-permute-done | bytes 196640 | tf_op jit(solution)/shard_map/ppermute | solution.py:137
  59.4 2.0 %collective-permute-done.15 = bf16[2,2,16,1536]{3,2,0,1:T(8,128)(2,1)S(1)} collective-permute-done((bf16[2,2,16,1536]{3,2,0,1:T(8,128)(2,1)S(1)}, bf16[2,2,16,1536]{3,2,0,1:T(8,128)(2,1)S(1)}, u32[]{:S(2)}, u32[]{:S(2)}) %collective-permute-start.15) | collective-permute-done | bytes 196640 | tf_op jit(solution)/shard_map/ppermute | solution.py:137
  62.0 1.7 %collective-permute-start.18 = (bf16[2,2,16,1536]{3,2,1,0:T(8,128)(2,1)S(1)}, bf16[2,2,16,1536]{3,2,1,0:T(8,128)(2,1)S(1)}, u32[]{:S(2)}, u32[]{:S(2)}) collective-permute-start(bf16[2,2,16,1536]{3,2,1,0:T(8,128)(2,1)S(1)} %pad_maximum_fusion.8), channel_id=1, source_target_pairs={{0,48},{1,193},{2,50},{3,195},{4,52},{5,197},{6,54},{7,199},{8,56}... | collective-permute-start | bytes 589832 | tf_op jit(solution)/shard_map/ppermute | solution.py:89
  63.7 2.3 %collective-permute-start.19 = (bf16[2,2,16,1536]{3,2,1,0:T(8,128)(2,1)S(1)}, bf16[2,2,16,1536]{3,2,1,0:T(8,128)(2,1)S(1)}, u32[]{:S(2)}, u32[]{:S(2)}) collective-permute-start(bf16[2,2,16,1536]{3,2,1,0:T(8,128)(2,1)S(1)} %pad_maximum_fusion.8), channel_id=1, source_target_pairs={{0,32},{1,129},{2,34},{3,131},{4,36},{5,133},{6,38},{7,135},{8,40}... | collective-permute-start | bytes 589832 | tf_op jit(solution)/shard_map/ppermute | solution.py:89
  66.1 1.5 %collective-permute-done.17 = bf16[2,2,16,1536]{3,2,1,0:T(8,128)(2,1)S(1)} collective-permute-done((bf16[2,2,16,1536]{3,2,1,0:T(8,128)(2,1)S(1)}, bf16[2,2,16,1536]{3,2,1,0:T(8,128)(2,1)S(1)}, u32[]{:S(2)}, u32[]{:S(2)}) %collective-permute-start.17) | collective-permute-done | bytes 196640 | tf_op jit(solution)/shard_map/ppermute | solution.py:89
  67.6 3.4 %collective-permute-done.18 = bf16[2,2,16,1536]{3,2,1,0:T(8,128)(2,1)S(1)} collective-permute-done((bf16[2,2,16,1536]{3,2,1,0:T(8,128)(2,1)S(1)}, bf16[2,2,16,1536]{3,2,1,0:T(8,128)(2,1)S(1)}, u32[]{:S(2)}, u32[]{:S(2)}) %collective-permute-start.18) | collective-permute-done | bytes 196640 | tf_op jit(solution)/shard_map/ppermute | solution.py:89
  71.1 1.9 %collective-permute-start.20 = (bf16[2,2,64,1536]{3,2,1,0:T(8,128)(2,1)S(1)}, bf16[2,2,64,1536]{3,2,1,0:T(8,128)(2,1)S(1)}, u32[]{:S(2)}, u32[]{:S(2)}) collective-permute-start(bf16[2,2,64,1536]{3,2,1,0:T(8,128)(2,1)S(1)} %bitcast.199), channel_id=1, source_target_pairs={{0,64},{1,17},{2,66},{3,19},{4,68},{5,21},{6,70},{7,23},{8,72},{9,... | collective-permute-start | bytes 2359304 | tf_op jit(solution)/shard_map/ppermute | solution.py:89
  74.2 1.4 %collective-permute-start.22 = (bf16[2,2,64,1536]{3,2,1,0:T(8,128)(2,1)S(1)}, bf16[2,2,64,1536]{3,2,1,0:T(8,128)(2,1)S(1)}, u32[]{:S(2)}, u32[]{:S(2)}) collective-permute-start(bf16[2,2,64,1536]{3,2,1,0:T(8,128)(2,1)S(1)} %bitcast.201), channel_id=1, source_target_pairs={{0,128},{1,33},{2,130},{3,35},{4,132},{5,37},{6,134},{7,39},{8,136... | collective-permute-start | bytes 2359304 | tf_op jit(solution)/shard_map/ppermute | solution.py:89
  76.0 7.2 %collective-permute-done.20 = bf16[2,2,64,1536]{3,2,1,0:T(8,128)(2,1)S(1)} collective-permute-done((bf16[2,2,64,1536]{3,2,1,0:T(8,128)(2,1)S(1)}, bf16[2,2,64,1536]{3,2,1,0:T(8,128)(2,1)S(1)}, u32[]{:S(2)}, u32[]{:S(2)}) %collective-permute-start.20) | collective-permute-done | bytes 786464 | tf_op jit(solution)/shard_map/ppermute | solution.py:89
  83.2 11.3 %collective-permute-done.21 = bf16[2,2,64,1536]{3,2,1,0:T(8,128)(2,1)S(1)} collective-permute-done((bf16[2,2,64,1536]{3,2,1,0:T(8,128)(2,1)S(1)}, bf16[2,2,64,1536]{3,2,1,0:T(8,128)(2,1)S(1)}, u32[]{:S(2)}, u32[]{:S(2)}) %collective-permute-start.21) | collective-permute-done | bytes 786464 | tf_op jit(solution)/shard_map/ppermute | solution.py:89
  99.2 3.2 %collective-permute-start.25 = (bf16[2,32,768]{2,1,0:T(8,128)(2,1)S(1)}, bf16[2,32,768]{2,1,0:T(8,128)(2,1)S(1)}, u32[]{:S(2)}, u32[]{:S(2)}) collective-permute-start(bf16[2,32,768]{2,1,0:T(8,128)(2,1)S(1)} %get-tuple-element.61), channel_id=1, source_target_pairs={{0,4},{1,5},{2,6},{3,7},{4,0},{5,1},{6,2},{7,3},{8,12},{9,13},{10,... | collective-permute-start | bytes 294920 | tf_op jit(solution)/shard_map/ppermute | solution.py:65
  102.6 4.5 %collective-permute-start.30 = (bf16[2,32,768]{2,1,0:T(8,128)(2,1)S(1)}, bf16[2,32,768]{2,1,0:T(8,128)(2,1)S(1)}, u32[]{:S(2)}, u32[]{:S(2)}) collective-permute-start(bf16[2,32,768]{2,1,0:T(8,128)(2,1)S(1)} %get-tuple-element.63), channel_id=1, source_target_pairs={{0,12},{1,13},{2,14},{3,15},{4,8},{5,9},{6,10},{7,11},{8,4},{9,5},... | collective-permute-start | bytes 294920 | tf_op jit(solution)/shard_map/ppermute | solution.py:65
  107.4 1.8 %collective-permute-start.28 = (bf16[2,32,768]{2,1,0:T(8,128)(2,1)S(1)}, bf16[2,32,768]{2,1,0:T(8,128)(2,1)S(1)}, u32[]{:S(2)}, u32[]{:S(2)}) collective-permute-start(bf16[2,32,768]{2,1,0:T(8,128)(2,1)S(1)} %get-tuple-element.58), channel_id=1, source_target_pairs={{0,6},{1,7},{2,4},{3,5},{4,2},{5,3},{6,0},{7,1},{8,14},{9,15},{10,... | collective-permute-start | bytes 294920 | tf_op jit(solution)/shard_map/ppermute | solution.py:65
  109.2 2.9 %collective-permute-start.27 = (bf16[2,32,768]{2,1,0:T(8,128)(2,1)S(1)}, bf16[2,32,768]{2,1,0:T(8,128)(2,1)S(1)}, u32[]{:S(2)}, u32[]{:S(2)}) collective-permute-start(bf16[2,32,768]{2,1,0:T(8,128)(2,1)S(1)} %get-tuple-element.59), channel_id=1, source_target_pairs={{0,10},{1,11},{2,8},{3,9},{4,14},{5,15},{6,12},{7,13},{8,2},{9,3},... | collective-permute-start | bytes 294920 | tf_op jit(solution)/shard_map/ppermute | solution.py:65
  112.1 2.0 %collective-permute-start.26 = (bf16[2,32,768]{2,1,0:T(8,128)(2,1)S(1)}, bf16[2,32,768]{2,1,0:T(8,128)(2,1)S(1)}, u32[]{:S(2)}, u32[]{:S(2)}) collective-permute-start(bf16[2,32,768]{2,1,0:T(8,128)(2,1)S(1)} %get-tuple-element.60), channel_id=1, source_target_pairs={{0,8},{1,9},{2,10},{3,11},{4,12},{5,13},{6,14},{7,15},{8,0},{9,1},... | collective-permute-start | bytes 294920 | tf_op jit(solution)/shard_map/ppermute | solution.py:65
  114.1 2.8 %multiply_convert_fusion.1 = bf16[768,1536]{1,0:T(8,128)(2,1)} fusion(bf16[2,512,1536]{2,1,0:T(8,128)(2,1)S(1)} %pad_maximum_fusion, bf16[2,256,768]{2,1,0:T(8,128)(2,1)S(1)} %bitcast.207, bf16[2,256,768]{2,1,0:T(8,128)(2,1)S(1)} %collective-permute-done.10), kind=kOutput, calls=%fused_computation.1 | convolution fusion | flops 1211891712 | bytes 5505024 | tf_op jit(solution)/shard_map/dot_general | solution.py:26
  117.0 2.8 %multiply_convert_fusion = bf16[1536,768]{1,0:T(8,128)(2,1)} fusion(bf16[2,512,1536]{2,1,0:T(8,128)(2,1)S(1)} %pad_maximum_fusion, bf16[2,256,768]{2,1,0:T(8,128)(2,1)S(1)} %collective-permute-done.10, bf16[2,256,768]{2,1,0:T(8,128)(2,1)S(1)} %bitcast.208), kind=kOutput, calls=%fused_computation | convolution fusion | flops 1211891712 | bytes 5505024 | tf_op jit(solution)/shard_map/dot_general | solution.py:26
  119.8 1.7 %collective-permute-done.29 = bf16[2,32,768]{2,1,0:T(8,128)(2,1)S(1)} collective-permute-done((bf16[2,32,768]{2,1,0:T(8,128)(2,1)S(1)}, bf16[2,32,768]{2,1,0:T(8,128)(2,1)S(1)}, u32[]{:S(2)}, u32[]{:S(2)}) %collective-permute-start.29) | collective-permute-done | bytes 98336 | tf_op jit(solution)/shard_map/ppermute | solution.py:65
  121.5 2.0 %collective-permute-done.27 = bf16[2,32,768]{2,1,0:T(8,128)(2,1)S(1)} collective-permute-done((bf16[2,32,768]{2,1,0:T(8,128)(2,1)S(1)}, bf16[2,32,768]{2,1,0:T(8,128)(2,1)S(1)}, u32[]{:S(2)}, u32[]{:S(2)}) %collective-permute-start.27) | collective-permute-done | bytes 98336 | tf_op jit(solution)/shard_map/ppermute | solution.py:65
  (83 shorter events, 18.6 us)
Async XLA Ops:
  0.6 26.4 %copy-start = (bf16[768,1536]{1,0:T(8,128)(2,1)S(1)}, bf16[768,1536]{1,0:T(8,128)(2,1)}, u32[]{:S(2)}) copy-start(bf16[768,1536]{1,0:T(8,128)(2,1)} %param.5) | copy-start | bytes 7077892
  1.6 10.8 %collective-permute-start = (bf16[2,32,768]{2,1,0:T(8,128)(2,1)S(1)}, bf16[2,32,768]{2,1,0:T(8,128)(2,1)S(1)}, u32[]{:S(2)}, u32[]{:S(2)}) collective-permute-start(bf16[2,32,768]{2,1,0:T(8,128)(2,1)S(1)} %pad_maximum_fusion.9), channel_id=1, source_target_pairs={{0,2},{1,3},{2,0},{3,1},{4,6},{5,7},{6,4},{7,5},{8,10},{9,11},{10,... | collective-permute-start | bytes 294920 | tf_op jit(solution)/shard_map/ppermute | solution.py:65
  3.6 12.9 %collective-permute-start.1 = (bf16[2,32,768]{2,1,0:T(8,128)(2,1)S(1)}, bf16[2,32,768]{2,1,0:T(8,128)(2,1)S(1)}, u32[]{:S(2)}, u32[]{:S(2)}) collective-permute-start(bf16[2,32,768]{2,1,0:T(8,128)(2,1)S(1)} %pad_maximum_fusion.9), channel_id=1, source_target_pairs={{0,4},{1,5},{2,6},{3,7},{4,0},{5,1},{6,2},{7,3},{8,12},{9,13},{10,... | collective-permute-start | bytes 294920 | tf_op jit(solution)/shard_map/ppermute | solution.py:65
  6.9 10.5 %collective-permute-start.2 = (bf16[2,32,768]{2,1,0:T(8,128)(2,1)S(1)}, bf16[2,32,768]{2,1,0:T(8,128)(2,1)S(1)}, u32[]{:S(2)}, u32[]{:S(2)}) collective-permute-start(bf16[2,32,768]{2,1,0:T(8,128)(2,1)S(1)} %pad_maximum_fusion.9), channel_id=1, source_target_pairs={{0,12},{1,13},{2,14},{3,15},{4,8},{5,9},{6,10},{7,11},{8,4},{9,5},... | collective-permute-start | bytes 294920 | tf_op jit(solution)/shard_map/ppermute | solution.py:65
  10.5 15.9 %collective-permute-start.3 = (bf16[2,32,768]{2,1,0:T(8,128)(2,1)S(1)}, bf16[2,32,768]{2,1,0:T(8,128)(2,1)S(1)}, u32[]{:S(2)}, u32[]{:S(2)}) collective-permute-start(bf16[2,32,768]{2,1,0:T(8,128)(2,1)S(1)} %pad_maximum_fusion.9), channel_id=1, source_target_pairs={{0,14},{1,15},{2,12},{3,13},{4,10},{5,11},{6,8},{7,9},{8,6},{9,7},... | collective-permute-start | bytes 294920 | tf_op jit(solution)/shard_map/ppermute | solution.py:65
  10.5 15.9 %collective-permute-start.4 = (bf16[2,32,768]{2,1,0:T(8,128)(2,1)S(1)}, bf16[2,32,768]{2,1,0:T(8,128)(2,1)S(1)}, u32[]{:S(2)}, u32[]{:S(2)}) collective-permute-start(bf16[2,32,768]{2,1,0:T(8,128)(2,1)S(1)} %pad_maximum_fusion.9), channel_id=1, source_target_pairs={{0,6},{1,7},{2,4},{3,5},{4,2},{5,3},{6,0},{7,1},{8,14},{9,15},{10,... | collective-permute-start | bytes 294920 | tf_op jit(solution)/shard_map/ppermute | solution.py:65
  12.4 14.3 %collective-permute-start.5 = (bf16[2,32,768]{2,1,0:T(8,128)(2,1)S(1)}, bf16[2,32,768]{2,1,0:T(8,128)(2,1)S(1)}, u32[]{:S(2)}, u32[]{:S(2)}) collective-permute-start(bf16[2,32,768]{2,1,0:T(8,128)(2,1)S(1)} %pad_maximum_fusion.9), channel_id=1, source_target_pairs={{0,10},{1,11},{2,8},{3,9},{4,14},{5,15},{6,12},{7,13},{8,2},{9,3},... | collective-permute-start | bytes 294920 | tf_op jit(solution)/shard_map/ppermute | solution.py:65
  16.5 10.2 %collective-permute-start.6 = (bf16[2,32,768]{2,1,0:T(8,128)(2,1)S(1)}, bf16[2,32,768]{2,1,0:T(8,128)(2,1)S(1)}, u32[]{:S(2)}, u32[]{:S(2)}) collective-permute-start(bf16[2,32,768]{2,1,0:T(8,128)(2,1)S(1)} %pad_maximum_fusion.9), channel_id=1, source_target_pairs={{0,8},{1,9},{2,10},{3,11},{4,12},{5,13},{6,14},{7,15},{8,0},{9,1},... | collective-permute-start | bytes 294920 | tf_op jit(solution)/shard_map/ppermute | solution.py:65
  26.9 6.8 %collective-permute-start.10 = (bf16[2,256,768]{2,1,0:T(8,128)(2,1)S(1)}, bf16[2,256,768]{2,1,0:T(8,128)(2,1)S(1)}, u32[]{:S(2)}, u32[]{:S(2)}) collective-permute-start(bf16[2,256,768]{2,1,0:T(8,128)(2,1)S(1)} %bitcast.206), channel_id=1, source_target_pairs={{0,1},{1,0},{2,3},{3,2},{4,5},{5,4},{6,7},{7,6},{8,9},{9,8},{10,11... | collective-permute-start | bytes 2359304 | tf_op jit(solution)/shard_map/ppermute | solution.py:59
  29.5 10.8 %collective-permute-start.9 = (bf16[2,64,1536]{2,1,0:T(8,128)(2,1)S(1)}, bf16[2,64,1536]{2,1,0:T(8,128)(2,1)S(1)}, u32[]{:S(2)}, u32[]{:S(2)}) collective-permute-start(bf16[2,64,1536]{2,1,0:T(8,128)(2,1)S(1)} %get-tuple-element.35), channel_id=1, source_target_pairs={{0,128},{1,33},{2,130},{3,35},{4,132},{5,37},{6,134},{7,39},{8,136... | collective-permute-start | bytes 1179656 | tf_op jit(solution)/shard_map/ppermute | solution.py:77
  32.6 10.5 %collective-permute-start.8 = (bf16[2,64,1536]{2,1,0:T(8,128)(2,1)S(1)}, bf16[2,64,1536]{2,1,0:T(8,128)(2,1)S(1)}, u32[]{:S(2)}, u32[]{:S(2)}) collective-permute-start(bf16[2,64,1536]{2,1,0:T(8,128)(2,1)S(1)} %get-tuple-element.34), channel_id=1, source_target_pairs={{0,192},{1,49},{2,194},{3,51},{4,196},{5,53},{6,198},{7,55},{8,200... | collective-permute-start | bytes 1179656 | tf_op jit(solution)/shard_map/ppermute | solution.py:77
  33.8 9.5 %collective-permute-start.7 = (bf16[2,64,1536]{2,1,0:T(8,128)(2,1)S(1)}, bf16[2,64,1536]{2,1,0:T(8,128)(2,1)S(1)}, u32[]{:S(2)}, u32[]{:S(2)}) collective-permute-start(bf16[2,64,1536]{2,1,0:T(8,128)(2,1)S(1)} %get-tuple-element.33), channel_id=1, source_target_pairs={{0,64},{1,17},{2,66},{3,19},{4,68},{5,21},{6,70},{7,23},{8,72},{9,... | collective-permute-start | bytes 1179656 | tf_op jit(solution)/shard_map/ppermute | solution.py:77
  35.5 11.9 %collective-permute-start.13 = (bf16[2,64,1536]{2,1,0:T(8,128)(2,1)S(1)}, bf16[2,64,1536]{2,1,0:T(8,128)(2,1)S(1)}, u32[]{:S(2)}, u32[]{:S(2)}) collective-permute-start(bf16[2,64,1536]{2,1,0:T(8,128)(2,1)S(1)} %get-tuple-element.40), channel_id=1, source_target_pairs={{0,128},{1,33},{2,130},{3,35},{4,132},{5,37},{6,134},{7,39},{8,136... | collective-permute-start | bytes 1179656 | tf_op jit(solution)/shard_map/ppermute | solution.py:77
  39.2 12.3 %collective-permute-start.12 = (bf16[2,64,1536]{2,1,0:T(8,128)(2,1)S(1)}, bf16[2,64,1536]{2,1,0:T(8,128)(2,1)S(1)}, u32[]{:S(2)}, u32[]{:S(2)}) collective-permute-start(bf16[2,64,1536]{2,1,0:T(8,128)(2,1)S(1)} %get-tuple-element.39), channel_id=1, source_target_pairs={{0,192},{1,49},{2,194},{3,51},{4,196},{5,53},{6,198},{7,55},{8,200... | collective-permute-start | bytes 1179656 | tf_op jit(solution)/shard_map/ppermute | solution.py:77
  40.3 11.4 %collective-permute-start.11 = (bf16[2,64,1536]{2,1,0:T(8,128)(2,1)S(1)}, bf16[2,64,1536]{2,1,0:T(8,128)(2,1)S(1)}, u32[]{:S(2)}, u32[]{:S(2)}) collective-permute-start(bf16[2,64,1536]{2,1,0:T(8,128)(2,1)S(1)} %get-tuple-element.38), channel_id=1, source_target_pairs={{0,64},{1,17},{2,66},{3,19},{4,68},{5,21},{6,70},{7,23},{8,72},{9,... | collective-permute-start | bytes 1179656 | tf_op jit(solution)/shard_map/ppermute | solution.py:77
  52.0 7.4 %collective-permute-start.16 = (bf16[2,2,16,1536]{3,2,0,1:T(8,128)(2,1)S(1)}, bf16[2,2,16,1536]{3,2,0,1:T(8,128)(2,1)S(1)}, u32[]{:S(2)}, u32[]{:S(2)}) collective-permute-start(bf16[2,2,16,1536]{3,2,0,1:T(8,128)(2,1)S(1)} %pad_maximum_fusion.6), channel_id=1, source_target_pairs={{0,32},{1,129},{2,34},{3,131},{4,36},{5,133},{6,38},{7,135},{8,40}... | collective-permute-start | bytes 589832 | tf_op jit(solution)/shard_map/ppermute | solution.py:137
  53.3 8.0 %collective-permute-start.15 = (bf16[2,2,16,1536]{3,2,0,1:T(8,128)(2,1)S(1)}, bf16[2,2,16,1536]{3,2,0,1:T(8,128)(2,1)S(1)}, u32[]{:S(2)}, u32[]{:S(2)}) collective-permute-start(bf16[2,2,16,1536]{3,2,0,1:T(8,128)(2,1)S(1)} %pad_maximum_fusion.5), channel_id=1, source_target_pairs={{0,48},{1,193},{2,50},{3,195},{4,52},{5,197},{6,54},{7,199},{8,56}... | collective-permute-start | bytes 589832 | tf_op jit(solution)/shard_map/ppermute | solution.py:137
  55.6 5.9 %collective-permute-start.14 = (bf16[2,2,16,1536]{3,2,0,1:T(8,128)(2,1)S(1)}, bf16[2,2,16,1536]{3,2,0,1:T(8,128)(2,1)S(1)}, u32[]{:S(2)}, u32[]{:S(2)}) collective-permute-start(bf16[2,2,16,1536]{3,2,0,1:T(8,128)(2,1)S(1)} %pad_maximum_fusion.4), channel_id=1, source_target_pairs={{0,16},{1,65},{2,18},{3,67},{4,20},{5,69},{6,22},{7,71},{8,24},{9,... | collective-permute-start | bytes 589832 | tf_op jit(solution)/shard_map/ppermute | solution.py:137
  61.8 5.8 %collective-permute-start.17 = (bf16[2,2,16,1536]{3,2,1,0:T(8,128)(2,1)S(1)}, bf16[2,2,16,1536]{3,2,1,0:T(8,128)(2,1)S(1)}, u32[]{:S(2)}, u32[]{:S(2)}) collective-permute-start(bf16[2,2,16,1536]{3,2,1,0:T(8,128)(2,1)S(1)} %pad_maximum_fusion.8), channel_id=1, source_target_pairs={{0,16},{1,65},{2,18},{3,67},{4,20},{5,69},{6,22},{7,71},{8,24},{9,... | collective-permute-start | bytes 589832 | tf_op jit(solution)/shard_map/ppermute | solution.py:89
  62.0 9.0 %collective-permute-start.18 = (bf16[2,2,16,1536]{3,2,1,0:T(8,128)(2,1)S(1)}, bf16[2,2,16,1536]{3,2,1,0:T(8,128)(2,1)S(1)}, u32[]{:S(2)}, u32[]{:S(2)}) collective-permute-start(bf16[2,2,16,1536]{3,2,1,0:T(8,128)(2,1)S(1)} %pad_maximum_fusion.8), channel_id=1, source_target_pairs={{0,48},{1,193},{2,50},{3,195},{4,52},{5,197},{6,54},{7,199},{8,56}... | collective-permute-start | bytes 589832 | tf_op jit(solution)/shard_map/ppermute | solution.py:89
  63.7 7.4 %collective-permute-start.19 = (bf16[2,2,16,1536]{3,2,1,0:T(8,128)(2,1)S(1)}, bf16[2,2,16,1536]{3,2,1,0:T(8,128)(2,1)S(1)}, u32[]{:S(2)}, u32[]{:S(2)}) collective-permute-start(bf16[2,2,16,1536]{3,2,1,0:T(8,128)(2,1)S(1)} %pad_maximum_fusion.8), channel_id=1, source_target_pairs={{0,32},{1,129},{2,34},{3,131},{4,36},{5,133},{6,38},{7,135},{8,40}... | collective-permute-start | bytes 589832 | tf_op jit(solution)/shard_map/ppermute | solution.py:89
  71.1 12.1 %collective-permute-start.20 = (bf16[2,2,64,1536]{3,2,1,0:T(8,128)(2,1)S(1)}, bf16[2,2,64,1536]{3,2,1,0:T(8,128)(2,1)S(1)}, u32[]{:S(2)}, u32[]{:S(2)}) collective-permute-start(bf16[2,2,64,1536]{3,2,1,0:T(8,128)(2,1)S(1)} %bitcast.199), channel_id=1, source_target_pairs={{0,64},{1,17},{2,66},{3,19},{4,68},{5,21},{6,70},{7,23},{8,72},{9,... | collective-permute-start | bytes 2359304 | tf_op jit(solution)/shard_map/ppermute | solution.py:89
  72.9 21.6 %collective-permute-start.21 = (bf16[2,2,64,1536]{3,2,1,0:T(8,128)(2,1)S(1)}, bf16[2,2,64,1536]{3,2,1,0:T(8,128)(2,1)S(1)}, u32[]{:S(2)}, u32[]{:S(2)}) collective-permute-start(bf16[2,2,64,1536]{3,2,1,0:T(8,128)(2,1)S(1)} %bitcast.200), channel_id=1, source_target_pairs={{0,192},{1,49},{2,194},{3,51},{4,196},{5,53},{6,198},{7,55},{8,200... | collective-permute-start | bytes 2359304 | tf_op jit(solution)/shard_map/ppermute | solution.py:89
  74.2 20.4 %collective-permute-start.22 = (bf16[2,2,64,1536]{3,2,1,0:T(8,128)(2,1)S(1)}, bf16[2,2,64,1536]{3,2,1,0:T(8,128)(2,1)S(1)}, u32[]{:S(2)}, u32[]{:S(2)}) collective-permute-start(bf16[2,2,64,1536]{3,2,1,0:T(8,128)(2,1)S(1)} %bitcast.201), channel_id=1, source_target_pairs={{0,128},{1,33},{2,130},{3,35},{4,132},{5,37},{6,134},{7,39},{8,136... | collective-permute-start | bytes 2359304 | tf_op jit(solution)/shard_map/ppermute | solution.py:89
  96.6 2.4 %collective-permute-start.23 = (bf16[2,256,768]{2,1,0:T(8,128)(2,1)S(1)}, bf16[2,256,768]{2,1,0:T(8,128)(2,1)S(1)}, u32[]{:S(2)}, u32[]{:S(2)}) collective-permute-start(bf16[2,256,768]{2,1,0:T(8,128)(2,1)S(1)} %pad_maximum_fusion.3), channel_id=1, source_target_pairs={{0,1},{1,0},{2,3},{3,2},{4,5},{5,4},{6,7},{7,6},{8,9},{9,8},{10,11... | collective-permute-start | bytes 2359304 | tf_op jit(solution)/shard_map/ppermute | solution.py:59
  99.2 10.0 %collective-permute-start.25 = (bf16[2,32,768]{2,1,0:T(8,128)(2,1)S(1)}, bf16[2,32,768]{2,1,0:T(8,128)(2,1)S(1)}, u32[]{:S(2)}, u32[]{:S(2)}) collective-permute-start(bf16[2,32,768]{2,1,0:T(8,128)(2,1)S(1)} %get-tuple-element.61), channel_id=1, source_target_pairs={{0,4},{1,5},{2,6},{3,7},{4,0},{5,1},{6,2},{7,3},{8,12},{9,13},{10,... | collective-permute-start | bytes 294920 | tf_op jit(solution)/shard_map/ppermute | solution.py:65
  102.4 9.7 %collective-permute-start.24 = (bf16[2,32,768]{2,1,0:T(8,128)(2,1)S(1)}, bf16[2,32,768]{2,1,0:T(8,128)(2,1)S(1)}, u32[]{:S(2)}, u32[]{:S(2)}) collective-permute-start(bf16[2,32,768]{2,1,0:T(8,128)(2,1)S(1)} %get-tuple-element.62), channel_id=1, source_target_pairs={{0,2},{1,3},{2,0},{3,1},{4,6},{5,7},{6,4},{7,5},{8,10},{9,11},{10,... | collective-permute-start | bytes 294920 | tf_op jit(solution)/shard_map/ppermute | solution.py:65
  102.6 17.2 %collective-permute-start.30 = (bf16[2,32,768]{2,1,0:T(8,128)(2,1)S(1)}, bf16[2,32,768]{2,1,0:T(8,128)(2,1)S(1)}, u32[]{:S(2)}, u32[]{:S(2)}) collective-permute-start(bf16[2,32,768]{2,1,0:T(8,128)(2,1)S(1)} %get-tuple-element.63), channel_id=1, source_target_pairs={{0,12},{1,13},{2,14},{3,15},{4,8},{5,9},{6,10},{7,11},{8,4},{9,5},... | collective-permute-start | bytes 294920 | tf_op jit(solution)/shard_map/ppermute | solution.py:65
  107.1 14.4 %collective-permute-start.29 = (bf16[2,32,768]{2,1,0:T(8,128)(2,1)S(1)}, bf16[2,32,768]{2,1,0:T(8,128)(2,1)S(1)}, u32[]{:S(2)}, u32[]{:S(2)}) collective-permute-start(bf16[2,32,768]{2,1,0:T(8,128)(2,1)S(1)} %get-tuple-element.57), channel_id=1, source_target_pairs={{0,14},{1,15},{2,12},{3,13},{4,10},{5,11},{6,8},{7,9},{8,6},{9,7},... | collective-permute-start | bytes 294920 | tf_op jit(solution)/shard_map/ppermute | solution.py:65
  107.4 14.1 %collective-permute-start.28 = (bf16[2,32,768]{2,1,0:T(8,128)(2,1)S(1)}, bf16[2,32,768]{2,1,0:T(8,128)(2,1)S(1)}, u32[]{:S(2)}, u32[]{:S(2)}) collective-permute-start(bf16[2,32,768]{2,1,0:T(8,128)(2,1)S(1)} %get-tuple-element.58), channel_id=1, source_target_pairs={{0,6},{1,7},{2,4},{3,5},{4,2},{5,3},{6,0},{7,1},{8,14},{9,15},{10,... | collective-permute-start | bytes 294920 | tf_op jit(solution)/shard_map/ppermute | solution.py:65
  109.2 14.3 %collective-permute-start.27 = (bf16[2,32,768]{2,1,0:T(8,128)(2,1)S(1)}, bf16[2,32,768]{2,1,0:T(8,128)(2,1)S(1)}, u32[]{:S(2)}, u32[]{:S(2)}) collective-permute-start(bf16[2,32,768]{2,1,0:T(8,128)(2,1)S(1)} %get-tuple-element.59), channel_id=1, source_target_pairs={{0,10},{1,11},{2,8},{3,9},{4,14},{5,15},{6,12},{7,13},{8,2},{9,3},... | collective-permute-start | bytes 294920 | tf_op jit(solution)/shard_map/ppermute | solution.py:65
  112.1 11.4 %collective-permute-start.26 = (bf16[2,32,768]{2,1,0:T(8,128)(2,1)S(1)}, bf16[2,32,768]{2,1,0:T(8,128)(2,1)S(1)}, u32[]{:S(2)}, u32[]{:S(2)}) collective-permute-start(bf16[2,32,768]{2,1,0:T(8,128)(2,1)S(1)} %get-tuple-element.60), channel_id=1, source_target_pairs={{0,8},{1,9},{2,10},{3,11},{4,12},{5,13},{6,14},{7,15},{8,0},{9,1},... | collective-permute-start | bytes 294920 | tf_op jit(solution)/shard_map/ppermute | solution.py:65
  (1 other events, 1.7 us)

commit v4 on v3

--- a/solution.py
+++ b/solution.py
@@ -7,8 +7,8 @@
 cubic_term = 0.044715
 side = 4
 planes = 8
-order = (0, 1, 2, 6, 7, 3, 5, 4)
-sent_order = (1, 2, 4, 5, 3, 7, 6)
+order = (0, 1, -1, 2, -2, 3, -3, 4)
+sent_order = (1, -1, 4, -3, 3, -2, 2)
 both = ("row", "col")
 
 
@@ -59,10 +59,10 @@
     return lax.ppermute(block, "col", core_pairs)
 
 
-def to_plane(block, flip):
-    if flip == 0:
+def to_plane(block, ahead):
+    if ahead == 0:
         return block
-    return lax.ppermute(block, "col", [(i, i ^ (2 * flip)) for i in range(planes * 2)])
+    return lax.ppermute(block, "col", [(i, (i + 2 * ahead) % (planes * 2)) for i in range(planes * 2)])
 
 
 def after(value, *others):
@@ -117,7 +117,7 @@
         return output_part, contract_cols(acts[1], weight_in)
 
     pair = jnp.stack([tokens, cotangent])
-    mine = lax.optimization_barrier([to_plane(pair, flip) for flip in order])
+    mine = lax.optimization_barrier([to_plane(pair, -ahead) for ahead in order])
     own = jnp.stack(mine, axis=1).reshape(2, planes * rows, width)
     other = other_core(own)
 
@@ -146,15 +146,15 @@
     own_act = after(acts[0], other_back)
     back = jnp.stack(project_back(own_act)) + other_core(other_back).astype(jnp.float32)
     back = back.astype(jnp.bfloat16).reshape(2, planes, rows, width)
-    came = {flip: to_plane(back[:, order.index(flip)], flip) for flip in sent_order}
+    came = {ahead: to_plane(back[:, order.index(ahead)], ahead) for ahead in sent_order}
 
-    acts = after(jnp.concatenate([acts[0], acts[1]], axis=1), came[1], came[2])
+    acts = after(jnp.concatenate([acts[0], acts[1]], axis=1), came[1], came[-1])
     gathered = jnp.concatenate([own, other], axis=1)
     grad_out = (contract_rows(acts[0], gathered[1]) * grad_scale).astype(jnp.bfloat16)
     grad_in = (contract_rows(gathered[0], acts[1]) * grad_scale).astype(jnp.bfloat16)
     total = after(back[:, order.index(0)], grad_in, grad_out).astype(jnp.float32)
-    for flip in sent_order:
-        total = total + came[flip].astype(jnp.float32)
+    for ahead in sent_order:
+        total = total + came[ahead].astype(jnp.float32)
     total = total.astype(jnp.bfloat16)
     return (total[0], total[1], grad_in, grad_out)
 

time: 127 us -> 127 us (level)
  the two profiles are of different devices: /device:TPU:24 before, /device:TPU:32 now
where the time goes in v4:
time: 127 us
  starting transfers between devices  54.8 us (43%)
  waiting for transfers between devices  53.6 us (42%)
  matrix products  12 us (9%)
  local copies, waits for them, and re-layouts  2.73 us (2%)
  other arithmetic  2.59 us (2%)
    ppermute x14, starting transfers between devices, to_plane(): lax.ppermute(block, 'col', [(i, (i + 2 * ahead) % (planes * 2)) for i in...  32.5 us
    ppermute x6, waiting for transfers between devices, ring_share(): return [lax.ppermute(block, both, ring[first, flip]) for flip in flips]  24.1 us
    ppermute x14, waiting for transfers between devices, to_plane(): lax.ppermute(block, 'col', [(i, (i + 2 * ahead) % (planes * 2)) for i in...  12.4 us
    ppermute x6, waiting for transfers between devices, ring_send(): lax.ppermute(piece, both, ring[first, flip])  11 us
    ppermute x6, starting transfers between devices, ring_send(): lax.ppermute(piece, both, ring[first, flip])  9.2 us
    ppermute x6, starting transfers between devices, ring_share(): return [lax.ppermute(block, both, ring[first, flip]) for flip in flips]  8.36 us
    ppermute x3, waiting for transfers between devices, local(): lax.ppermute(pick(place_two ^ flip), both, ring[False, flip])  5.7 us
    dot_general x2, matrix products, contract_rows(): lax.dot_general(left, right, (((0,), (0,)), ((), ())), preferred_element_...  5.67 us
  transfers between devices with their start and end apart: 31, of which 17 were waited for; matrix products, arithmetic and copies ran while one was open for 10% of the time, Pallas kernels for 0%

profile of v4, /device:TPU:32, one launch (start us, length us, event | category | flops | bytes accessed | tf_op | source)
XLA Modules:
  0.0 126.8 jit_solution(1698670095766372743)
XLA Ops:
  1.6 1.9 %collective-permute-start = (bf16[2,32,768]{2,1,0:T(8,128)(2,1)S(1)}, bf16[2,32,768]{2,1,0:T(8,128)(2,1)S(1)}, u32[]{:S(2)}, u32[]{:S(2)}) collective-permute-start(bf16[2,32,768]{2,1,0:T(8,128)(2,1)S(1)} %pad_maximum_fusion.9), channel_id=1, source_target_pairs={{0,14},{1,15},{2,0},{3,1},{4,2},{5,3},{6,4},{7,5},{8,6},{9,7},{10,... | collective-permute-start | bytes 294920 | tf_op jit(solution)/shard_map/ppermute | solution.py:65
  3.7 6.6 %collective-permute-start.2 = (bf16[2,32,768]{2,1,0:T(8,128)(2,1)S(1)}, bf16[2,32,768]{2,1,0:T(8,128)(2,1)S(1)}, u32[]{:S(2)}, u32[]{:S(2)}) collective-permute-start(bf16[2,32,768]{2,1,0:T(8,128)(2,1)S(1)} %pad_maximum_fusion.9), channel_id=1, source_target_pairs={{0,12},{1,13},{2,14},{3,15},{4,0},{5,1},{6,2},{7,3},{8,4},{9,5},{1... | collective-permute-start | bytes 294920 | tf_op jit(solution)/shard_map/ppermute | solution.py:65
  10.4 3.4 %collective-permute-start.4 = (bf16[2,32,768]{2,1,0:T(8,128)(2,1)S(1)}, bf16[2,32,768]{2,1,0:T(8,128)(2,1)S(1)}, u32[]{:S(2)}, u32[]{:S(2)}) collective-permute-start(bf16[2,32,768]{2,1,0:T(8,128)(2,1)S(1)} %pad_maximum_fusion.9), channel_id=1, source_target_pairs={{0,10},{1,11},{2,12},{3,13},{4,14},{5,15},{6,0},{7,1},{8,2},{9,3},... | collective-permute-start | bytes 294920 | tf_op jit(solution)/shard_map/ppermute | solution.py:65
  13.7 1.7 %collective-permute-start.5 = (bf16[2,32,768]{2,1,0:T(8,128)(2,1)S(1)}, bf16[2,32,768]{2,1,0:T(8,128)(2,1)S(1)}, u32[]{:S(2)}, u32[]{:S(2)}) collective-permute-start(bf16[2,32,768]{2,1,0:T(8,128)(2,1)S(1)} %pad_maximum_fusion.9), channel_id=1, source_target_pairs={{0,6},{1,7},{2,8},{3,9},{4,10},{5,11},{6,12},{7,13},{8,14},{9,15},... | collective-permute-start | bytes 294920 | tf_op jit(solution)/shard_map/ppermute | solution.py:65
  15.4 2.6 %collective-permute-start.6 = (bf16[2,32,768]{2,1,0:T(8,128)(2,1)S(1)}, bf16[2,32,768]{2,1,0:T(8,128)(2,1)S(1)}, u32[]{:S(2)}, u32[]{:S(2)}) collective-permute-start(bf16[2,32,768]{2,1,0:T(8,128)(2,1)S(1)} %pad_maximum_fusion.9), channel_id=1, source_target_pairs={{0,8},{1,9},{2,10},{3,11},{4,12},{5,13},{6,14},{7,15},{8,0},{9,1},... | collective-permute-start | bytes 294920 | tf_op jit(solution)/shard_map/ppermute | solution.py:65
  20.3 5.7 %collective-permute-done.5 = bf16[2,32,768]{2,1,0:T(8,128)(2,1)S(1)} collective-permute-done((bf16[2,32,768]{2,1,0:T(8,128)(2,1)S(1)}, bf16[2,32,768]{2,1,0:T(8,128)(2,1)S(1)}, u32[]{:S(2)}, u32[]{:S(2)}) %collective-permute-start.5) | collective-permute-done | bytes 98336 | tf_op jit(solution)/shard_map/ppermute | solution.py:65
  28.8 3.1 %collective-permute-start.9 = (bf16[2,64,1536]{2,1,0:T(8,128)(2,1)S(1)}, bf16[2,64,1536]{2,1,0:T(8,128)(2,1)S(1)}, u32[]{:S(2)}, u32[]{:S(2)}) collective-permute-start(bf16[2,64,1536]{2,1,0:T(8,128)(2,1)S(1)} %get-tuple-element.35), channel_id=1, source_target_pairs={{0,128},{1,33},{2,130},{3,35},{4,132},{5,37},{6,134},{7,39},{8,136... | collective-permute-start | bytes 1179656 | tf_op jit(solution)/shard_map/ppermute | solution.py:77
  34.8 3.6 %collective-permute-start.13 = (bf16[2,64,1536]{2,1,0:T(8,128)(2,1)S(1)}, bf16[2,64,1536]{2,1,0:T(8,128)(2,1)S(1)}, u32[]{:S(2)}, u32[]{:S(2)}) collective-permute-start(bf16[2,64,1536]{2,1,0:T(8,128)(2,1)S(1)} %get-tuple-element.40), channel_id=1, source_target_pairs={{0,128},{1,33},{2,130},{3,35},{4,132},{5,37},{6,134},{7,39},{8,136... | collective-permute-start | bytes 1179656 | tf_op jit(solution)/shard_map/ppermute | solution.py:77
  39.8 2.6 %collective-permute-done.8 = bf16[2,64,1536]{2,1,0:T(8,128)(2,1)S(1)} collective-permute-done((bf16[2,64,1536]{2,1,0:T(8,128)(2,1)S(1)}, bf16[2,64,1536]{2,1,0:T(8,128)(2,1)S(1)}, u32[]{:S(2)}, u32[]{:S(2)}) %collective-permute-start.8) | collective-permute-done | bytes 393248 | tf_op jit(solution)/shard_map/ppermute | solution.py:77
  42.7 4.0 %collective-permute-done.13 = bf16[2,64,1536]{2,1,0:T(8,128)(2,1)S(1)} collective-permute-done((bf16[2,64,1536]{2,1,0:T(8,128)(2,1)S(1)}, bf16[2,64,1536]{2,1,0:T(8,128)(2,1)S(1)}, u32[]{:S(2)}, u32[]{:S(2)}) %collective-permute-start.13) | collective-permute-done | bytes 393248 | tf_op jit(solution)/shard_map/ppermute | solution.py:77
  46.7 4.1 %collective-permute-done.12 = bf16[2,64,1536]{2,1,0:T(8,128)(2,1)S(1)} collective-permute-done((bf16[2,64,1536]{2,1,0:T(8,128)(2,1)S(1)}, bf16[2,64,1536]{2,1,0:T(8,128)(2,1)S(1)}, u32[]{:S(2)}, u32[]{:S(2)}) %collective-permute-start.12) | collective-permute-done | bytes 393248 | tf_op jit(solution)/shard_map/ppermute | solution.py:77
  51.3 3.3 %collective-permute-start.16 = (bf16[2,2,16,1536]{3,2,0,1:T(8,128)(2,1)S(1)}, bf16[2,2,16,1536]{3,2,0,1:T(8,128)(2,1)S(1)}, u32[]{:S(2)}, u32[]{:S(2)}) collective-permute-start(bf16[2,2,16,1536]{3,2,0,1:T(8,128)(2,1)S(1)} %pad_maximum_fusion.6), channel_id=1, source_target_pairs={{0,32},{1,129},{2,34},{3,131},{4,36},{5,133},{6,38},{7,135},{8,40}... | collective-permute-start | bytes 589832 | tf_op jit(solution)/shard_map/ppermute | solution.py:137
  55.9 2.7 %collective-permute-done.16 = bf16[2,2,16,1536]{3,2,0,1:T(8,128)(2,1)S(1)} collective-permute-done((bf16[2,2,16,1536]{3,2,0,1:T(8,128)(2,1)S(1)}, bf16[2,2,16,1536]{3,2,0,1:T(8,128)(2,1)S(1)}, u32[]{:S(2)}, u32[]{:S(2)}) %collective-permute-start.16) | collective-permute-done | bytes 196640 | tf_op jit(solution)/shard_map/ppermute | solution.py:137
  58.5 3.0 %collective-permute-done.15 = bf16[2,2,16,1536]{3,2,0,1:T(8,128)(2,1)S(1)} collective-permute-done((bf16[2,2,16,1536]{3,2,0,1:T(8,128)(2,1)S(1)}, bf16[2,2,16,1536]{3,2,0,1:T(8,128)(2,1)S(1)}, u32[]{:S(2)}, u32[]{:S(2)}) %collective-permute-start.15) | collective-permute-done | bytes 196640 | tf_op jit(solution)/shard_map/ppermute | solution.py:137
  62.7 1.4 %collective-permute-start.18 = (bf16[2,2,16,1536]{3,2,1,0:T(8,128)(2,1)S(1)}, bf16[2,2,16,1536]{3,2,1,0:T(8,128)(2,1)S(1)}, u32[]{:S(2)}, u32[]{:S(2)}) collective-permute-start(bf16[2,2,16,1536]{3,2,1,0:T(8,128)(2,1)S(1)} %pad_maximum_fusion.8), channel_id=1, source_target_pairs={{0,48},{1,193},{2,50},{3,195},{4,52},{5,197},{6,54},{7,199},{8,56}... | collective-permute-start | bytes 589832 | tf_op jit(solution)/shard_map/ppermute | solution.py:89
  64.2 1.9 %collective-permute-start.19 = (bf16[2,2,16,1536]{3,2,1,0:T(8,128)(2,1)S(1)}, bf16[2,2,16,1536]{3,2,1,0:T(8,128)(2,1)S(1)}, u32[]{:S(2)}, u32[]{:S(2)}) collective-permute-start(bf16[2,2,16,1536]{3,2,1,0:T(8,128)(2,1)S(1)} %pad_maximum_fusion.8), channel_id=1, source_target_pairs={{0,32},{1,129},{2,34},{3,131},{4,36},{5,133},{6,38},{7,135},{8,40}... | collective-permute-start | bytes 589832 | tf_op jit(solution)/shard_map/ppermute | solution.py:89
  66.1 1.5 %collective-permute-done.17 = bf16[2,2,16,1536]{3,2,1,0:T(8,128)(2,1)S(1)} collective-permute-done((bf16[2,2,16,1536]{3,2,1,0:T(8,128)(2,1)S(1)}, bf16[2,2,16,1536]{3,2,1,0:T(8,128)(2,1)S(1)}, u32[]{:S(2)}, u32[]{:S(2)}) %collective-permute-start.17) | collective-permute-done | bytes 196640 | tf_op jit(solution)/shard_map/ppermute | solution.py:89
  67.6 4.1 %collective-permute-done.18 = bf16[2,2,16,1536]{3,2,1,0:T(8,128)(2,1)S(1)} collective-permute-done((bf16[2,2,16,1536]{3,2,1,0:T(8,128)(2,1)S(1)}, bf16[2,2,16,1536]{3,2,1,0:T(8,128)(2,1)S(1)}, u32[]{:S(2)}, u32[]{:S(2)}) %collective-permute-start.18) | collective-permute-done | bytes 196640 | tf_op jit(solution)/shard_map/ppermute | solution.py:89
  71.8 1.5 %collective-permute-start.20 = (bf16[2,2,64,1536]{3,2,1,0:T(8,128)(2,1)S(1)}, bf16[2,2,64,1536]{3,2,1,0:T(8,128)(2,1)S(1)}, u32[]{:S(2)}, u32[]{:S(2)}) collective-permute-start(bf16[2,2,64,1536]{3,2,1,0:T(8,128)(2,1)S(1)} %bitcast.199), channel_id=1, source_target_pairs={{0,64},{1,17},{2,66},{3,19},{4,68},{5,21},{6,70},{7,23},{8,72},{9,... | collective-permute-start | bytes 2359304 | tf_op jit(solution)/shard_map/ppermute | solution.py:89
  73.3 1.3 collective-permute-start.21
  74.6 1.4 %collective-permute-start.22 = (bf16[2,2,64,1536]{3,2,1,0:T(8,128)(2,1)S(1)}, bf16[2,2,64,1536]{3,2,1,0:T(8,128)(2,1)S(1)}, u32[]{:S(2)}, u32[]{:S(2)}) collective-permute-start(bf16[2,2,64,1536]{3,2,1,0:T(8,128)(2,1)S(1)} %bitcast.201), channel_id=1, source_target_pairs={{0,128},{1,33},{2,130},{3,35},{4,132},{5,37},{6,134},{7,39},{8,136... | collective-permute-start | bytes 2359304 | tf_op jit(solution)/shard_map/ppermute | solution.py:89
  76.4 7.5 %collective-permute-done.20 = bf16[2,2,64,1536]{3,2,1,0:T(8,128)(2,1)S(1)} collective-permute-done((bf16[2,2,64,1536]{3,2,1,0:T(8,128)(2,1)S(1)}, bf16[2,2,64,1536]{3,2,1,0:T(8,128)(2,1)S(1)}, u32[]{:S(2)}, u32[]{:S(2)}) %collective-permute-start.20) | collective-permute-done | bytes 786464 | tf_op jit(solution)/shard_map/ppermute | solution.py:89
  83.9 11.0 %collective-permute-done.21 = bf16[2,2,64,1536]{3,2,1,0:T(8,128)(2,1)S(1)} collective-permute-done((bf16[2,2,64,1536]{3,2,1,0:T(8,128)(2,1)S(1)}, bf16[2,2,64,1536]{3,2,1,0:T(8,128)(2,1)S(1)}, u32[]{:S(2)}, u32[]{:S(2)}) %collective-permute-start.21) | collective-permute-done | bytes 786464 | tf_op jit(solution)/shard_map/ppermute | solution.py:89
  99.7 3.8 %collective-permute-start.24 = (bf16[2,32,768]{2,1,0:T(8,128)(2,1)S(1)}, bf16[2,32,768]{2,1,0:T(8,128)(2,1)S(1)}, u32[]{:S(2)}, u32[]{:S(2)}) collective-permute-start(bf16[2,32,768]{2,1,0:T(8,128)(2,1)S(1)} %get-tuple-element.62), channel_id=1, source_target_pairs={{0,2},{1,3},{2,4},{3,5},{4,6},{5,7},{6,8},{7,9},{8,10},{9,11},{10,... | collective-permute-start | bytes 294920 | tf_op jit(solution)/shard_map/ppermute | solution.py:65
  103.7 1.5 %collective-permute-start.30 = (bf16[2,32,768]{2,1,0:T(8,128)(2,1)S(1)}, bf16[2,32,768]{2,1,0:T(8,128)(2,1)S(1)}, u32[]{:S(2)}, u32[]{:S(2)}) collective-permute-start(bf16[2,32,768]{2,1,0:T(8,128)(2,1)S(1)} %get-tuple-element.63), channel_id=1, source_target_pairs={{0,4},{1,5},{2,6},{3,7},{4,8},{5,9},{6,10},{7,11},{8,12},{9,13},{1... | collective-permute-start | bytes 294920 | tf_op jit(solution)/shard_map/ppermute | solution.py:65
  105.1 2.8 %collective-permute-start.29 = (bf16[2,32,768]{2,1,0:T(8,128)(2,1)S(1)}, bf16[2,32,768]{2,1,0:T(8,128)(2,1)S(1)}, u32[]{:S(2)}, u32[]{:S(2)}) collective-permute-start(bf16[2,32,768]{2,1,0:T(8,128)(2,1)S(1)} %get-tuple-element.57), channel_id=1, source_target_pairs={{0,12},{1,13},{2,14},{3,15},{4,0},{5,1},{6,2},{7,3},{8,4},{9,5},{1... | collective-permute-start | bytes 294920 | tf_op jit(solution)/shard_map/ppermute | solution.py:65
  107.9 1.7 %collective-permute-start.28 = (bf16[2,32,768]{2,1,0:T(8,128)(2,1)S(1)}, bf16[2,32,768]{2,1,0:T(8,128)(2,1)S(1)}, u32[]{:S(2)}, u32[]{:S(2)}) collective-permute-start(bf16[2,32,768]{2,1,0:T(8,128)(2,1)S(1)} %get-tuple-element.58), channel_id=1, source_target_pairs={{0,6},{1,7},{2,8},{3,9},{4,10},{5,11},{6,12},{7,13},{8,14},{9,15},... | collective-permute-start | bytes 294920 | tf_op jit(solution)/shard_map/ppermute | solution.py:65
  109.6 3.4 %collective-permute-start.27 = (bf16[2,32,768]{2,1,0:T(8,128)(2,1)S(1)}, bf16[2,32,768]{2,1,0:T(8,128)(2,1)S(1)}, u32[]{:S(2)}, u32[]{:S(2)}) collective-permute-start(bf16[2,32,768]{2,1,0:T(8,128)(2,1)S(1)} %get-tuple-element.59), channel_id=1, source_target_pairs={{0,10},{1,11},{2,12},{3,13},{4,14},{5,15},{6,0},{7,1},{8,2},{9,3},... | collective-permute-start | bytes 294920 | tf_op jit(solution)/shard_map/ppermute | solution.py:65
  112.9 3.0 %collective-permute-start.26 = (bf16[2,32,768]{2,1,0:T(8,128)(2,1)S(1)}, bf16[2,32,768]{2,1,0:T(8,128)(2,1)S(1)}, u32[]{:S(2)}, u32[]{:S(2)}) collective-permute-start(bf16[2,32,768]{2,1,0:T(8,128)(2,1)S(1)} %get-tuple-element.60), channel_id=1, source_target_pairs={{0,8},{1,9},{2,10},{3,11},{4,12},{5,13},{6,14},{7,15},{8,0},{9,1},... | collective-permute-start | bytes 294920 | tf_op jit(solution)/shard_map/ppermute | solution.py:65
  116.0 2.8 %multiply_convert_fusion.1 = bf16[768,1536]{1,0:T(8,128)(2,1)} fusion(bf16[2,512,1536]{2,1,0:T(8,128)(2,1)S(1)} %pad_maximum_fusion, bf16[2,256,768]{2,1,0:T(8,128)(2,1)S(1)} %bitcast.207, bf16[2,256,768]{2,1,0:T(8,128)(2,1)S(1)} %collective-permute-done.10), kind=kOutput, calls=%fused_computation.1 | convolution fusion | flops 1211891712 | bytes 5505024 | tf_op jit(solution)/shard_map/dot_general | solution.py:26
  118.8 2.8 %multiply_convert_fusion = bf16[1536,768]{1,0:T(8,128)(2,1)} fusion(bf16[2,512,1536]{2,1,0:T(8,128)(2,1)S(1)} %pad_maximum_fusion, bf16[2,256,768]{2,1,0:T(8,128)(2,1)S(1)} %collective-permute-done.10, bf16[2,256,768]{2,1,0:T(8,128)(2,1)S(1)} %bitcast.208), kind=kOutput, calls=%fused_computation | convolution fusion | flops 1211891712 | bytes 5505024 | tf_op jit(solution)/shard_map/dot_general | solution.py:26
  122.8 3.2 %collective-permute-done.26 = bf16[2,32,768]{2,1,0:T(8,128)(2,1)S(1)} collective-permute-done((bf16[2,32,768]{2,1,0:T(8,128)(2,1)S(1)}, bf16[2,32,768]{2,1,0:T(8,128)(2,1)S(1)}, u32[]{:S(2)}, u32[]{:S(2)}) %collective-permute-start.26) | collective-permute-done | bytes 98336 | tf_op jit(solution)/shard_map/ppermute | solution.py:65
  (83 shorter events, 20.9 us)
Async XLA Ops:
  0.6 25.7 %copy-start = (bf16[768,1536]{1,0:T(8,128)(2,1)S(1)}, bf16[768,1536]{1,0:T(8,128)(2,1)}, u32[]{:S(2)}) copy-start(bf16[768,1536]{1,0:T(8,128)(2,1)} %param.5) | copy-start | bytes 7077892
  1.6 12.1 %collective-permute-start = (bf16[2,32,768]{2,1,0:T(8,128)(2,1)S(1)}, bf16[2,32,768]{2,1,0:T(8,128)(2,1)S(1)}, u32[]{:S(2)}, u32[]{:S(2)}) collective-permute-start(bf16[2,32,768]{2,1,0:T(8,128)(2,1)S(1)} %pad_maximum_fusion.9), channel_id=1, source_target_pairs={{0,14},{1,15},{2,0},{3,1},{4,2},{5,3},{6,4},{7,5},{8,6},{9,7},{10,... | collective-permute-start | bytes 294920 | tf_op jit(solution)/shard_map/ppermute | solution.py:65
  3.6 11.8 %collective-permute-start.1 = (bf16[2,32,768]{2,1,0:T(8,128)(2,1)S(1)}, bf16[2,32,768]{2,1,0:T(8,128)(2,1)S(1)}, u32[]{:S(2)}, u32[]{:S(2)}) collective-permute-start(bf16[2,32,768]{2,1,0:T(8,128)(2,1)S(1)} %pad_maximum_fusion.9), channel_id=1, source_target_pairs={{0,2},{1,3},{2,4},{3,5},{4,6},{5,7},{6,8},{7,9},{8,10},{9,11},{10,... | collective-permute-start | bytes 294920 | tf_op jit(solution)/shard_map/ppermute | solution.py:65
  3.7 14.3 %collective-permute-start.2 = (bf16[2,32,768]{2,1,0:T(8,128)(2,1)S(1)}, bf16[2,32,768]{2,1,0:T(8,128)(2,1)S(1)}, u32[]{:S(2)}, u32[]{:S(2)}) collective-permute-start(bf16[2,32,768]{2,1,0:T(8,128)(2,1)S(1)} %pad_maximum_fusion.9), channel_id=1, source_target_pairs={{0,12},{1,13},{2,14},{3,15},{4,0},{5,1},{6,2},{7,3},{8,4},{9,5},{1... | collective-permute-start | bytes 294920 | tf_op jit(solution)/shard_map/ppermute | solution.py:65
  10.3 8.8 %collective-permute-start.3 = (bf16[2,32,768]{2,1,0:T(8,128)(2,1)S(1)}, bf16[2,32,768]{2,1,0:T(8,128)(2,1)S(1)}, u32[]{:S(2)}, u32[]{:S(2)}) collective-permute-start(bf16[2,32,768]{2,1,0:T(8,128)(2,1)S(1)} %pad_maximum_fusion.9), channel_id=1, source_target_pairs={{0,4},{1,5},{2,6},{3,7},{4,8},{5,9},{6,10},{7,11},{8,12},{9,13},{1... | collective-permute-start | bytes 294920 | tf_op jit(solution)/shard_map/ppermute | solution.py:65
  10.4 10.0 %collective-permute-start.4 = (bf16[2,32,768]{2,1,0:T(8,128)(2,1)S(1)}, bf16[2,32,768]{2,1,0:T(8,128)(2,1)S(1)}, u32[]{:S(2)}, u32[]{:S(2)}) collective-permute-start(bf16[2,32,768]{2,1,0:T(8,128)(2,1)S(1)} %pad_maximum_fusion.9), channel_id=1, source_target_pairs={{0,10},{1,11},{2,12},{3,13},{4,14},{5,15},{6,0},{7,1},{8,2},{9,3},... | collective-permute-start | bytes 294920 | tf_op jit(solution)/shard_map/ppermute | solution.py:65
  13.7 12.3 %collective-permute-start.5 = (bf16[2,32,768]{2,1,0:T(8,128)(2,1)S(1)}, bf16[2,32,768]{2,1,0:T(8,128)(2,1)S(1)}, u32[]{:S(2)}, u32[]{:S(2)}) collective-permute-start(bf16[2,32,768]{2,1,0:T(8,128)(2,1)S(1)} %pad_maximum_fusion.9), channel_id=1, source_target_pairs={{0,6},{1,7},{2,8},{3,9},{4,10},{5,11},{6,12},{7,13},{8,14},{9,15},... | collective-permute-start | bytes 294920 | tf_op jit(solution)/shard_map/ppermute | solution.py:65
  15.4 10.6 %collective-permute-start.6 = (bf16[2,32,768]{2,1,0:T(8,128)(2,1)S(1)}, bf16[2,32,768]{2,1,0:T(8,128)(2,1)S(1)}, u32[]{:S(2)}, u32[]{:S(2)}) collective-permute-start(bf16[2,32,768]{2,1,0:T(8,128)(2,1)S(1)} %pad_maximum_fusion.9), channel_id=1, source_target_pairs={{0,8},{1,9},{2,10},{3,11},{4,12},{5,13},{6,14},{7,15},{8,0},{9,1},... | collective-permute-start | bytes 294920 | tf_op jit(solution)/shard_map/ppermute | solution.py:65
  26.2 6.8 %collective-permute-start.10 = (bf16[2,256,768]{2,1,0:T(8,128)(2,1)S(1)}, bf16[2,256,768]{2,1,0:T(8,128)(2,1)S(1)}, u32[]{:S(2)}, u32[]{:S(2)}) collective-permute-start(bf16[2,256,768]{2,1,0:T(8,128)(2,1)S(1)} %bitcast.206), channel_id=1, source_target_pairs={{0,1},{1,0},{2,3},{3,2},{4,5},{5,4},{6,7},{7,6},{8,9},{9,8},{10,11... | collective-permute-start | bytes 2359304 | tf_op jit(solution)/shard_map/ppermute | solution.py:59
  28.8 10.8 %collective-permute-start.9 = (bf16[2,64,1536]{2,1,0:T(8,128)(2,1)S(1)}, bf16[2,64,1536]{2,1,0:T(8,128)(2,1)S(1)}, u32[]{:S(2)}, u32[]{:S(2)}) collective-permute-start(bf16[2,64,1536]{2,1,0:T(8,128)(2,1)S(1)} %get-tuple-element.35), channel_id=1, source_target_pairs={{0,128},{1,33},{2,130},{3,35},{4,132},{5,37},{6,134},{7,39},{8,136... | collective-permute-start | bytes 1179656 | tf_op jit(solution)/shard_map/ppermute | solution.py:77
  31.9 10.5 %collective-permute-start.8 = (bf16[2,64,1536]{2,1,0:T(8,128)(2,1)S(1)}, bf16[2,64,1536]{2,1,0:T(8,128)(2,1)S(1)}, u32[]{:S(2)}, u32[]{:S(2)}) collective-permute-start(bf16[2,64,1536]{2,1,0:T(8,128)(2,1)S(1)} %get-tuple-element.34), channel_id=1, source_target_pairs={{0,192},{1,49},{2,194},{3,51},{4,196},{5,53},{6,198},{7,55},{8,200... | collective-permute-start | bytes 1179656 | tf_op jit(solution)/shard_map/ppermute | solution.py:77
  33.1 9.5 %collective-permute-start.7 = (bf16[2,64,1536]{2,1,0:T(8,128)(2,1)S(1)}, bf16[2,64,1536]{2,1,0:T(8,128)(2,1)S(1)}, u32[]{:S(2)}, u32[]{:S(2)}) collective-permute-start(bf16[2,64,1536]{2,1,0:T(8,128)(2,1)S(1)} %get-tuple-element.33), channel_id=1, source_target_pairs={{0,64},{1,17},{2,66},{3,19},{4,68},{5,21},{6,70},{7,23},{8,72},{9,... | collective-permute-start | bytes 1179656 | tf_op jit(solution)/shard_map/ppermute | solution.py:77
  34.8 11.9 %collective-permute-start.13 = (bf16[2,64,1536]{2,1,0:T(8,128)(2,1)S(1)}, bf16[2,64,1536]{2,1,0:T(8,128)(2,1)S(1)}, u32[]{:S(2)}, u32[]{:S(2)}) collective-permute-start(bf16[2,64,1536]{2,1,0:T(8,128)(2,1)S(1)} %get-tuple-element.40), channel_id=1, source_target_pairs={{0,128},{1,33},{2,130},{3,35},{4,132},{5,37},{6,134},{7,39},{8,136... | collective-permute-start | bytes 1179656 | tf_op jit(solution)/shard_map/ppermute | solution.py:77
  38.5 12.3 %collective-permute-start.12 = (bf16[2,64,1536]{2,1,0:T(8,128)(2,1)S(1)}, bf16[2,64,1536]{2,1,0:T(8,128)(2,1)S(1)}, u32[]{:S(2)}, u32[]{:S(2)}) collective-permute-start(bf16[2,64,1536]{2,1,0:T(8,128)(2,1)S(1)} %get-tuple-element.39), channel_id=1, source_target_pairs={{0,192},{1,49},{2,194},{3,51},{4,196},{5,53},{6,198},{7,55},{8,200... | collective-permute-start | bytes 1179656 | tf_op jit(solution)/shard_map/ppermute | solution.py:77
  39.6 11.4 %collective-permute-start.11 = (bf16[2,64,1536]{2,1,0:T(8,128)(2,1)S(1)}, bf16[2,64,1536]{2,1,0:T(8,128)(2,1)S(1)}, u32[]{:S(2)}, u32[]{:S(2)}) collective-permute-start(bf16[2,64,1536]{2,1,0:T(8,128)(2,1)S(1)} %get-tuple-element.38), channel_id=1, source_target_pairs={{0,64},{1,17},{2,66},{3,19},{4,68},{5,21},{6,70},{7,23},{8,72},{9,... | collective-permute-start | bytes 1179656 | tf_op jit(solution)/shard_map/ppermute | solution.py:77
  51.3 7.3 %collective-permute-start.16 = (bf16[2,2,16,1536]{3,2,0,1:T(8,128)(2,1)S(1)}, bf16[2,2,16,1536]{3,2,0,1:T(8,128)(2,1)S(1)}, u32[]{:S(2)}, u32[]{:S(2)}) collective-permute-start(bf16[2,2,16,1536]{3,2,0,1:T(8,128)(2,1)S(1)} %pad_maximum_fusion.6), channel_id=1, source_target_pairs={{0,32},{1,129},{2,34},{3,131},{4,36},{5,133},{6,38},{7,135},{8,40}... | collective-permute-start | bytes 589832 | tf_op jit(solution)/shard_map/ppermute | solution.py:137
  54.6 7.0 %collective-permute-start.15 = (bf16[2,2,16,1536]{3,2,0,1:T(8,128)(2,1)S(1)}, bf16[2,2,16,1536]{3,2,0,1:T(8,128)(2,1)S(1)}, u32[]{:S(2)}, u32[]{:S(2)}) collective-permute-start(bf16[2,2,16,1536]{3,2,0,1:T(8,128)(2,1)S(1)} %pad_maximum_fusion.5), channel_id=1, source_target_pairs={{0,48},{1,193},{2,50},{3,195},{4,52},{5,197},{6,54},{7,199},{8,56}... | collective-permute-start | bytes 589832 | tf_op jit(solution)/shard_map/ppermute | solution.py:137
  55.8 5.8 %collective-permute-start.14 = (bf16[2,2,16,1536]{3,2,0,1:T(8,128)(2,1)S(1)}, bf16[2,2,16,1536]{3,2,0,1:T(8,128)(2,1)S(1)}, u32[]{:S(2)}, u32[]{:S(2)}) collective-permute-start(bf16[2,2,16,1536]{3,2,0,1:T(8,128)(2,1)S(1)} %pad_maximum_fusion.4), channel_id=1, source_target_pairs={{0,16},{1,65},{2,18},{3,67},{4,20},{5,69},{6,22},{7,71},{8,24},{9,... | collective-permute-start | bytes 589832 | tf_op jit(solution)/shard_map/ppermute | solution.py:137
  61.8 5.8 %collective-permute-start.17 = (bf16[2,2,16,1536]{3,2,1,0:T(8,128)(2,1)S(1)}, bf16[2,2,16,1536]{3,2,1,0:T(8,128)(2,1)S(1)}, u32[]{:S(2)}, u32[]{:S(2)}) collective-permute-start(bf16[2,2,16,1536]{3,2,1,0:T(8,128)(2,1)S(1)} %pad_maximum_fusion.8), channel_id=1, source_target_pairs={{0,16},{1,65},{2,18},{3,67},{4,20},{5,69},{6,22},{7,71},{8,24},{9,... | collective-permute-start | bytes 589832 | tf_op jit(solution)/shard_map/ppermute | solution.py:89
  62.7 9.0 %collective-permute-start.18 = (bf16[2,2,16,1536]{3,2,1,0:T(8,128)(2,1)S(1)}, bf16[2,2,16,1536]{3,2,1,0:T(8,128)(2,1)S(1)}, u32[]{:S(2)}, u32[]{:S(2)}) collective-permute-start(bf16[2,2,16,1536]{3,2,1,0:T(8,128)(2,1)S(1)} %pad_maximum_fusion.8), channel_id=1, source_target_pairs={{0,48},{1,193},{2,50},{3,195},{4,52},{5,197},{6,54},{7,199},{8,56}... | collective-permute-start | bytes 589832 | tf_op jit(solution)/shard_map/ppermute | solution.py:89
  64.2 7.6 %collective-permute-start.19 = (bf16[2,2,16,1536]{3,2,1,0:T(8,128)(2,1)S(1)}, bf16[2,2,16,1536]{3,2,1,0:T(8,128)(2,1)S(1)}, u32[]{:S(2)}, u32[]{:S(2)}) collective-permute-start(bf16[2,2,16,1536]{3,2,1,0:T(8,128)(2,1)S(1)} %pad_maximum_fusion.8), channel_id=1, source_target_pairs={{0,32},{1,129},{2,34},{3,131},{4,36},{5,133},{6,38},{7,135},{8,40}... | collective-permute-start | bytes 589832 | tf_op jit(solution)/shard_map/ppermute | solution.py:89
  71.8 12.1 %collective-permute-start.20 = (bf16[2,2,64,1536]{3,2,1,0:T(8,128)(2,1)S(1)}, bf16[2,2,64,1536]{3,2,1,0:T(8,128)(2,1)S(1)}, u32[]{:S(2)}, u32[]{:S(2)}) collective-permute-start(bf16[2,2,64,1536]{3,2,1,0:T(8,128)(2,1)S(1)} %bitcast.199), channel_id=1, source_target_pairs={{0,64},{1,17},{2,66},{3,19},{4,68},{5,21},{6,70},{7,23},{8,72},{9,... | collective-permute-start | bytes 2359304 | tf_op jit(solution)/shard_map/ppermute | solution.py:89
  73.3 21.6 %collective-permute-start.21 = (bf16[2,2,64,1536]{3,2,1,0:T(8,128)(2,1)S(1)}, bf16[2,2,64,1536]{3,2,1,0:T(8,128)(2,1)S(1)}, u32[]{:S(2)}, u32[]{:S(2)}) collective-permute-start(bf16[2,2,64,1536]{3,2,1,0:T(8,128)(2,1)S(1)} %bitcast.200), channel_id=1, source_target_pairs={{0,192},{1,49},{2,194},{3,51},{4,196},{5,53},{6,198},{7,55},{8,200... | collective-permute-start | bytes 2359304 | tf_op jit(solution)/shard_map/ppermute | solution.py:89
  74.6 20.5 %collective-permute-start.22 = (bf16[2,2,64,1536]{3,2,1,0:T(8,128)(2,1)S(1)}, bf16[2,2,64,1536]{3,2,1,0:T(8,128)(2,1)S(1)}, u32[]{:S(2)}, u32[]{:S(2)}) collective-permute-start(bf16[2,2,64,1536]{3,2,1,0:T(8,128)(2,1)S(1)} %bitcast.201), channel_id=1, source_target_pairs={{0,128},{1,33},{2,130},{3,35},{4,132},{5,37},{6,134},{7,39},{8,136... | collective-permute-start | bytes 2359304 | tf_op jit(solution)/shard_map/ppermute | solution.py:89
  97.0 2.4 %collective-permute-start.23 = (bf16[2,256,768]{2,1,0:T(8,128)(2,1)S(1)}, bf16[2,256,768]{2,1,0:T(8,128)(2,1)S(1)}, u32[]{:S(2)}, u32[]{:S(2)}) collective-permute-start(bf16[2,256,768]{2,1,0:T(8,128)(2,1)S(1)} %pad_maximum_fusion.3), channel_id=1, source_target_pairs={{0,1},{1,0},{2,3},{3,2},{4,5},{5,4},{6,7},{7,6},{8,9},{9,8},{10,11... | collective-permute-start | bytes 2359304 | tf_op jit(solution)/shard_map/ppermute | solution.py:59
  99.6 10.0 %collective-permute-start.25 = (bf16[2,32,768]{2,1,0:T(8,128)(2,1)S(1)}, bf16[2,32,768]{2,1,0:T(8,128)(2,1)S(1)}, u32[]{:S(2)}, u32[]{:S(2)}) collective-permute-start(bf16[2,32,768]{2,1,0:T(8,128)(2,1)S(1)} %get-tuple-element.61), channel_id=1, source_target_pairs={{0,14},{1,15},{2,0},{3,1},{4,2},{5,3},{6,4},{7,5},{8,6},{9,7},{10,... | collective-permute-start | bytes 294920 | tf_op jit(solution)/shard_map/ppermute | solution.py:65
  99.7 13.3 %collective-permute-start.24 = (bf16[2,32,768]{2,1,0:T(8,128)(2,1)S(1)}, bf16[2,32,768]{2,1,0:T(8,128)(2,1)S(1)}, u32[]{:S(2)}, u32[]{:S(2)}) collective-permute-start(bf16[2,32,768]{2,1,0:T(8,128)(2,1)S(1)} %get-tuple-element.62), channel_id=1, source_target_pairs={{0,2},{1,3},{2,4},{3,5},{4,6},{5,7},{6,8},{7,9},{8,10},{9,11},{10,... | collective-permute-start | bytes 294920 | tf_op jit(solution)/shard_map/ppermute | solution.py:65
  103.7 18.0 %collective-permute-start.30 = (bf16[2,32,768]{2,1,0:T(8,128)(2,1)S(1)}, bf16[2,32,768]{2,1,0:T(8,128)(2,1)S(1)}, u32[]{:S(2)}, u32[]{:S(2)}) collective-permute-start(bf16[2,32,768]{2,1,0:T(8,128)(2,1)S(1)} %get-tuple-element.63), channel_id=1, source_target_pairs={{0,4},{1,5},{2,6},{3,7},{4,8},{5,9},{6,10},{7,11},{8,12},{9,13},{1... | collective-permute-start | bytes 294920 | tf_op jit(solution)/shard_map/ppermute | solution.py:65
  105.1 16.5 %collective-permute-start.29 = (bf16[2,32,768]{2,1,0:T(8,128)(2,1)S(1)}, bf16[2,32,768]{2,1,0:T(8,128)(2,1)S(1)}, u32[]{:S(2)}, u32[]{:S(2)}) collective-permute-start(bf16[2,32,768]{2,1,0:T(8,128)(2,1)S(1)} %get-tuple-element.57), channel_id=1, source_target_pairs={{0,12},{1,13},{2,14},{3,15},{4,0},{5,1},{6,2},{7,3},{8,4},{9,5},{1... | collective-permute-start | bytes 294920 | tf_op jit(solution)/shard_map/ppermute | solution.py:65
  107.9 14.9 %collective-permute-start.28 = (bf16[2,32,768]{2,1,0:T(8,128)(2,1)S(1)}, bf16[2,32,768]{2,1,0:T(8,128)(2,1)S(1)}, u32[]{:S(2)}, u32[]{:S(2)}) collective-permute-start(bf16[2,32,768]{2,1,0:T(8,128)(2,1)S(1)} %get-tuple-element.58), channel_id=1, source_target_pairs={{0,6},{1,7},{2,8},{3,9},{4,10},{5,11},{6,12},{7,13},{8,14},{9,15},... | collective-permute-start | bytes 294920 | tf_op jit(solution)/shard_map/ppermute | solution.py:65
  109.6 13.2 %collective-permute-start.27 = (bf16[2,32,768]{2,1,0:T(8,128)(2,1)S(1)}, bf16[2,32,768]{2,1,0:T(8,128)(2,1)S(1)}, u32[]{:S(2)}, u32[]{:S(2)}) collective-permute-start(bf16[2,32,768]{2,1,0:T(8,128)(2,1)S(1)} %get-tuple-element.59), channel_id=1, source_target_pairs={{0,10},{1,11},{2,12},{3,13},{4,14},{5,15},{6,0},{7,1},{8,2},{9,3},... | collective-permute-start | bytes 294920 | tf_op jit(solution)/shard_map/ppermute | solution.py:65
  112.9 13.1 %collective-permute-start.26 = (bf16[2,32,768]{2,1,0:T(8,128)(2,1)S(1)}, bf16[2,32,768]{2,1,0:T(8,128)(2,1)S(1)}, u32[]{:S(2)}, u32[]{:S(2)}) collective-permute-start(bf16[2,32,768]{2,1,0:T(8,128)(2,1)S(1)} %get-tuple-element.60), channel_id=1, source_target_pairs={{0,8},{1,9},{2,10},{3,11},{4,12},{5,13},{6,14},{7,15},{8,0},{9,1},... | collective-permute-start | bytes 294920 | tf_op jit(solution)/shard_map/ppermute | solution.py:65
  (1 other events, 1.7 us)
